TPU v7x, 512 devices: a whole 4x4x16 slice. The times are simulated.
512 devices in a mesh: sector: 64 (over z, x), chan: 8 (over y, core).
Axes of the slice: x: 4, y: 4, z: 16, core: 2. Of those that a mesh axis runs over, the one named last changes fastest.
Arguments:
- psi: float32 [2, 4096, 4096], P(None, 'chan', 'sector'), may hold values from -6 to 6
- potential: bfloat16 [4096, 4096], P('chan', 'sector'), may hold values from -0.796875 to 0.796875
- dipole: bfloat16 [16, 8, 256, 256], P('chan'), may hold values from -0.125 to 0.125
- coupling: int32 [16, 8], P('chan'), may hold values from 0 to 15
- amp: bfloat16 [4096, 2048], P('chan'), may hold values from -0.125 to 0.125
- sym: int32 [4096], P('chan'), may hold values from 0 to 15
- sizes: int32 [16], P('chan'), may hold values from 1 to 2048, 24576 in all
- inner_ham: bfloat16 [16, 2048, 2048], P('chan', 'sector'), as said below
- inner_state: float32 [2, 16, 2048], P(None, 'chan'), may hold values from -6 to 6
- field: float32 [1], replicated, may hold values from 0.5 to 1.5
Outputs:
- psi_next: float32 [2, 4096, 4096], P(None, 'chan', 'sector')
- state_next: float32 [2, 16, 2048], P(None, 'chan')
Inputs may be any that keep to these rules, and one draw needn't show every extreme that they name: `coupling`: block indices. `sym`: symmetry block indices. The sizes sum to 24576. `inner_ham`: each block is symmetric.
All inputs are finite; a program needn't handle non-finite values. No bound on the sum of `sizes` on one device may be relied on, other than what follows from the above.
Results may differ from a plain program's by a relative error of at most 0.002.
The roundings to bfloat16 on the way count: a program that leaves them out, or rounds other values in their place, can miss the bound.
Values may be sent and summed in bfloat16 or wider, within the bound.
No kernel may reach another device: no remote copies, remote signals or barrier semaphores. Data moves between devices by JAX's collectives and lax.ppermute only.
A program may use at most 64 MiB of HBM per device.

v0:
```python
import jax
import jax.numpy as jnp
from jax import lax
from jax.sharding import PartitionSpec as P

ORDER = 4


kinetic_coeff = 1.0 / 48.0


def from_root(value, axis, source):
    kept = jnp.where(lax.axis_index(axis) == source, value, 0).astype(value.dtype)
    return lax.psum(kept, axis)


def extended(cells, sides, width):
    for axis, dim in sides:
        count = lax.axis_size(axis)
        ends = count - 1
        head = lax.slice_in_dim(cells, 0, width, axis=dim)
        tail = lax.slice_in_dim(cells, cells.shape[dim] - width, cells.shape[dim], axis=dim)
        cells = jnp.concatenate(
            [
                lax.ppermute(tail, axis, [(i, (i + 1) % count) for i in range(ends)]),
                cells,
                lax.ppermute(head, axis, [((i + 1) % count, i) for i in range(ends)]),
            ],
            axis=dim,
        )
    return cells


def shards(psi, potential, dipole, coupling, amp, sym, sizes, inner_ham, inner_state, field):
    hi = lax.Precision.HIGHEST
    n_sector = lax.axis_size("sector")
    points = psi.shape[2]
    chans = psi.shape[1]
    width = dipole.shape[2]
    states = inner_ham.shape[2]
    radius = (lax.axis_index("sector") * points + jnp.arange(points) + 1).astype(jnp.float32) / (
        points * n_sector
    )
    at_first = lax.axis_index("sector") == 0
    mask = (jnp.arange(states)[None, :] < sizes[:, None]).astype(jnp.float32)
    all_sym = sizes.shape[0] * lax.axis_size("chan")
    onehot = (sym[None, :] == jnp.arange(all_sym)[:, None]).astype(jnp.float32)
    amp_f = amp.astype(jnp.float32)
    ham_f = inner_ham.astype(jnp.float32)
    pot = potential.astype(jnp.float32)
    strength = field[0]
    term = psi
    state = mask * inner_state
    total = term
    total_in = state
    for order in range(1, ORDER + 1):
        state_all = lax.all_gather(state.astype(jnp.bfloat16), "chan", axis=1, tiled=True).astype(
            state.dtype
        )
        product = jnp.einsum("zsk,ck->zsc", state_all, amp_f, precision=hi)
        ghost = jnp.sum(product * onehot[None], axis=1)
        first = from_root(term[:, :, 0], "sector", 0)
        chosen = onehot[None] * first[:, None, :]
        partial_terms = jnp.einsum("zsc,ck->zsk", chosen, amp_f, precision=hi)
        surface = lax.psum_scatter(
            partial_terms.astype(jnp.bfloat16), "chan", scatter_dimension=1, tiled=True
        ).astype(jnp.float32)
        own_rows = jnp.einsum("skl,zsl->zsk", ham_f, state, precision=hi)
        ham_rows = lax.all_gather(own_rows, "sector", axis=2, tiled=True)
        inner = mask * (ham_rows + surface)
        padded = extended(term, (("sector", 2),), 2)
        left = jnp.where(
            at_first, jnp.broadcast_to(ghost[:, :, None], (2, chans, 2)), padded[:, :, :2]
        )
        padded = jnp.concatenate([left, padded[:, :, 2:]], axis=2)
        stencil = (
            -padded[:, :, :-4]
            + 16.0 * padded[:, :, 1:-3]
            - 30.0 * term
            + 16.0 * padded[:, :, 3:-1]
            - padded[:, :, 4:]
        )
        low = term.astype(jnp.bfloat16)
        whole = lax.all_gather(low, "chan", axis=1, tiled=True)
        grouped = whole.reshape(2, -1, width, points)
        picked = grouped[:, coupling]
        out = jnp.einsum("bjci,zbjip->zbcp", dipole, picked, preferred_element_type=jnp.float32)
        outer = (
            -kinetic_coeff * stencil
            + pot * term
            + strength * radius * out.reshape(2, chans, points)
        )
        outer, inner = (outer, inner)
        term = jnp.stack([outer[1], -outer[0]]) / order
        state = jnp.stack([inner[1], -inner[0]]) / order
        total = total + term
        total_in = total_in + state
    return (total, total_in)


def solution(mesh):
    return jax.shard_map(
        shards,
        mesh=mesh,
        in_specs=(
            P(None, "chan", "sector"),
            P("chan", "sector"),
            P("chan", None, None, None),
            P("chan", None),
            P("chan", None),
            P("chan"),
            P("chan"),
            P("chan", "sector", None),
            P(None, "chan", None),
            P(),
        ),
        out_specs=(P(None, "chan", "sector"), P(None, "chan", None)),
        check_vma=False,
    )
```

profile of v0, /device:TPU:6, one launch (start us, length us, event | category | flops | bytes accessed | tf_op | source)
XLA Modules:
  0.0 1029.6 jit_solution(10813171538038351544)
XLA Ops:
  7.2 0.9 fusion.133
  8.2 3.7 collective-permute-start
  11.9 1.7 fusion.132
  13.7 2.1 collective-permute-start.1
  17.3 1.3 convolution_bitcast_fusion.3
  21.8 13.3 %all_gather.36 = bf16[2,16,2048]{2,0,1:T(2,128)(2,1)S(1)} all-gather(bf16[2,2,2048]{2,0,1:T(2,128)(2,1)S(1)} %fusion.122), channel_id=1, replica_groups=mesh['sector'=64,'chan'=8] {'chan'}, dimensions={1}, use_global_device_ids=true | all-gather | bytes 147456 | tf_op jit(solution)/shard_map/all_gather | solution.py:57
  37.3 117.6 %all_gather.38 = f32[2,2,2048]{1,0,2:T(2,128)} all-gather(f32[2,2,32]{1,0,2:T(2,128)S(1)} %copy.61), channel_id=1, replica_groups=mesh['sector'=64,'chan'=8] {'sector'}, dimensions={2}, use_global_device_ids=true | all-gather | bytes 33280 | tf_op jit(solution)/shard_map/all_gather | solution.py:69
  154.9 2.7 copy.63
  157.6 1.3 dynamic-slice
  160.3 1.3 copy.140
  161.7 1.7 gather_fusion
  163.3 2.8 fusion.20
  166.4 138.4 %all-reduce.5 = (f32[2,512]{1,0:T(2,128)S(1)}, f32[2,512]{1,0:T(2,128)S(1)}) all-reduce(f32[2,512]{1,0:T(2,128)S(1)} %bitcast.175, f32[2,512]{1,0:T(2,128)S(1)} %bitcast.177), channel_id=1, replica_groups=mesh['sector'=64,'chan'=8] {'sector'}, use_global_device_ids=true, to_apply=%region_1.2 | all-reduce | flops 2048 | bytes 16384 | tf_op jit(solution)/shard_map/psum | solution.py:14
  304.8 1.8 convolution_convert_fusion.2
  306.5 1.8 convolution_convert_fusion.3
  308.4 3.3 collective-permute-start.2
  311.7 3.1 collective-permute-start.3
  315.6 67.8 %all-reduce.13.cloned.1.call-done = (bf16[2,16,2048]{2,1,0:T(8,128)(2,1)}, bf16[2,16,2048]{2,1,0:T(8,128)(2,1)}) async-done(((bf16[2,16,2048]{2,1,0:T(8,128)(2,1)}, bf16[2,16,2048]{2,1,0:T(8,128)(2,1)}), (bf16[2,16,2048]{2,1,0:T(8,128)(2,1)}, bf16[2,16,2048]{2,1,0:T(8,128)(2,1)})) %all-reduce.13.cloned.1.call-update) | async-done | bytes 262160
  384.4 12.8 %all_gather.39 = bf16[2,16,2048]{2,0,1:T(2,128)(2,1)S(1)} all-gather(bf16[2,2,2048]{2,0,1:T(2,128)(2,1)S(1)} %fusion.121), channel_id=1, replica_groups=mesh['sector'=64,'chan'=8] {'chan'}, dimensions={1}, use_global_device_ids=true | all-gather | bytes 147456 | tf_op jit(solution)/shard_map/all_gather | solution.py:57
  398.4 112.2 %all_gather.41 = f32[2,2,2048]{1,0,2:T(2,128)} all-gather(f32[2,2,32]{1,0,2:T(2,128)S(1)} %copy.68), channel_id=1, replica_groups=mesh['sector'=64,'chan'=8] {'sector'}, dimensions={2}, use_global_device_ids=true | all-gather | bytes 33280 | tf_op jit(solution)/shard_map/all_gather | solution.py:69
  510.6 2.7 copy.70
  513.3 0.9 maximum_maximum_fusion
  515.2 1.3 copy.139
  516.5 1.7 gather_fusion.1
  518.2 2.8 fusion.23
  522.6 109.1 %all_gather.44 = f32[2,2,2048]{1,0,2:T(2,128)} all-gather(f32[2,2,32]{1,0,2:T(2,128)S(1)} %copy.75), channel_id=1, replica_groups=mesh['sector'=64,'chan'=8] {'sector'}, dimensions={2}, use_global_device_ids=true | all-gather | bytes 33280 | tf_op jit(solution)/shard_map/all_gather | solution.py:69
  631.7 2.7 copy.77
  634.4 12.9 %all_gather.42 = bf16[2,16,2048]{2,0,1:T(2,128)(2,1)S(1)} all-gather(bf16[2,2,2048]{2,0,1:T(2,128)(2,1)S(1)} %fusion.124), channel_id=1, replica_groups=mesh['sector'=64,'chan'=8] {'chan'}, dimensions={1}, use_global_device_ids=true | all-gather | bytes 147456 | tf_op jit(solution)/shard_map/all_gather | solution.py:57
  648.7 3.9 collective-permute-start.4
  652.6 2.0 collective-permute-start.5
  655.8 1.3 copy.138
  657.1 1.8 gather_fusion.2
  658.9 2.8 fusion.26
  661.8 1.0 fusion.73
  664.2 135.9 %all-reduce.4 = (f32[2,512]{1,0:T(2,128)S(1)}, f32[2,512]{1,0:T(2,128)S(1)}) all-reduce(f32[2,512]{1,0:T(2,128)S(1)} %bitcast.176, f32[2,512]{1,0:T(2,128)S(1)} %bitcast.178), channel_id=1, replica_groups=mesh['sector'=64,'chan'=8] {'sector'}, use_global_device_ids=true, to_apply=%region_7.8 | all-reduce | flops 2048 | bytes 16384 | tf_op jit(solution)/shard_map/psum | solution.py:14
  800.2 1.8 convolution_convert_fusion
  801.9 1.8 convolution_convert_fusion.1
  804.4 5.8 collective-permute-start.6
  810.1 3.1 collective-permute-start.7
  813.3 69.9 %all-reduce.11.cloned.1.call-done = (bf16[2,16,2048]{2,1,0:T(8,128)(2,1)}, bf16[2,16,2048]{2,1,0:T(8,128)(2,1)}) async-done(((bf16[2,16,2048]{2,1,0:T(8,128)(2,1)}, bf16[2,16,2048]{2,1,0:T(8,128)(2,1)}), (bf16[2,16,2048]{2,1,0:T(8,128)(2,1)}, bf16[2,16,2048]{2,1,0:T(8,128)(2,1)})) %all-reduce.11.cloned.1.call-update) | async-done | bytes 262160
  884.6 112.2 %all_gather.47 = f32[2,2,2048]{1,0,2:T(2,128)} all-gather(f32[2,2,32]{1,0,2:T(2,128)S(1)} %copy.82), channel_id=1, replica_groups=mesh['sector'=64,'chan'=8] {'sector'}, dimensions={2}, use_global_device_ids=true | all-gather | bytes 33280 | tf_op jit(solution)/shard_map/all_gather | solution.py:69
  996.8 2.7 copy.84
  999.5 0.9 constant_dynamic-slice_fusion
  1000.6 12.8 %all_gather.45 = bf16[2,16,2048]{2,0,1:T(2,128)(2,1)S(1)} all-gather(bf16[2,2,2048]{2,0,1:T(2,128)(2,1)S(1)} %get-tuple-element.39), channel_id=1, replica_groups=mesh['sector'=64,'chan'=8] {'chan'}, dimensions={1}, use_global_device_ids=true | all-gather | bytes 147456 | tf_op jit(solution)/shard_map/all_gather | solution.py:57
  1014.8 1.3 copy.137
  1016.1 1.8 gather_fusion.3
  1017.9 2.8 fusion.29
  1020.8 1.0 fusion.62
  (161 shorter events, 21.3 us)
Async XLA Ops:
  7.2 28.6 %copy-start = (bf16[512,2048]{1,0:T(8,128)(2,1)S(1)}, bf16[512,2048]{1,0:T(8,128)(2,1)}, u32[]{:S(2)}) copy-start(bf16[512,2048]{1,0:T(8,128)(2,1)} %param.14) | copy-start | bytes 6291460
  7.2 29.4 %copy-start.28 = (bf16[512,64]{0,1:T(8,128)(2,1)S(1)}, bf16[512,64]{0,1:T(8,128)(2,1)}, u32[]{:S(2)}) copy-start(bf16[512,64]{0,1:T(8,128)(2,1)} %param.11) | copy-start | bytes 196612
  7.2 152.4 %all-gather.5.cloned.1.call-start = ((), (), s32[]{:S(2)}) async-start(), calls=%async_computation | async-start | bytes 1179648 | tf_op jit(solution)/shard_map/all_gather | solution.py:84
  8.2 151.4 %collective-permute-start = (f32[2,512,2]{1,2,0:T(2,128)S(1)}, f32[2,512,2]{1,2,0:T(2,128)S(1)}, u32[]{:S(2)}, u32[]{:S(2)}) collective-permute-start(f32[2,512,2]{1,2,0:T(2,128)S(1)} %get-tuple-element.35), channel_id=1, source_target_pairs={{0,8},{8,16},{16,24},{24,32},{32,40},{40,48},{48,56},{56,64},{64,7... | collective-permute-start | bytes 24584 | tf_op jit(solution)/shard_map/ppermute | solution.py:25
  13.6 369.8 %all-reduce.13.cloned.1.call-start = ((), (), s32[]{:S(2)}) async-start(), calls=%async_computation.5 | async-start | bytes 524288
  13.7 145.8 %collective-permute-start.1 = (f32[2,512,2]{1,2,0:T(2,128)S(1)}, f32[2,512,2]{1,2,0:T(2,128)S(1)}, u32[]{:S(2)}, u32[]{:S(2)}) collective-permute-start(f32[2,512,2]{1,2,0:T(2,128)S(1)} %get-tuple-element.34), channel_id=1, source_target_pairs={{8,0},{16,8},{24,16},{32,24},{40,32},{48,40},{56,48},{64,56},{72,6... | collective-permute-start | bytes 24584 | tf_op jit(solution)/shard_map/ppermute | solution.py:27
  20.9 145.2 %copy-start.20 = (f32[512,64]{0,1:T(8,128)}, f32[512,64]{0,1:T(8,128)S(1)}, u32[]{:S(2)}) copy-start(f32[512,64]{0,1:T(8,128)S(1)} %convert_element_type.86) | copy-start | bytes 393220
  35.1 485.9 %copy-start.33 = (f32[64]{0:T(128)}, f32[64]{0:T(128)S(1)}, u32[]{:S(2)}) copy-start(f32[64]{0:T(128)S(1)} %convert_multiply_fusion) | copy-start | bytes 772
  35.1 481.4 %copy-start.31 = (s32[1024]{0:T(1024)}, s32[1024]{0:T(1024)S(1)}, u32[]{:S(2)}) copy-start(s32[1024]{0:T(1024)S(1)} %pad_clamp_fusion) | copy-start | bytes 12292
  163.3 2.8 copy-start.1
  163.3 2.8 copy-start.19
  308.3 89.7 %copy-start.3 = (bf16[2,32,2048]{2,1,0:T(8,128)(2,1)S(1)}, bf16[2,32,2048]{2,1,0:T(8,128)(2,1)}, u32[]{:S(2)}) copy-start(bf16[2,32,2048]{2,1,0:T(8,128)(2,1)} %param.17) | copy-start | bytes 786436
  308.3 206.8 %all-gather.7.cloned.1.call-start = ((), (), s32[]{:S(2)}) async-start(), calls=%async_computation.1 | async-start | bytes 1179648 | tf_op jit(solution)/shard_map/all_gather | solution.py:84
  308.4 89.5 %collective-permute-start.2 = (f32[2,512,2]{1,2,0:T(2,128)S(1)}, f32[2,512,2]{1,2,0:T(2,128)S(1)}, u32[]{:S(2)}, u32[]{:S(2)}) collective-permute-start(f32[2,512,2]{1,2,0:T(2,128)S(1)} %get-tuple-element.28), channel_id=1, source_target_pairs={{0,8},{8,16},{16,24},{24,32},{32,40},{40,48},{48,56},{56,64},{64,7... | collective-permute-start | bytes 24584 | tf_op jit(solution)/shard_map/ppermute | solution.py:25
  311.7 201.6 %collective-permute-start.3 = (f32[2,512,2]{1,2,0:T(2,128)S(1)}, f32[2,512,2]{1,2,0:T(2,128)S(1)}, u32[]{:S(2)}, u32[]{:S(2)}) collective-permute-start(f32[2,512,2]{1,2,0:T(2,128)S(1)} %get-tuple-element.29), channel_id=1, source_target_pairs={{8,0},{16,8},{24,16},{32,24},{40,32},{48,40},{56,48},{64,56},{72,6... | collective-permute-start | bytes 24584 | tf_op jit(solution)/shard_map/ppermute | solution.py:27
  315.6 340.2 %all-gather.9.cloned.1.call-start = ((), (), s32[]{:S(2)}) async-start(), calls=%async_computation.2 | async-start | bytes 1179648 | tf_op jit(solution)/shard_map/all_gather | solution.py:84
  518.2 2.8 copy-start.6
  518.2 2.8 copy-start.7
  518.2 2.9 copy-start.21
  521.0 1.2 copy-start.4
  521.2 113.1 %copy-start.8 = (f32[1,512,64]{1,2,0:T(8,128)}, f32[1,512,64]{1,2,0:T(8,128)S(1)}, u32[]{:S(2)}) copy-start(f32[1,512,64]{1,2,0:T(8,128)S(1)} %get-tuple-element.24) | copy-start | bytes 393220
  521.3 113.1 %copy-start.11 = (f32[1,512,64]{1,2,0:T(8,128)}, f32[1,512,64]{1,2,0:T(8,128)S(1)}, u32[]{:S(2)}) copy-start(f32[1,512,64]{1,2,0:T(8,128)S(1)} %get-tuple-element.25) | copy-start | bytes 393220
  522.0 130.5 %copy-start.24 = (f32[2,512,64]{1,2,0:T(8,128)}, f32[2,512,64]{1,2,0:T(8,128)S(1)}, u32[]{:S(2)}) copy-start(f32[2,512,64]{1,2,0:T(8,128)S(1)} %get-tuple-element.21) | copy-start | bytes 786436
  522.1 361.1 %all-reduce.11.cloned.1.call-start = ((), (), s32[]{:S(2)}) async-start(), calls=%async_computation.4 | async-start | bytes 524288
  648.7 6.5 collective-permute-start.4
  652.6 9.1 collective-permute-start.5
  658.9 2.9 copy-start.9
  658.9 2.9 copy-start.12
  658.9 2.9 copy-start.25
  658.9 2.9 copy-start.27
  658.9 2.9 copy-start.30
  658.9 2.9 copy-start.34
  661.7 2.5 copy-start.32
  662.8 1.3 copy-start.16
  664.2 139.6 %copy-start.22 = (f32[2,512,64]{1,2,0:T(8,128)}, f32[2,512,64]{1,2,0:T(8,128)S(1)}, u32[]{:S(2)}) copy-start(f32[2,512,64]{1,2,0:T(8,128)S(1)} %get-tuple-element.15) | copy-start | bytes 786436
  800.1 84.0 %copy-start.5 = (bf16[2,32,2048]{2,1,0:T(8,128)(2,1)S(1)}, bf16[2,32,2048]{2,1,0:T(8,128)(2,1)}, u32[]{:S(2)}) copy-start(bf16[2,32,2048]{2,1,0:T(8,128)(2,1)} %param.17) | copy-start | bytes 786436
  803.7 211.0 %all-gather.11.cloned.1.call-start = ((), (), s32[]{:S(2)}) async-start(), calls=%async_computation.3 | async-start | bytes 1179648 | tf_op jit(solution)/shard_map/all_gather | solution.py:84
  804.4 210.3 %collective-permute-start.6 = (f32[2,512,2]{1,2,0:T(2,128)S(1)}, f32[2,512,2]{1,2,0:T(2,128)S(1)}, u32[]{:S(2)}, u32[]{:S(2)}) collective-permute-start(f32[2,512,2]{1,2,0:T(2,128)S(1)} %get-tuple-element.16), channel_id=1, source_target_pairs={{0,8},{8,16},{16,24},{24,32},{32,40},{40,48},{48,56},{56,64},{64,7... | collective-permute-start | bytes 24584 | tf_op jit(solution)/shard_map/ppermute | solution.py:25
  810.1 210.6 %collective-permute-start.7 = (f32[2,512,2]{1,2,0:T(2,128)}, f32[2,512,2]{1,2,0:T(2,128)}, u32[]{:S(2)}, u32[]{:S(2)}) collective-permute-start(f32[2,512,2]{1,2,0:T(2,128)} %get-tuple-element.17), channel_id=1, source_target_pairs={{8,0},{16,8},{24,16},{32,24},{40,32},{48,40},{56,48},{64,56},{72,6... | collective-permute-start | bytes 24584 | tf_op jit(solution)/shard_map/ppermute | solution.py:27
  884.6 115.8 %copy-start.29 = (f32[2,2,2048]{2,1,0:T(2,128)S(1)}, f32[2,2,2048]{2,1,0:T(2,128)}, u32[]{:S(2)}) copy-start(f32[2,2,2048]{2,1,0:T(2,128)} %param.18) | copy-start | bytes 98308
  1017.9 2.9 copy-start.15
  1017.9 2.9 copy-start.17
  1017.9 2.9 copy-start.23
  1017.9 2.9 copy-start.26
  1017.9 2.9 copy-start.35
  1017.9 3.9 copy-start.2
  1017.9 3.9 copy-start.10
  1017.9 3.9 copy-start.13
  (2 other events, 1.4 us)
Sparse Core Ops, SparseCore 0:
  13.8 34.8 all-gather.4
  308.5 74.9 all-reduce.12
  385.8 30.2 all-gather.6
  522.2 27.6 all-gather.8
  803.8 79.3 all-reduce.10
  885.2 30.2 all-gather.10
where the time goes:
time: 1030 us
  blocking collectives  777 us (75%)
  waiting for transfers between devices  138 us (13%)
  local copies, waits for them, and re-layouts  33.2 us (3%)
  starting transfers between devices  27.3 us (3%)
  matrix products  23.3 us (2%)
  between operations  16.3 us (2%)
  other arithmetic  14.4 us (1%)
    all_gather x4, blocking collectives, shards(): ham_rows = lax.all_gather(own_rows, 'sector', axis=2, tiled=True)  451 us
    psum x2, blocking collectives, from_root(): return lax.psum(kept, axis)  274 us
    unnamed x8, waiting for transfers between devices  138 us
    all_gather x4, blocking collectives, shards(): lax.all_gather(state.astype(jnp.bfloat16), 'chan', axis=1, tiled=True)  51.7 us
  transfers between devices with their start and end apart: 14, of which 2 were waited for; matrix products, arithmetic and copies ran while one was open for 4% of the time, Pallas kernels for 0%

commit v1 on v0

v1 whole, which is shorter than its diff:
```python
from types import SimpleNamespace

import jax
import jax.numpy as jnp
from jax import lax
from jax.experimental import pallas as pl
from jax.experimental.pallas import tpu as pltpu
from jax.sharding import PartitionSpec as P


F32 = jnp.float32
BF16 = jnp.bfloat16
VMEM = pltpu.VMEM
SMEM = pltpu.SMEM
KINETIC = 1.0 / 48.0


def call(body, ins, outs, scratch, flops, moved):
    names = list(ins) + list(outs) + list(scratch)

    def kernel(*refs):
        body(SimpleNamespace(**dict(zip(names, refs))))

    results = pl.pallas_call(
        kernel,
        out_shape=[jax.ShapeDtypeStruct(shape, kind) for shape, kind in outs.values()],
        in_specs=[pl.BlockSpec(memory_space=space) for _, space in ins.values()],
        out_specs=[pl.BlockSpec(memory_space=VMEM) for _ in outs],
        scratch_shapes=list(scratch.values()),
        compiler_params=pltpu.CompilerParams(vmem_limit_bytes=24 * 1024 * 1024),
        cost_estimate=pl.CostEstimate(flops=flops, bytes_accessed=moved, transcendentals=0),
    )(*[value for value, _ in ins.values()])
    return dict(zip(outs, results))


def dot_t(a, b):
    return lax.dot_general(a, b, (((1,), (1,)), ((), ())), preferred_element_type=F32)


def dot(a, b):
    return lax.dot_general(a, b, (((1,), (0,)), ((), ())), preferred_element_type=F32)


def split(value):
    high = value.astype(BF16)
    return high, (value - high.astype(F32)).astype(BF16)


def rows_of(shape):
    return lax.broadcasted_iota(jnp.int32, shape, 0)


def fetch(r):
    mine = r.info[0]
    copies = [
        pltpu.make_async_copy(r.ya, r.ys.at[mine], r.sem.at[0]),
        pltpu.make_async_copy(r.yb, r.ys.at[1 - mine], r.sem.at[1]),
    ]
    for copy in copies:
        copy.start()
    return copies


def ghost_of(r, base):
    states = jnp.concatenate([r.ys[c, y, base : base + 16, :] for y in range(4) for c in range(2)], axis=0)
    row = rows_of((128, 512))
    quarter = (row >> 1) & 3
    total = jnp.zeros((128, 512), F32)
    for q in range(4):
        part = dot_t(states, r.amp[:, q * 512 : (q + 1) * 512])
        total = total + jnp.where(quarter == q, part, 0.0)
    block = (row >> 4) * 2 + (row & 1)
    total = jnp.where(block == r.sym[...], total, 0.0)
    comp = (row >> 3) & 1
    g0 = jnp.sum(jnp.where(comp == 0, total, 0.0), axis=0, keepdims=True)
    g1 = jnp.sum(jnp.where(comp == 1, total, 0.0), axis=0, keepdims=True)
    return g0, g1


def surface_part(r, first0, first1):
    row = rows_of((128, 512))
    block = (row >> 4) * 2 + (row & 1)
    comp = (row >> 3) & 1
    chosen = jnp.where(block == r.sym[...], jnp.where(comp == 0, first0, first1), 0.0)
    both = jnp.concatenate(split(chosen), axis=0)
    quarter = (row >> 1) & 3
    total = jnp.zeros((128, 512), F32)
    for q in range(4):
        part = dot(both, r.amp[:, q * 512 : (q + 1) * 512])
        total = total + jnp.where(quarter == q, part[:128] + part[128:], 0.0)
    return total.astype(BF16)


def surface_of(r, base):
    mine = r.info[0]
    total = jnp.zeros((16, 512), F32)
    for y in range(4):
        for c in range(2):
            both = r.ys[c, y, base : base + 32, :].astype(F32)
            total = total + jnp.where(mine == 0, both[:16], both[16:])
    return total


def mask_of(r):
    row = rows_of((16, 512))
    lane = lax.broadcasted_iota(jnp.int32, (16, 512), 1)
    size = jnp.where((row & 1) == 0, r.sizes[0], r.sizes[1])
    return (((row >> 1) & 3) * 512 + lane) < size


def ham_full(r):
    for z in range(16):
        for comp in range(2):
            at = comp * 8 + (z // 4) * 2
            r.full[at : at + 2, (z % 4) * 128 : (z % 4 + 1) * 128] = r.zr[z, comp * 2 : comp * 2 + 2, :]
    return r.full[...]


def next_state(r, ham, surface, order):
    image = jnp.where(mask_of(r), ham + surface, 0.0)
    return jnp.concatenate([image[8:], -image[:8]], axis=0) * (1.0 / order)


def first_received(r):
    for comp in range(2):
        for part in range(4):
            at = 8 + comp * 4 + part
            r.first[comp : comp + 1, part * 128 : (part + 1) * 128] = r.zr[0, at : at + 1, :]
    return r.first[0:1, :], r.first[1:2, :]


def ham_rows(r, state):
    both = jnp.concatenate(split(state), axis=0)
    row = rows_of((16, 128))
    total = jnp.zeros((16, 128), F32)
    for block in range(2):
        for q in range(4):
            ham = jnp.concatenate([r.ham[x, block, :, q * 512 : (q + 1) * 512] for x in range(4)], axis=0)
            part = dot_t(both, ham)
            keep = (((row >> 1) & 3) == q) & ((row & 1) == block)
            total = total + jnp.where(keep, part[:16] + part[16:], 0.0)
    r.sums[...] = total
    for comp in range(2):
        at = comp * 8
        r.piece[comp * 2 : comp * 2 + 2, :] = (
            r.sums[at : at + 2, :] + r.sums[at + 2 : at + 4, :] + r.sums[at + 4 : at + 6, :] + r.sums[at + 6 : at + 8, :]
        )


def first_rows(r, first0, first1):
    for comp, first in enumerate((first0, first1)):
        for part in range(4):
            at = 8 + comp * 4 + part
            r.piece[at : at + 1, :] = first[:, part * 128 : (part + 1) * 128]


def z_out(r):
    piece = r.piece[...]
    for z in range(16):
        r.zo[z] = piece


def dipole_image(r):
    halves = []
    for b in range(2):
        total = None
        for j in range(8):
            n = r.coupling[b, j]
            lanes = pl.ds(pl.multiple_of((n & 1) * 256, 256), 256)
            block = r.ys[(n >> 1) & 1, n >> 2, 0:128, lanes]
            part = dot_t(block, r.dipole[b, j])
            total = part if total is None else total + part
        halves.append(total)
    return jnp.concatenate(halves, axis=1)


def outer_image(r, dip):
    images = []
    row = rows_of((64, 512))
    radius = (r.info[1] * 64 + row + 1).astype(F32) * (1.0 / r.points)
    for comp in range(2):
        u = r.u[comp * 64 : (comp + 1) * 64, :]
        r.pad[comp, 6:8, :] = r.left[comp * 2 : comp * 2 + 2, :]
        r.pad[comp, 8:72, :] = u
        r.pad[comp, 72:74, :] = r.right[comp * 2 : comp * 2 + 2, :]
        stencil = 16.0 * (r.pad[comp, 7:71, :] + r.pad[comp, 9:73, :]) - 30.0 * u
        stencil = stencil - (r.pad[comp, 6:70, :] + r.pad[comp, 10:74, :])
        images.append(
            -KINETIC * stencil + r.pot[...] * u + r.field[0] * radius * dip[comp * 64 : (comp + 1) * 64, :]
        )
    return images


def ghost_image(r, ghosts):
    row = rows_of((64, 512))
    hub = jnp.where(r.info[1] == 0, 1.0, 0.0).astype(F32)
    images = []
    for ghost in ghosts:
        ghost = ghost * hub
        images.append(jnp.where(row == 0, (-15.0 * KINETIC) * ghost, jnp.where(row == 1, KINETIC * ghost, 0.0)))
    return images


def term_of(images, order):
    return images[1] * (1.0 / order), images[0] * (-1.0 / order)


def ends_out(r, term):
    for comp in range(2):
        r.head[comp * 2 : comp * 2 + 2, :] = term[comp][0:2, :]
        r.tail[comp * 2 : comp * 2 + 2, :] = term[comp][62:64, :]
    r.head[4:8, :] = jnp.zeros((4, 512), F32)
    r.tail[4:8, :] = jnp.zeros((4, 512), F32)


def low_out(r, term):
    low = jnp.concatenate([term[0].astype(BF16), term[1].astype(BF16)], axis=0)
    for y in range(4):
        r.yo[y, 0:128, :] = low


def state_out(r, state, base):
    low = state.astype(BF16)
    for y in range(4):
        r.yo[y, base : base + 16, :] = low


def surface_out(r, part, base):
    for y in range(4):
        r.yo[y, base : base + 32, :] = part[y * 32 : (y + 1) * 32]


def shards(psi, potential, dipole, coupling, amp, sym, sizes, inner_ham, inner_state, field):
    n_sector = lax.axis_size("sector")
    sector = lax.axis_index("sector")
    chan = lax.axis_index("chan")
    points = float(64 * n_sector)
    x_groups = [[z * 4 + x for x in range(4)] for z in range(16)]
    z_groups = [[z * 4 + x for z in range(16)] for x in range(4)]
    y_groups = [[y * 2 + c for y in range(4)] for c in range(2)]
    swap = [(c, c ^ 1) for c in range(8)]
    up = [(i, i + 1) for i in range(n_sector - 1)]
    down = [(i + 1, i) for i in range(n_sector - 1)]

    info = jnp.stack([chan & 1, sector]).astype(jnp.int32)
    sym_row = sym.reshape(1, 512)
    first_state = inner_state.reshape(2, 2, 4, 512).transpose(0, 2, 1, 3).reshape(16, 512)

    def over_y(piece):
        mine = lax.all_to_all(piece, "chan", 0, 0, axis_index_groups=y_groups)
        return mine, lax.ppermute(mine, "chan", swap)

    def over_z(piece):
        return lax.all_to_all(piece, "sector", 0, 0, axis_index_groups=z_groups)

    def over_x(piece):
        return lax.all_to_all(piece, "sector", 0, 0, axis_index_groups=x_groups)

    def halos(out):
        return lax.ppermute(out["tail"], "sector", up), lax.ppermute(out["head"], "sector", down)

    def stage(body, ins, outs, rows=0, low=False, inner=True):
        ins = dict(ins)
        ins["info"] = (info, SMEM)
        scratch = {"sem": pltpu.SemaphoreType.DMA((2,))}
        moved = 1 << 20
        if rows:
            scratch["ys"] = VMEM((2, 4, rows, 512), BF16)
        if low:
            ins["dipole"] = (dipole, VMEM)
            ins["coupling"] = (coupling, SMEM)
            ins["field"] = (field, SMEM)
            ins["pot"] = (pot, VMEM)
            scratch["pad"] = VMEM((2, 80, 512), F32)
            moved += 3 << 20
        if inner:
            ins["sizes"] = (sizes, SMEM)
            ins["sym"] = (sym_row, VMEM)
            ins["amp"] = (amp, VMEM)
            scratch["full"] = VMEM((16, 512), F32)
            scratch["first"] = VMEM((2, 512), F32)
            scratch["sums"] = VMEM((16, 128), F32)
            scratch["piece"] = VMEM((16, 128), F32)
            moved += 3 << 20

        def whole(r):
            r.points = points
            if "zo" in outs:
                r.piece[...] = jnp.zeros((16, 128), F32)
            body(r)

        return call(whole, ins, outs, scratch, 400_000_000, moved)

    def y_spec(rows):
        return ((4, rows, 512), BF16)

    z_spec = ((16, 16, 128), F32)
    outer_spec = ((128, 512), F32)
    inner_spec = ((16, 512), F32)
    end_spec = ((8, 512), F32)


    def begin(r):
        first = []
        term = []
        for comp in range(2):
            u = r.psi[comp].T
            r.u[comp * 64 : (comp + 1) * 64, :] = u
            term.append(u)
            first.append(u[0:1, :])
        r.pot_o[...] = r.potential[...].astype(F32).T
        low_out(r, term)
        ends_out(r, term)
        state = jnp.where(mask_of(r), r.given[...], 0.0)
        r.state[...] = state
        state_out(r, state, 128)
        first_rows(r, first[0], first[1])
        z_out(r)

    hams = over_x(jnp.broadcast_to(inner_ham[None], (4,) + inner_ham.shape))
    out = stage(
        begin,
        {"psi": (psi, VMEM), "potential": (potential, VMEM), "given": (first_state, VMEM)},
        {"u": outer_spec, "pot_o": ((64, 512), F32), "yo": y_spec(144), "head": end_spec, "tail": end_spec,
         "state": inner_spec, "zo": z_spec},
    )
    pot = out["pot_o"]
    u0, state0 = out["u"], out["state"]
    ya, yb = over_y(out["yo"])
    zr = over_z(out["zo"])
    left, right = halos(out)


    def end0(r):
        copies = fetch(r)
        ham_rows(r, r.state[...])
        part = surface_part(r, *first_received(r))
        surface_out(r, part, 128)
        for copy in copies:
            copy.wait()
        images = outer_image(r, dipole_image(r))
        more = ghost_image(r, ghost_of(r, 128))
        term = term_of([a + b for a, b in zip(images, more)], 1)
        for comp in range(2):
            r.u_o[comp * 64 : (comp + 1) * 64, :] = term[comp]
        first_rows(r, term[0][0:1, :], term[1][0:1, :])
        z_out(r)
        low_out(r, term)
        ends_out(r, term)

    out = stage(
        end0,
        {"ya": (ya, pl.ANY), "yb": (yb, pl.ANY), "zr": (zr, VMEM), "u": (u0, VMEM), "left": (left, VMEM),
         "right": (right, VMEM), "state": (state0, VMEM), "ham": (hams, VMEM)},
        {"u_o": outer_spec, "yo": y_spec(160), "zo": z_spec, "head": end_spec, "tail": end_spec},
        rows=144, low=True,
    )
    u1 = out["u_o"]
    ya, yb = over_y(out["yo"])
    zr = over_z(out["zo"])
    left, right = halos(out)


    def end1(r):
        copies = fetch(r)
        part = surface_part(r, *first_received(r))
        surface_out(r, part, 16)
        ham = ham_full(r)
        for copy in copies:
            copy.wait()
        state = next_state(r, ham, surface_of(r, 128), 1)
        r.state_o[...] = state
        state_out(r, state, 0)
        ham_rows(r, state)
        z_out(r)

    def outer1(r):
        copies = fetch(r)
        for copy in copies:
            copy.wait()
        term = term_of(outer_image(r, dipole_image(r)), 2)
        for comp in range(2):
            r.u_o[comp * 64 : (comp + 1) * 64, :] = term[comp]

    y_in = {"ya": (ya, pl.ANY), "yb": (yb, pl.ANY)}
    out = stage(
        end1,
        {**y_in, "zr": (zr, VMEM), "ham": (hams, VMEM)},
        {"yo": y_spec(48), "zo": z_spec, "state_o": inner_spec},
        rows=160,
    )
    state1 = out["state_o"]
    ya, yb = over_y(out["yo"])
    zr = over_z(out["zo"])
    base2 = stage(
        outer1,
        {**y_in, "u": (u1, VMEM), "left": (left, VMEM), "right": (right, VMEM)},
        {"u_o": outer_spec},
        rows=160, low=True, inner=False,
    )["u_o"]


    def end2(r):
        copies = fetch(r)
        ham = ham_full(r)
        for copy in copies:
            copy.wait()
        state = next_state(r, ham, surface_of(r, 16), 2)
        r.state_o[...] = state
        state_out(r, state, 128)
        more = term_of(ghost_image(r, ghost_of(r, 0)), 2)
        term = [r.u[comp * 64 : (comp + 1) * 64, :] + more[comp] for comp in range(2)]
        for comp in range(2):
            r.u_o[comp * 64 : (comp + 1) * 64, :] = term[comp]
        first = (term[0][0:1, :], term[1][0:1, :])
        first_rows(r, *first)
        ham_rows(r, state)
        z_out(r)
        low_out(r, term)
        ends_out(r, term)
        surface_out(r, surface_part(r, *first), 144)

    out = stage(
        end2,
        {"ya": (ya, pl.ANY), "yb": (yb, pl.ANY), "zr": (zr, VMEM), "u": (base2, VMEM), "ham": (hams, VMEM)},
        {"u_o": outer_spec, "yo": y_spec(176), "zo": z_spec, "head": end_spec, "tail": end_spec, "state_o": inner_spec},
        rows=48,
    )
    u2, state2 = out["u_o"], out["state_o"]
    ya, yb = over_y(out["yo"])
    zr = over_z(out["zo"])
    left, right = halos(out)


    def end3(r):
        copies = fetch(r)
        ham = ham_full(r)
        r.ham_o[...] = ham
        part = surface_part(r, *first_received(r))
        surface_out(r, part, 144)
        for copy in copies:
            copy.wait()
        state_out(r, next_state(r, ham, surface_of(r, 144), 3), 128)
        images = outer_image(r, dipole_image(r))
        more = ghost_image(r, ghost_of(r, 128))
        term = term_of([a + b for a, b in zip(images, more)], 3)
        for comp in range(2):
            r.u_o[comp * 64 : (comp + 1) * 64, :] = term[comp]
        first_rows(r, term[0][0:1, :], term[1][0:1, :])
        z_out(r)
        low_out(r, term)
        ends_out(r, term)

    out = stage(
        end3,
        {"ya": (ya, pl.ANY), "yb": (yb, pl.ANY), "zr": (zr, VMEM), "u": (u2, VMEM), "left": (left, VMEM),
         "right": (right, VMEM)},
        {"u_o": outer_spec, "yo": y_spec(176), "zo": z_spec, "head": end_spec, "tail": end_spec, "ham_o": inner_spec},
        rows=176, low=True,
    )
    u3, image2 = out["u_o"], out["ham_o"]
    ya, yb = over_y(out["yo"])
    zr = over_z(out["zo"])
    left, right = halos(out)


    def end4(r):
        copies = fetch(r)
        surface_out(r, surface_part(r, *first_received(r)), 0)
        for copy in copies:
            copy.wait()
        state = next_state(r, r.image[...], surface_of(r, 144), 3)
        r.state_o[...] = state
        ham_rows(r, state)
        z_out(r)

    def outer4(r):
        copies = fetch(r)
        for copy in copies:
            copy.wait()
        images = outer_image(r, dipole_image(r))
        more = ghost_image(r, ghost_of(r, 128))
        term = term_of([a + b for a, b in zip(images, more)], 4)
        for comp in range(2):
            at = slice(comp * 64, (comp + 1) * 64)
            total = r.u0[at, :] + r.u1[at, :] + r.u2[at, :] + r.u[at, :] + term[comp]
            r.psi_o[comp] = total.T

    y_in = {"ya": (ya, pl.ANY), "yb": (yb, pl.ANY)}
    out = stage(
        end4,
        {**y_in, "zr": (zr, VMEM), "image": (image2, VMEM), "ham": (hams, VMEM)},
        {"yo": y_spec(32), "zo": z_spec, "state_o": inner_spec},
        rows=176,
    )
    state3 = out["state_o"]
    ya, yb = over_y(out["yo"])
    zr = over_z(out["zo"])
    psi_next = stage(
        outer4,
        {**y_in, "u": (u3, VMEM), "u0": (u0, VMEM), "u1": (u1, VMEM), "u2": (u2, VMEM), "left": (left, VMEM),
         "right": (right, VMEM)},
        {"psi_o": ((2, 512, 64), F32)},
        rows=176, low=True,
    )["psi_o"]


    def end5(r):
        copies = fetch(r)
        ham = ham_full(r)
        for copy in copies:
            copy.wait()
        state = next_state(r, ham, surface_of(r, 0), 4)
        total = r.s0[...] + r.s1[...] + r.s2[...] + r.s3[...] + state
        for x in range(4):
            r.sum_o[x] = total

    total = stage(
        end5,
        {"ya": (ya, pl.ANY), "yb": (yb, pl.ANY), "zr": (zr, VMEM), "s0": (state0, VMEM), "s1": (state1, VMEM),
         "s2": (state2, VMEM), "s3": (state3, VMEM)},
        {"sum_o": ((4, 16, 512), F32)},
        rows=32,
    )["sum_o"]
    state_next = over_x(total)[0].reshape(2, 4, 2, 512).transpose(0, 2, 1, 3).reshape(2, 2, 2048)
    return psi_next, state_next


def solution(mesh):
    return jax.shard_map(
        shards,
        mesh=mesh,
        in_specs=(
            P(None, "chan", "sector"),
            P("chan", "sector"),
            P("chan", None, None, None),
            P("chan", None),
            P("chan", None),
            P("chan"),
            P("chan"),
            P("chan", "sector", None),
            P(None, "chan", None),
            P(),
        ),
        out_specs=(P(None, "chan", "sector"), P(None, "chan", None)),
        check_vma=False,
    )
```

time: 1030 us -> 315 us (0.31)
  blocking collectives: 777 us -> 144 us
  waiting for transfers between devices: 138 us -> 30.7 us
  starting transfers between devices: 27.3 us -> 66.5 us
  matrix products: 23.3 us -> 0 us
  Pallas kernels: 0 us -> 23.1 us
  between operations: 16.3 us -> 1.94 us
  other arithmetic: 14.4 us -> 0.08 us
  local copies, waits for them, and re-layouts: 33.2 us -> 45.4 us
    all_gather x8 -> x0, blocking collectives: 503 us -> none  [the longest x4 451 us: shards(): ham_rows = lax.all_gather(own_rows, 'sector', axis=2, tiled=True)]
    psum x2 -> x0, blocking collectives: 274 us -> none  [from_root(): return lax.psum(kept, axis)]
    all_to_all x0 -> x9, blocking collectives: none -> 144 us  [the longest x6 72.4 us: over_y(): mine = lax.all_to_all(piece, 'chan', 0, 0, axis_index_groups=y_groups)]
    unnamed x8 -> x0, waiting for transfers between devices: 138 us -> none
    unnamed x82 -> x147, local copies, waits for them, and re-layouts: 7.46 us -> 42.1 us
    all_to_all x0 -> x5, starting transfers between devices: none -> 31.7 us  [the longest x3 22 us: over_z(): return lax.all_to_all(piece, 'sector', 0, 0, axis_index_groups=z_groups)]
    dot_general x16 -> x0, matrix products: 23.3 us -> none  [the longest x4 11.1 us: shards(): jnp.einsum('bjci,zbjip->zbcp', dipole, picked, preferred_element_type=jnp...]
    pallas_call x0 -> x9, Pallas kernels: none -> 23.1 us  [call(): pl.pallas_call(kernel, out_shape=[jax.ShapeDtypeStruct(shape, kind) for s...]
  transfers between devices with their start and end apart: 14 -> 19, of which waited for: 2 -> 8; matrix products, arithmetic and copies ran while one was open for 4% -> 1% of each run, Pallas kernels for 0% -> 2%
where the time goes in v1:
time: 315 us; the launch traced here: 312 us
  blocking collectives  144 us (46%)
  starting transfers between devices  66.5 us (21%)
  local copies, waits for them, and re-layouts  45.4 us (14%)
  waiting for transfers between devices  30.7 us (10%)
  Pallas kernels  23.1 us (7%)
    all_to_all x6, blocking collectives, over_y(): mine = lax.all_to_all(piece, 'chan', 0, 0, axis_index_groups=y_groups)  72.4 us
    all_to_all x3, blocking collectives, over_z(): return lax.all_to_all(piece, 'sector', 0, 0, axis_index_groups=z_groups)  71.7 us
    unnamed x147, local copies, waits for them, and re-layouts  42.1 us
    pallas_call x9, Pallas kernels, call(): pl.pallas_call(kernel, out_shape=[jax.ShapeDtypeStruct(shape, kind) for s...  23.1 us
    all_to_all x3, starting transfers between devices, over_z(): return lax.all_to_all(piece, 'sector', 0, 0, axis_index_groups=z_groups)  22 us
    ppermute x4, waiting for transfers between devices, halos(): lax.ppermute(out['head'], 'sector', down)  15 us
    ppermute x4, starting transfers between devices, halos(): lax.ppermute(out['head'], 'sector', down)  13.7 us
    all_to_all x3, waiting for transfers between devices, over_z(): return lax.all_to_all(piece, 'sector', 0, 0, axis_index_groups=z_groups)  12.9 us
  transfers between devices with their start and end apart: 19, of which 8 were waited for; matrix products, arithmetic and copies ran while one was open for 1% of the time, Pallas kernels for 2%

profile of v1, /device:TPU:6, one launch (start us, length us, event | category | flops | bytes accessed | tf_op | source)
XLA Modules:
  0.0 311.8 jit_solution(17899026594523304680)
XLA Ops:
  3.6 1.6 copy-done
  9.2 14.5 %all_to_all.70.refs_0_ = bf16[4,144,512]{2,1,0:T(8,128)(2,1)} all-to-all(bf16[4,144,512]{2,1,0:T(8,128)(2,1)S(1)} %get-tuple-element.32), channel_id=1, replica_groups={{0,2,4,6},{1,3,5,7},{8,10,12,14},{9,11,13,15},{16,18,20,22},{17,19,21,2..., dimensions={0} | all-to-all | bytes 1179648 | tf_op jit(solution)/shard_map/all_to_all | solution.py:250
  23.7 28.6 %all_to_all.71.refs_2_ = f32[16,16,128]{2,1,0:T(8,128)} all-to-all(f32[16,16,128]{2,1,0:T(8,128)S(1)} %get-tuple-element.33), channel_id=1, replica_groups={{0,32,64,96,128,160,192,224,256,288,320,352,384,416,448,480},{8,40,72,1..., dimensions={0} | all-to-all | bytes 262144 | tf_op jit(solution)/shard_map/all_to_all | solution.py:254
  53.4 4.8 %all-to-all-start.2 = ((bf16[4,2,32,2048]{3,2,1,0:T(8,128)(2,1)}), bf16[4,2,32,2048]{3,2,1,0:T(8,128)(2,1)S(1)}, u32[]{:S(2)}, u32[]{:S(2)}) async-start(bf16[4,2,32,2048]{3,2,1,0:T(8,128)(2,1)} %broadcast_in_dim.2), calls=%async_computation.2 | async-start | bytes 2097152 | tf_op jit(solution)/shard_map/all_to_all | solution.py:257
  58.2 1.9 collective-permute-start
  60.1 2.4 collective-permute-start.1
  62.5 3.4 %collective-permute-start.2 = (f32[8,512]{1,0:T(8,128)}, f32[8,512]{1,0:T(8,128)S(1)}, u32[]{:S(2)}, u32[]{:S(2)}) collective-permute-start(f32[8,512]{1,0:T(8,128)} %copy-done.67), channel_id=1, source_target_pairs={{8,0},{16,8},{24,16},{32,24},{40,32},{48,40},{56,48},{64,56},{72,6... | collective-permute-start | bytes 49160 | tf_op jit(solution)/shard_map/ppermute | solution.py:260
  68.4 2.0 collective-permute-done.2.refs_5_
  71.1 1.6 copy-done.2
  76.9 3.9 %shard_map.114 = (f32[128,512]{1,0:T(8,128)S(1)}, bf16[4,160,512]{2,1,0:T(8,128)(2,1)S(1)}, f32[16,16,128]{2,1,0:T(8,128)S(1)}, f32[8,512]{1,0:T(8,128)S(1)}, f32[8,512]{1,0:T(8,128)S(1)}) custom-call(bf16[4,144,512]{2,1,0:T(8,128)(2,1)S(1)} %copy-done.14, bf16[4,144,512]{2,1,0:T(8,128)(2,1)} %collective-permute-done.refs_1_, f32[16,16,128]{2,1,0:T(8,128)S(1)} %copy-done.29, ...), custom_call_target="tpu_custom_call" | custom-call | flops 400000000 | bytes 7340032 | tf_op jit(solution)/shard_map/pallas_call | solution.py:24
  80.8 12.8 %all_to_all.72.refs_0_ = bf16[4,160,512]{2,1,0:T(8,128)(2,1)S(1)} all-to-all(bf16[4,160,512]{2,1,0:T(8,128)(2,1)S(1)} %get-tuple-element.39), channel_id=1, replica_groups={{0,2,4,6},{1,3,5,7},{8,10,12,14},{9,11,13,15},{16,18,20,22},{17,19,21,2..., dimensions={0} | all-to-all | bytes 1310720 | tf_op jit(solution)/shard_map/all_to_all | solution.py:250
  93.6 1.9 collective-permute-start.3
  95.6 20.0 %all_to_all.73.refs_2_ = f32[16,16,128]{2,1,0:T(8,128)S(1)} all-to-all(f32[16,16,128]{2,1,0:T(8,128)S(1)} %get-tuple-element.40), channel_id=1, replica_groups={{0,32,64,96,128,160,192,224,256,288,320,352,384,416,448,480},{8,40,72,1..., dimensions={0} | all-to-all | bytes 262144 | tf_op jit(solution)/shard_map/all_to_all | solution.py:254
  115.5 2.2 shard_map.115
  117.8 8.7 %all_to_all.74.refs_0_ = bf16[4,48,512]{2,1,0:T(8,128)(2,1)S(1)} all-to-all(bf16[4,48,512]{2,1,0:T(8,128)(2,1)S(1)} %get-tuple-element.41), channel_id=1, replica_groups={{0,2,4,6},{1,3,5,7},{8,10,12,14},{9,11,13,15},{16,18,20,22},{17,19,21,2..., dimensions={0} | all-to-all | bytes 393216 | tf_op jit(solution)/shard_map/all_to_all | solution.py:250
  126.5 5.2 %all-to-all-start.6 = ((f32[16,16,128]{2,1,0:T(8,128)}), f32[16,16,128]{2,1,0:T(8,128)}, u32[]{:S(2)}, u32[]{:S(2)}) async-start(f32[16,16,128]{2,1,0:T(8,128)} %copy-done.43), calls=%async_computation.6 | async-start | bytes 262144 | tf_op jit(solution)/shard_map/all_to_all | solution.py:254
  131.7 1.9 collective-permute-start.4
  133.6 2.1 collective-permute-start.5
  135.7 3.7 %collective-permute-start.6 = (f32[8,512]{1,0:T(8,128)}, f32[8,512]{1,0:T(8,128)S(1)}, u32[]{:S(2)}, u32[]{:S(2)}) collective-permute-start(f32[8,512]{1,0:T(8,128)} %copy-done.65), channel_id=1, source_target_pairs={{8,0},{16,8},{24,16},{32,24},{40,32},{48,40},{56,48},{64,56},{72,6... | collective-permute-start | bytes 49160 | tf_op jit(solution)/shard_map/ppermute | solution.py:260
  139.5 4.2 %collective-permute-done.6.refs_4_ = f32[8,512]{1,0:T(8,128)S(1)} collective-permute-done((f32[8,512]{1,0:T(8,128)}, f32[8,512]{1,0:T(8,128)S(1)}, u32[]{:S(2)}, u32[]{:S(2)}) %collective-permute-start.6) | collective-permute-done | bytes 16416 | tf_op jit(solution)/shard_map/ppermute | solution.py:260
  143.7 1.6 copy-done.3
  148.4 2.0 shard_map.116.refs_3_
  154.6 3.3 %shard_map.117 = (f32[128,512]{1,0:T(8,128)S(1)}, bf16[4,176,512]{2,1,0:T(8,128)(2,1)S(1)}, f32[16,16,128]{2,1,0:T(8,128)S(1)}, f32[8,512]{1,0:T(8,128)S(1)}, f3...) custom-call(bf16[4,48,512]{2,1,0:T(8,128)(2,1)S(1)} %copy-done.28, bf16[4,48,512]{2,1,0:T(8,128)(2,1)S(1)} %copy-done.35, ...), custom_call_target="tpu_custom_call" | custom-call | flops 400000000 | bytes 4194304 | tf_op jit(solution)/shard_map/pallas_call | solution.py:24
  157.9 14.7 %all_to_all.75.refs_0_ = bf16[4,176,512]{2,1,0:T(8,128)(2,1)} all-to-all(bf16[4,176,512]{2,1,0:T(8,128)(2,1)S(1)} %get-tuple-element.46), channel_id=1, replica_groups={{0,2,4,6},{1,3,5,7},{8,10,12,14},{9,11,13,15},{16,18,20,22},{17,19,21,2..., dimensions={0} | all-to-all | bytes 1441792 | tf_op jit(solution)/shard_map/all_to_all | solution.py:250
  172.7 1.9 collective-permute-start.7
  174.6 11.6 %all-to-all-start.8 = ((f32[16,16,128]{2,1,0:T(8,128)}), f32[16,16,128]{2,1,0:T(8,128)}, u32[]{:S(2)}, u32[]{:S(2)}) async-start(f32[16,16,128]{2,1,0:T(8,128)} %copy-done.44), calls=%async_computation.8 | async-start | bytes 262144 | tf_op jit(solution)/shard_map/all_to_all | solution.py:254
  186.2 3.0 collective-permute-start.8
  189.3 2.8 collective-permute-start.9
  192.7 4.5 %collective-permute-done.9.refs_5_ = f32[8,512]{1,0:T(8,128)S(1)} collective-permute-done((f32[8,512]{1,0:T(8,128)}, f32[8,512]{1,0:T(8,128)S(1)}, u32[]{:S(2)}, u32[]{:S(2)}) %collective-permute-start.9) | collective-permute-done | bytes 16416 | tf_op jit(solution)/shard_map/ppermute | solution.py:260
  197.8 3.0 all-to-all-done.8.refs_2_
  200.8 1.6 copy-done.4
  203.9 4.1 %shard_map.118 = (f32[128,512]{1,0:T(8,128)S(1)}, bf16[4,176,512]{2,1,0:T(8,128)(2,1)S(1)}, f32[16,16,128]{2,1,0:T(8,128)S(1)}, f32[8,512]{1,0:T(8,128)S(1)}, f3...) custom-call(bf16[4,176,512]{2,1,0:T(8,128)(2,1)} %all_to_all.75.refs_0_, bf16[4,176,512]{2,1,0:T(8,128)(2,1)} %collective-permute-done.7.refs_1_, ...), custom_call_target="tpu_custom_call" | custom-call | flops 400000000 | bytes 7340032 | tf_op jit(solution)/shard_map/pallas_call | solution.py:24
  208.1 12.5 %all_to_all.76.refs_0_ = bf16[4,176,512]{2,1,0:T(8,128)(2,1)S(1)} all-to-all(bf16[4,176,512]{2,1,0:T(8,128)(2,1)S(1)} %get-tuple-element.51), channel_id=1, replica_groups={{0,2,4,6},{1,3,5,7},{8,10,12,14},{9,11,13,15},{16,18,20,22},{17,19,21,2..., dimensions={0} | all-to-all | bytes 1441792 | tf_op jit(solution)/shard_map/all_to_all | solution.py:250
  220.6 1.9 collective-permute-start.10
  222.5 23.1 %all_to_all.77.refs_2_ = f32[16,16,128]{2,1,0:T(8,128)S(1)} all-to-all(f32[16,16,128]{2,1,0:T(8,128)S(1)} %get-tuple-element.55), channel_id=1, replica_groups={{0,32,64,96,128,160,192,224,256,288,320,352,384,416,448,480},{8,40,72,1..., dimensions={0} | all-to-all | bytes 262144 | tf_op jit(solution)/shard_map/all_to_all | solution.py:254
  245.6 2.3 shard_map.120
  248.0 9.1 %all_to_all.78.refs_0_ = bf16[4,32,512]{2,1,0:T(8,128)(2,1)} all-to-all(bf16[4,32,512]{2,1,0:T(8,128)(2,1)S(1)} %get-tuple-element.57), channel_id=1, replica_groups={{0,2,4,6},{1,3,5,7},{8,10,12,14},{9,11,13,15},{16,18,20,22},{17,19,21,2..., dimensions={0} | all-to-all | bytes 262144 | tf_op jit(solution)/shard_map/all_to_all | solution.py:250
  257.2 5.2 %all-to-all-start.12 = ((f32[16,16,128]{2,1,0:T(8,128)}), f32[16,16,128]{2,1,0:T(8,128)}, u32[]{:S(2)}, u32[]{:S(2)}) async-start(f32[16,16,128]{2,1,0:T(8,128)} %copy-done.45), calls=%async_computation.12 | async-start | bytes 262144 | tf_op jit(solution)/shard_map/all_to_all | solution.py:254
  262.4 1.9 collective-permute-start.13
  264.3 1.5 collective-permute-done.13.refs_1_
  266.5 9.9 %all-to-all-done.12.refs_2_ = f32[16,16,128]{2,1,0:T(8,128)} async-done(((f32[16,16,128]{2,1,0:T(8,128)}), f32[16,16,128]{2,1,0:T(8,128)}, u32[]{:S(2)}, u32[]{:S(2)}) %all-to-all-start.12) | async-done | bytes 131104 | tf_op jit(solution)/shard_map/all_to_all | solution.py:254
  283.3 4.9 %all-to-all-start.13 = ((f32[4,16,512]{2,1,0:T(8,128)}), f32[4,16,512]{2,1,0:T(8,128)}, u32[]{:S(2)}, u32[]{:S(2)}) async-start(f32[4,16,512]{2,1,0:T(8,128)} %copy-done.30), calls=%async_computation.13 | async-start | bytes 262144 | tf_op jit(solution)/shard_map/all_to_all | solution.py:257
  288.2 2.1 collective-permute-start.11
  290.3 3.7 %collective-permute-start.12 = (f32[8,512]{1,0:T(8,128)}, f32[8,512]{1,0:T(8,128)S(1)}, u32[]{:S(2)}, u32[]{:S(2)}) collective-permute-start(f32[8,512]{1,0:T(8,128)} %copy-done.63), channel_id=1, source_target_pairs={{8,0},{16,8},{24,16},{32,24},{40,32},{48,40},{56,48},{64,56},{72,6... | collective-permute-start | bytes 49160 | tf_op jit(solution)/shard_map/ppermute | solution.py:260
  294.0 4.2 %collective-permute-done.12.refs_7_ = f32[8,512]{1,0:T(8,128)S(1)} collective-permute-done((f32[8,512]{1,0:T(8,128)}, f32[8,512]{1,0:T(8,128)S(1)}, u32[]{:S(2)}, u32[]{:S(2)}) %collective-permute-start.12) | collective-permute-done | bytes 16416 | tf_op jit(solution)/shard_map/ppermute | solution.py:260
  298.3 1.6 copy-done.5
  304.6 3.1 shard_map.119
  308.5 1.9 copy.16
  (160 shorter events, 39.0 us)
Async XLA Ops:
  6.6 45.8 %copy-start.71 = (bf16[2,32,2048]{2,1,0:T(8,128)(2,1)S(1)}, bf16[2,32,2048]{2,1,0:T(8,128)(2,1)}, u32[]{:S(2)}) copy-start(bf16[2,32,2048]{2,1,0:T(8,128)(2,1)} %param.17) | copy-start | bytes 786436
  9.2 61.9 %copy-start.18 = (f32[128,512]{1,0:T(8,128)}, f32[128,512]{1,0:T(8,128)S(1)}, u32[]{:S(2)}) copy-start(f32[128,512]{1,0:T(8,128)S(1)} %get-tuple-element.34.refs_3_) | copy-start | bytes 786436
  9.2 191.7 %copy-start.15 = (f32[64,512]{1,0:T(8,128)}, f32[64,512]{1,0:T(8,128)S(1)}, u32[]{:S(2)}) copy-start(f32[64,512]{1,0:T(8,128)S(1)} %get-tuple-element.38.refs_12_.refs_9_.refs_10_) | copy-start | bytes 393220
  23.7 47.4 %copy-start.1 = (bf16[512,2048]{1,0:T(8,128)(2,1)S(1)}, bf16[512,2048]{1,0:T(8,128)(2,1)}, u32[]{:S(2)}) copy-start(bf16[512,2048]{1,0:T(8,128)(2,1)} %refs_10_.5) | copy-start | bytes 6291460
  23.7 47.4 %copy-start.37 = (s32[512]{0:T(512)S(1)}, s32[512]{0:T(512)}, u32[]{:S(2)}) copy-start(s32[512]{0:T(512)} %param.15) | copy-start | bytes 6148
  23.7 47.4 %copy-start.53 = (s32[2]{0:T(128)S(1)}, s32[2]{0:T(128)}, u32[]{:S(2)}) copy-start(s32[2]{0:T(128)} %refs_8_.8) | copy-start | bytes 28
  23.7 47.4 %copy-start.62 = (s32[2,8]{1,0:T(2,128)S(1)}, s32[2,8]{1,0:T(2,128)}, u32[]{:S(2)}) copy-start(s32[2,8]{1,0:T(2,128)} %refs_10_.4) | copy-start | bytes 196
  53.4 17.6 %all-to-all-start.2 = ((bf16[4,2,32,2048]{3,2,1,0:T(8,128)(2,1)}), bf16[4,2,32,2048]{3,2,1,0:T(8,128)(2,1)S(1)}, u32[]{:S(2)}, u32[]{:S(2)}) async-start(bf16[4,2,32,2048]{3,2,1,0:T(8,128)(2,1)} %broadcast_in_dim.2), calls=%async_computation.2 | async-start | bytes 2097152 | tf_op jit(solution)/shard_map/all_to_all | solution.py:257
  58.2 12.9 %collective-permute-start = (bf16[4,144,512]{2,1,0:T(8,128)(2,1)}, bf16[4,144,512]{2,1,0:T(8,128)(2,1)}, u32[]{:S(2)}, u32[]{:S(2)}) collective-permute-start(bf16[4,144,512]{2,1,0:T(8,128)(2,1)} %all_to_all.70.refs_0_), channel_id=1, source_target_pairs={{0,1},{1,0},{2,3},{3,2},{4,5},{5,4},{6,7},{7,6},{8,9},{9,8},{10,11... | collective-permute-start | bytes 1769480 | tf_op jit(solution)/shard_map/ppermute | solution.py:251
  60.1 7.7 %collective-permute-start.1 = (f32[8,512]{1,0:T(8,128)}, f32[8,512]{1,0:T(8,128)S(1)}, u32[]{:S(2)}, u32[]{:S(2)}) collective-permute-start(f32[8,512]{1,0:T(8,128)} %copy-done.68), channel_id=1, source_target_pairs={{0,8},{8,16},{16,24},{24,32},{32,40},{40,48},{48,56},{56,64},{64,7... | collective-permute-start | bytes 49160 | tf_op jit(solution)/shard_map/ppermute | solution.py:260
  62.5 8.0 %collective-permute-start.2 = (f32[8,512]{1,0:T(8,128)}, f32[8,512]{1,0:T(8,128)S(1)}, u32[]{:S(2)}, u32[]{:S(2)}) collective-permute-start(f32[8,512]{1,0:T(8,128)} %copy-done.67), channel_id=1, source_target_pairs={{8,0},{16,8},{24,16},{32,24},{40,32},{48,40},{56,48},{64,56},{72,6... | collective-permute-start | bytes 49160 | tf_op jit(solution)/shard_map/ppermute | solution.py:260
  80.8 36.9 %copy-start.20 = (f32[128,512]{1,0:T(8,128)}, f32[128,512]{1,0:T(8,128)S(1)}, u32[]{:S(2)}) copy-start(f32[128,512]{1,0:T(8,128)S(1)} %get-tuple-element.43.refs_2_.refs_4_) | copy-start | bytes 786436
  80.8 36.9 %copy-start.65 = (f32[8,512]{1,0:T(8,128)}, f32[8,512]{1,0:T(8,128)S(1)}, u32[]{:S(2)}) copy-start(f32[8,512]{1,0:T(8,128)S(1)} %get-tuple-element.45) | copy-start | bytes 49156
  80.8 36.9 %copy-start.66 = (f32[8,512]{1,0:T(8,128)}, f32[8,512]{1,0:T(8,128)S(1)}, u32[]{:S(2)}) copy-start(f32[8,512]{1,0:T(8,128)S(1)} %get-tuple-element.44) | copy-start | bytes 49156
  93.6 24.1 %copy-start.8 = (bf16[4,160,512]{2,1,0:T(8,128)(2,1)}, bf16[4,160,512]{2,1,0:T(8,128)(2,1)S(1)}, u32[]{:S(2)}) copy-start(bf16[4,160,512]{2,1,0:T(8,128)(2,1)S(1)} %all_to_all.72.refs_0_) | copy-start | bytes 1966084
  93.6 21.9 %collective-permute-start.3 = (bf16[4,160,512]{2,1,0:T(8,128)(2,1)S(1)}, bf16[4,160,512]{2,1,0:T(8,128)(2,1)S(1)}, u32[]{:S(2)}, u32[]{:S(2)}) collective-permute-start(bf16[4,160,512]{2,1,0:T(8,128)(2,1)S(1)} %all_to_all.72.refs_0_), channel_id=1, source_target_pairs={{0,1},{1,0},{2,3},{3,2},{4,5},{5,4},{6,7},{7,6},{8,9},{9,8},{10,11... | collective-permute-start | bytes 1966088 | tf_op jit(solution)/shard_map/ppermute | solution.py:251
  115.5 2.2 copy-start.12
  117.8 8.7 %copy-start.43 = (f32[16,16,128]{2,1,0:T(8,128)}, f32[16,16,128]{2,1,0:T(8,128)S(1)}, u32[]{:S(2)}) copy-start(f32[16,16,128]{2,1,0:T(8,128)S(1)} %get-tuple-element.42) | copy-start | bytes 393220
  117.8 8.7 %copy-start.46 = (f32[16,512]{1,0:T(8,128)}, f32[16,512]{1,0:T(8,128)S(1)}, u32[]{:S(2)}) copy-start(f32[16,512]{1,0:T(8,128)S(1)} %get-tuple-element.59.refs_4_) | copy-start | bytes 98308
  126.5 23.9 %copy-start.27 = (bf16[4,48,512]{2,1,0:T(8,128)(2,1)}, bf16[4,48,512]{2,1,0:T(8,128)(2,1)S(1)}, u32[]{:S(2)}) copy-start(bf16[4,48,512]{2,1,0:T(8,128)(2,1)S(1)} %all_to_all.74.refs_0_) | copy-start | bytes 589828
  126.5 25.3 %all-to-all-start.6 = ((f32[16,16,128]{2,1,0:T(8,128)}), f32[16,16,128]{2,1,0:T(8,128)}, u32[]{:S(2)}, u32[]{:S(2)}) async-start(f32[16,16,128]{2,1,0:T(8,128)} %copy-done.43), calls=%async_computation.6 | async-start | bytes 262144 | tf_op jit(solution)/shard_map/all_to_all | solution.py:254
  131.7 19.4 %collective-permute-start.4 = (bf16[4,48,512]{2,1,0:T(8,128)(2,1)S(1)}, bf16[4,48,512]{2,1,0:T(8,128)(2,1)S(1)}, u32[]{:S(2)}, u32[]{:S(2)}) collective-permute-start(bf16[4,48,512]{2,1,0:T(8,128)(2,1)S(1)} %all_to_all.74.refs_0_), channel_id=1, source_target_pairs={{0,1},{1,0},{2,3},{3,2},{4,5},{5,4},{6,7},{7,6},{8,9},{9,8},{10,11... | collective-permute-start | bytes 589832 | tf_op jit(solution)/shard_map/ppermute | solution.py:251
  133.6 5.9 %collective-permute-start.5 = (f32[8,512]{1,0:T(8,128)}, f32[8,512]{1,0:T(8,128)S(1)}, u32[]{:S(2)}, u32[]{:S(2)}) collective-permute-start(f32[8,512]{1,0:T(8,128)} %copy-done.66), channel_id=1, source_target_pairs={{0,8},{8,16},{16,24},{24,32},{32,40},{40,48},{48,56},{56,64},{64,7... | collective-permute-start | bytes 49160 | tf_op jit(solution)/shard_map/ppermute | solution.py:260
  135.7 8.0 %collective-permute-start.6 = (f32[8,512]{1,0:T(8,128)}, f32[8,512]{1,0:T(8,128)S(1)}, u32[]{:S(2)}, u32[]{:S(2)}) collective-permute-start(f32[8,512]{1,0:T(8,128)} %copy-done.65), channel_id=1, source_target_pairs={{8,0},{16,8},{24,16},{32,24},{40,32},{48,40},{56,48},{64,56},{72,6... | collective-permute-start | bytes 49160 | tf_op jit(solution)/shard_map/ppermute | solution.py:260
  157.9 14.8 %copy-start.48 = (f32[16,512]{1,0:T(8,128)}, f32[16,512]{1,0:T(8,128)S(1)}, u32[]{:S(2)}) copy-start(f32[16,512]{1,0:T(8,128)S(1)} %get-tuple-element.60.refs_5_) | copy-start | bytes 98308
  157.9 16.7 %copy-start.44 = (f32[16,16,128]{2,1,0:T(8,128)}, f32[16,16,128]{2,1,0:T(8,128)S(1)}, u32[]{:S(2)}) copy-start(f32[16,16,128]{2,1,0:T(8,128)S(1)} %get-tuple-element.47) | copy-start | bytes 393220
  157.9 16.7 %copy-start.69 = (f32[8,512]{1,0:T(8,128)}, f32[8,512]{1,0:T(8,128)S(1)}, u32[]{:S(2)}) copy-start(f32[8,512]{1,0:T(8,128)S(1)} %get-tuple-element.50) | copy-start | bytes 49156
  157.9 16.7 %copy-start.70 = (f32[8,512]{1,0:T(8,128)}, f32[8,512]{1,0:T(8,128)S(1)}, u32[]{:S(2)}) copy-start(f32[8,512]{1,0:T(8,128)S(1)} %get-tuple-element.49) | copy-start | bytes 49156
  157.9 50.1 %copy-start.23 = (f32[128,512]{1,0:T(8,128)}, f32[128,512]{1,0:T(8,128)S(1)}, u32[]{:S(2)}) copy-start(f32[128,512]{1,0:T(8,128)S(1)} %get-tuple-element.48.refs_3_.refs_5_) | copy-start | bytes 786436
  172.7 28.2 %collective-permute-start.7 = (bf16[4,176,512]{2,1,0:T(8,128)(2,1)}, bf16[4,176,512]{2,1,0:T(8,128)(2,1)}, u32[]{:S(2)}, u32[]{:S(2)}) collective-permute-start(bf16[4,176,512]{2,1,0:T(8,128)(2,1)} %all_to_all.75.refs_0_), channel_id=1, source_target_pairs={{0,1},{1,0},{2,3},{3,2},{4,5},{5,4},{6,7},{7,6},{8,9},{9,8},{10,11... | collective-permute-start | bytes 2162696 | tf_op jit(solution)/shard_map/ppermute | solution.py:251
  174.6 26.2 %all-to-all-start.8 = ((f32[16,16,128]{2,1,0:T(8,128)}), f32[16,16,128]{2,1,0:T(8,128)}, u32[]{:S(2)}, u32[]{:S(2)}) async-start(f32[16,16,128]{2,1,0:T(8,128)} %copy-done.44), calls=%async_computation.8 | async-start | bytes 262144 | tf_op jit(solution)/shard_map/all_to_all | solution.py:254
  186.2 5.9 %collective-permute-start.8 = (f32[8,512]{1,0:T(8,128)}, f32[8,512]{1,0:T(8,128)S(1)}, u32[]{:S(2)}, u32[]{:S(2)}) collective-permute-start(f32[8,512]{1,0:T(8,128)} %copy-done.70), channel_id=1, source_target_pairs={{0,8},{8,16},{16,24},{24,32},{32,40},{40,48},{48,56},{56,64},{64,7... | collective-permute-start | bytes 49160 | tf_op jit(solution)/shard_map/ppermute | solution.py:260
  189.3 8.0 %collective-permute-start.9 = (f32[8,512]{1,0:T(8,128)}, f32[8,512]{1,0:T(8,128)S(1)}, u32[]{:S(2)}, u32[]{:S(2)}) collective-permute-start(f32[8,512]{1,0:T(8,128)} %copy-done.69), channel_id=1, source_target_pairs={{8,0},{16,8},{24,16},{32,24},{40,32},{48,40},{56,48},{64,56},{72,6... | collective-permute-start | bytes 49160 | tf_op jit(solution)/shard_map/ppermute | solution.py:260
  208.0 39.9 %copy-start.32 = (f32[128,512]{1,0:T(8,128)}, f32[128,512]{1,0:T(8,128)S(1)}, u32[]{:S(2)}) copy-start(f32[128,512]{1,0:T(8,128)S(1)} %get-tuple-element.52.refs_2_) | copy-start | bytes 786436
  208.0 39.9 %copy-start.63 = (f32[8,512]{1,0:T(8,128)}, f32[8,512]{1,0:T(8,128)S(1)}, u32[]{:S(2)}) copy-start(f32[8,512]{1,0:T(8,128)S(1)} %get-tuple-element.54) | copy-start | bytes 49156
  208.0 39.9 %copy-start.64 = (f32[8,512]{1,0:T(8,128)}, f32[8,512]{1,0:T(8,128)S(1)}, u32[]{:S(2)}) copy-start(f32[8,512]{1,0:T(8,128)S(1)} %get-tuple-element.53) | copy-start | bytes 49156
  220.6 27.4 %copy-start.6 = (bf16[4,176,512]{2,1,0:T(8,128)(2,1)}, bf16[4,176,512]{2,1,0:T(8,128)(2,1)S(1)}, u32[]{:S(2)}) copy-start(bf16[4,176,512]{2,1,0:T(8,128)(2,1)S(1)} %all_to_all.76.refs_0_) | copy-start | bytes 2162692
  220.6 25.0 %collective-permute-start.10 = (bf16[4,176,512]{2,1,0:T(8,128)(2,1)S(1)}, bf16[4,176,512]{2,1,0:T(8,128)(2,1)S(1)}, u32[]{:S(2)}, u32[]{:S(2)}) collective-permute-start(bf16[4,176,512]{2,1,0:T(8,128)(2,1)S(1)} %all_to_all.76.refs_0_), channel_id=1, source_target_pairs={{0,1},{1,0},{2,3},{3,2},{4,5},{5,4},{6,7},{7,6},{8,9},{9,8},{10,11... | collective-permute-start | bytes 2162696 | tf_op jit(solution)/shard_map/ppermute | solution.py:251
  245.6 2.4 copy-start.10
  248.0 9.2 %copy-start.45 = (f32[16,16,128]{2,1,0:T(8,128)}, f32[16,16,128]{2,1,0:T(8,128)S(1)}, u32[]{:S(2)}) copy-start(f32[16,16,128]{2,1,0:T(8,128)S(1)} %get-tuple-element.58) | copy-start | bytes 393220
  248.0 9.2 %copy-start.50 = (f32[16,512]{1,0:T(8,128)}, f32[16,512]{1,0:T(8,128)S(1)}, u32[]{:S(2)}) copy-start(f32[16,512]{1,0:T(8,128)S(1)} %get-tuple-element.61.refs_6_) | copy-start | bytes 98308
  248.0 50.2 %copy-start.7 = (bf16[4,176,512]{2,1,0:T(8,128)(2,1)S(1)}, bf16[4,176,512]{2,1,0:T(8,128)(2,1)}, u32[]{:S(2)}) copy-start(bf16[4,176,512]{2,1,0:T(8,128)(2,1)} %copy-done.6) | copy-start | bytes 2162692
  248.0 50.2 %copy-start.11 = (bf16[4,176,512]{2,1,0:T(8,128)(2,1)S(1)}, bf16[4,176,512]{2,1,0:T(8,128)(2,1)}, u32[]{:S(2)}) copy-start(bf16[4,176,512]{2,1,0:T(8,128)(2,1)} %copy-done.10) | copy-start | bytes 2162692
  257.2 19.2 %all-to-all-start.12 = ((f32[16,16,128]{2,1,0:T(8,128)}), f32[16,16,128]{2,1,0:T(8,128)}, u32[]{:S(2)}, u32[]{:S(2)}) async-start(f32[16,16,128]{2,1,0:T(8,128)} %copy-done.45), calls=%async_computation.12 | async-start | bytes 262144 | tf_op jit(solution)/shard_map/all_to_all | solution.py:254
  262.4 3.5 %collective-permute-start.13 = (bf16[4,32,512]{2,1,0:T(8,128)(2,1)}, bf16[4,32,512]{2,1,0:T(8,128)(2,1)S(1)}, u32[]{:S(2)}, u32[]{:S(2)}) collective-permute-start(bf16[4,32,512]{2,1,0:T(8,128)(2,1)} %all_to_all.78.refs_0_), channel_id=1, source_target_pairs={{0,1},{1,0},{2,3},{3,2},{4,5},{5,4},{6,7},{7,6},{8,9},{9,8},{10,11... | collective-permute-start | bytes 393224 | tf_op jit(solution)/shard_map/ppermute | solution.py:251
  283.3 27.1 %all-to-all-start.13 = ((f32[4,16,512]{2,1,0:T(8,128)}), f32[4,16,512]{2,1,0:T(8,128)}, u32[]{:S(2)}, u32[]{:S(2)}) async-start(f32[4,16,512]{2,1,0:T(8,128)} %copy-done.30), calls=%async_computation.13 | async-start | bytes 262144 | tf_op jit(solution)/shard_map/all_to_all | solution.py:257
  288.2 5.8 %collective-permute-start.11 = (f32[8,512]{1,0:T(8,128)}, f32[8,512]{1,0:T(8,128)S(1)}, u32[]{:S(2)}, u32[]{:S(2)}) collective-permute-start(f32[8,512]{1,0:T(8,128)} %copy-done.64), channel_id=1, source_target_pairs={{0,8},{8,16},{16,24},{24,32},{32,40},{40,48},{48,56},{56,64},{64,7... | collective-permute-start | bytes 49160 | tf_op jit(solution)/shard_map/ppermute | solution.py:260
  290.3 8.0 %collective-permute-start.12 = (f32[8,512]{1,0:T(8,128)}, f32[8,512]{1,0:T(8,128)S(1)}, u32[]{:S(2)}, u32[]{:S(2)}) collective-permute-start(f32[8,512]{1,0:T(8,128)} %copy-done.63), channel_id=1, source_target_pairs={{8,0},{16,8},{24,16},{32,24},{40,32},{48,40},{56,48},{64,56},{72,6... | collective-permute-start | bytes 49160 | tf_op jit(solution)/shard_map/ppermute | solution.py:260
  (43 other events, 38.1 us)

commit v2 on v0

v2 whole, which is shorter than its diff:
```python
import itertools
from types import SimpleNamespace

import jax
import jax.numpy as jnp
from jax import lax
from jax.experimental import pallas as pl
from jax.experimental.pallas import tpu as pltpu
from jax.sharding import PartitionSpec as P


F32 = jnp.float32
BF16 = jnp.bfloat16
VMEM = pltpu.VMEM
SMEM = pltpu.SMEM
KINETIC = 1.0 / 48.0


KEPT = ("u", "state", "amp", "dipole", "ham", "mark")
BIG = ("keep_amp", "keep_dipole", "keep_ham", "ys")


def call(body, ins, outs, scratch, flops):
    arrays = dict(ins)
    scratch = dict(scratch)
    for name, value in arrays.items():
        if name not in ("info", "field") + KEPT and not name.startswith("keep_"):
            scratch[name + "_v"] = VMEM(value.shape, value.dtype)
    scratch["info_s"] = SMEM((128,), jnp.int32)
    scratch["field_s"] = SMEM((128,), F32)
    parts = {name: 4 if name in BIG else 1 for name in arrays if name not in KEPT}
    first_sem = dict(zip(parts, itertools.accumulate([0] + list(parts.values()))))
    scratch["sem"] = pltpu.SemaphoreType.DMA((sum(parts.values()),))
    names = [name if name in KEPT else "hbm_" + name for name in arrays] + list(outs) + list(scratch)

    def kernel(*refs):
        r = SimpleNamespace(**dict(zip(names, refs)))
        copies = {}

        def target(name):
            if name.startswith("keep_"):
                return getattr(r, name[5:] + "_o")
            return getattr(r, name + ("_s" if name in ("info", "field") else "_v"))

        def start(name):
            source, dest = getattr(r, "hbm_" + name), target(name)
            views = [(source, dest)]
            if name == "keep_dipole":
                views = [(source.at[b, pl.ds(j, 4)], dest.at[b, pl.ds(j, 4)]) for b in range(2) for j in (0, 4)]
            elif name in BIG:
                size = source.shape[0] // 4
                views = [(source.at[pl.ds(i * size, size)], dest.at[pl.ds(i * size, size)]) for i in range(4)]
            copies[name] = [
                pltpu.make_async_copy(view[0], view[1], r.sem.at[first_sem[name] + i]) for i, view in enumerate(views)
            ]
            for copy in copies[name]:
                copy.start()

        def wait(*wanted):
            for name in wanted:
                if name in copies:
                    for copy in copies.pop(name):
                        copy.wait()
                    setattr(r, name, target(name))

        r.wait = wait
        for name in arrays:
            if name not in KEPT:
                start(name)
        wait("info")
        body(r)
        wait(*list(copies))

    results = pl.pallas_call(
        kernel,
        out_shape=[jax.ShapeDtypeStruct(shape, kind) for shape, kind in outs.values()],
        in_specs=[pl.BlockSpec(memory_space=VMEM if name in KEPT else pltpu.HBM) for name in arrays],
        out_specs=[pl.BlockSpec(memory_space=VMEM) for _ in outs],
        scratch_shapes=list(scratch.values()),
        compiler_params=pltpu.CompilerParams(vmem_limit_bytes=52 * 1024 * 1024),
        cost_estimate=pl.CostEstimate(flops=flops, bytes_accessed=1024, transcendentals=0),
    )(*arrays.values())
    return dict(zip(outs, results))


def dot_t(a, b):
    return lax.dot_general(a, b, (((1,), (1,)), ((), ())), preferred_element_type=F32)


def dot(a, b):
    return lax.dot_general(a, b, (((1,), (0,)), ((), ())), preferred_element_type=F32)


def split(value):
    high = value.astype(BF16)
    return high, (value - high.astype(F32)).astype(BF16)


def rows_of(shape):
    return lax.broadcasted_iota(jnp.int32, shape, 0)


def ghost_of(r):
    states = jnp.concatenate([r.pr[c, 16:32, :] for c in range(8)], axis=0)
    row = rows_of((128, 512))
    quarter = (row >> 1) & 3
    total = jnp.zeros((128, 512), F32)
    for q in range(4):
        part = dot_t(states, r.amp[:, q * 512 : (q + 1) * 512])
        total = total + jnp.where(quarter == q, part, 0.0)
    block = (row >> 4) * 2 + (row & 1)
    total = jnp.where(block == r.sym[...], total, 0.0)
    comp = (row >> 3) & 1
    g0 = jnp.sum(jnp.where(comp == 0, total, 0.0), axis=0, keepdims=True)
    g1 = jnp.sum(jnp.where(comp == 1, total, 0.0), axis=0, keepdims=True)
    return g0, g1


def surface_part(r, first0, first1):
    row = rows_of((32, 512))
    block = (row >> 2) * 2 + (row & 1)
    chosen = jnp.where(block == r.sym[...], jnp.where(((row >> 1) & 1) == 0, first0, first1), 0.0)
    both = jnp.concatenate(split(chosen), axis=0)
    for q in range(4):
        part = dot(both, r.amp[:, q * 512 : (q + 1) * 512])
        r.sum[...] = part[:32] + part[32:]
        for c in range(8):
            for comp in range(2):
                at = c * 16 + comp * 8 + q * 2
                r.terms[at : at + 2, :] = r.sum[c * 4 + comp * 2 : c * 4 + comp * 2 + 2, :]


def surface_of(r):
    total = r.pr[0, 0:16, :].astype(F32)
    for c in range(1, 8):
        total = total + r.pr[c, 0:16, :].astype(F32)
    return total


def mask_of(r):
    row = rows_of((16, 512))
    lane = lax.broadcasted_iota(jnp.int32, (16, 512), 1)
    size = jnp.where((row & 1) == 0, r.info[16], r.info[17])
    return (((row >> 1) & 3) * 512 + lane) < size


def ham_full(r):
    for z in range(16):
        for comp in range(2):
            at = comp * 8 + (z // 4) * 2
            for block in range(2):
                lanes = (comp * 2 + block) * 128
                r.full[at + block : at + block + 1, (z % 4) * 128 : (z % 4 + 1) * 128] = r.zr[z, :, lanes : lanes + 128]
    return r.full[...]


def next_state(r, ham, surface, order):
    image = jnp.where(mask_of(r), ham + surface, 0.0)
    return jnp.concatenate([image[8:], -image[:8]], axis=0) * (1.0 / order)


def first_received(r):
    return r.zr[0, :, 512:1024], r.zr[0, :, 1024:1536]


def ham_rows(r, state):
    both = jnp.concatenate(split(state), axis=0)
    row = rows_of((16, 128))
    total = jnp.zeros((16, 128), F32)
    for block in range(2):
        for q in range(4):
            ham = jnp.concatenate([r.ham[x, block, :, q * 512 : (q + 1) * 512] for x in range(4)], axis=0)
            part = dot_t(both, ham)
            keep = (((row >> 1) & 3) == q) & ((row & 1) == block)
            total = total + jnp.where(keep, part[:16] + part[16:], 0.0)
    r.sums[...] = total
    for comp in range(2):
        for block in range(2):
            at = comp * 8 + block
            rows = [r.sums[at + 2 * q : at + 2 * q + 1, :] for q in range(4)]
            lanes = (comp * 2 + block) * 128
            r.piece[:, lanes : lanes + 128] = (rows[0] + rows[1]) + (rows[2] + rows[3])


def first_out(r, first0, first1):
    r.piece[:, 512:1024] = first0
    r.piece[:, 1024:1536] = first1


def z_out(r):
    piece = r.piece[...]
    for z in range(16):
        r.zo[z] = piece


def dipole_image(r):
    for b in range(2):
        total = None
        for j in range(8):
            n = r.info[b * 8 + j]
            lanes = pl.ds(pl.multiple_of((n & 1) * 256, 256), 256)
            part = dot_t(r.ys[n >> 1, 0:160, lanes], r.dipole[b, j])
            total = part if total is None else total + part
        r.dip[:, b * 256 : (b + 1) * 256] = total


def outer_term(r, order):
    images = []
    row = rows_of((80, 512))
    point = r.info[18] * 64 + row - 8
    radius = (point + 1).astype(F32) * (1.0 / r.points)
    for comp in range(2):
        u = r.u[comp * 80 : (comp + 1) * 80, :]
        r.pad[comp, 0:8, :] = jnp.zeros((8, 512), F32)
        r.pad[comp, 8:88, :] = u
        r.pad[comp, 88:96, :] = jnp.zeros((8, 512), F32)
        stencil = 16.0 * (r.pad[comp, 7:87, :] + r.pad[comp, 9:89, :]) - 30.0 * u
        stencil = stencil - (r.pad[comp, 6:86, :] + r.pad[comp, 10:90, :])
        image = -KINETIC * stencil + r.pot[...] * u + r.field[0] * radius * r.dip[comp * 80 : (comp + 1) * 80, :]
        images.append(jnp.where((point >= 0) & (point < r.all_points), image, 0.0))
    return images[1] * (1.0 / order), images[0] * (-1.0 / order)


def ghost_term(r, order):
    row = rows_of((8, 512))
    hub = jnp.where(r.info[18] == 0, 1.0 / order, 0.0).astype(F32)
    images = []
    for ghost in ghost_of(r):
        ghost = ghost * hub
        images.append(jnp.where(row == 0, (-15.0 * KINETIC) * ghost, jnp.where(row == 1, KINETIC * ghost, 0.0)))
    return images[1], -images[0]


def shards(psi, potential, dipole, coupling, amp, sym, sizes, inner_ham, inner_state, field):
    n_sector = lax.axis_size("sector")
    sector = lax.axis_index("sector")
    all_points = 64 * n_sector
    x_groups = [[z * 4 + x for x in range(4)] for z in range(16)]
    z_groups = [[z * 4 + x for z in range(16)] for x in range(4)]
    up = [(i, i + 1) for i in range(n_sector - 1)]
    down = [(i + 1, i) for i in range(n_sector - 1)]

    info = jnp.concatenate([coupling.reshape(16), sizes, sector[None].astype(jnp.int32), jnp.zeros((109,), jnp.int32)])
    common = {"info": info, "sym": sym.reshape(1, 512)}
    strength = jnp.broadcast_to(field, (128,))

    def over_z(piece):
        return lax.all_to_all(piece, "sector", 0, 0, axis_index_groups=z_groups)

    def over_x(piece):
        return lax.all_to_all(piece, "sector", 0, 0, axis_index_groups=x_groups)

    low_spec = ((160, 512), BF16)
    z_spec = ((16, 1, 1536), F32)
    outer_spec = ((160, 512), F32)
    inner_spec = ((16, 512), F32)
    end_spec = ((24, 512), F32)
    z_scratch = {"sums": VMEM((16, 128), F32), "piece": VMEM((1, 1536), F32)}
    surface_scratch = {"sum": VMEM((32, 512), F32), "terms": VMEM((128, 512), F32)}
    full_scratch = {"full": VMEM((16, 512), F32)}
    outer_scratch = {"dip": VMEM((160, 512), F32), "pad": VMEM((2, 96, 512), F32)}


    def prepare(r):
        r.wait("ham", "psi", "pot")
        for x in range(4):
            r.copies[x] = r.ham[...]
        for comp in range(2):
            r.head[comp * 8 : (comp + 1) * 8, :] = r.psi[comp, 0:8, :]
            r.tail[comp * 8 : (comp + 1) * 8, :] = r.psi[comp, 56:64, :]
        r.head[16:24, :] = r.pot[0:8, :].astype(F32)
        r.tail[16:24, :] = r.pot[56:64, :].astype(F32)

    own = {"psi": psi.transpose(0, 2, 1), "pot": potential.T}
    out = call(
        prepare,
        {"info": info, "ham": inner_ham, **own},
        {"copies": ((4,) + inner_ham.shape, BF16), "head": end_spec, "tail": end_spec},
        {}, 1_000_000,
    )
    hams = over_x(out["copies"])
    out_kept = call(
        lambda r: None, {"keep_amp": amp, "keep_dipole": dipole},
        {"amp_o": (amp.shape, BF16), "dipole_o": (dipole.shape, BF16)}, {}, 1_000_000,
    )
    amp, dipole = out_kept["amp_o"], out_kept["dipole_o"]
    left = lax.ppermute(out["tail"], "sector", up)
    right = lax.ppermute(out["head"], "sector", down)

    def begin(r):
        r.wait("psi", "pot", "left", "right", "given")
        for comp in range(2):
            for q in range(4):
                at = comp * 8 + q * 2
                r.state_o[at : at + 2, :] = r.given[comp, :, q * 512 : (q + 1) * 512]
            at = comp * 80
            r.u_o[at : at + 8, :] = r.left[comp * 8 : (comp + 1) * 8, :]
            r.u_o[at + 8 : at + 72, :] = r.psi[comp]
            r.u_o[at + 72 : at + 80, :] = r.right[comp * 8 : (comp + 1) * 8, :]
        r.pot_o[0:8, :] = r.left[16:24, :]
        r.pot_o[8:72, :] = r.pot[...].astype(F32)
        r.pot_o[72:80, :] = r.right[16:24, :]
        r.low_o[...] = r.u_o[...].astype(BF16)
        state = jnp.where(mask_of(r), r.state_o[...], 0.0)
        r.state_o[...] = state
        first_out(r, r.u_o[8:9, :], r.u_o[88:89, :])
        r.wait("keep_ham")
        r.ham = r.ham_o
        ham_rows(r, state)
        z_out(r)

    out = call(
        begin,
        {"info": info, **own, "left": left, "right": right, "given": inner_state, "keep_ham": hams},
        {"ham_o": (hams.shape, BF16), "u_o": outer_spec, "pot_o": ((80, 512), F32), "state_o": inner_spec, "low_o": low_spec, "zo": z_spec},
        z_scratch, 1_000_000_000,
    )
    outer = [out["u_o"]]
    inner = [out["state_o"]]
    pot = out["pot_o"]
    hams = out["ham_o"]


    def surface_body(r):
        for c in range(8):
            r.po[c, 16:32, :] = r.state[...].astype(BF16)
        r.wait("zr", "sym", "amp")
        surface_part(r, *first_received(r))
        for c in range(8):
            r.po[c, 0:16, :] = r.terms[c * 16 : (c + 1) * 16, :].astype(BF16)

    def outer_body(order):
        def body(r):
            r.points = float(all_points)
            r.all_points = all_points
            r.wait("pr", "sym")
            more = ghost_term(r, order)
            r.wait("ys", "field", "pot")
            dipole_image(r)
            term = outer_term(r, order)
            for comp in range(2):
                at = comp * 80
                head = term[comp][8:16, :] + more[comp]
                if order == 4:
                    r.wait("u0", "u1", "u2")
                    total = r.u[at + 8 : at + 72, :] + r.u0[at + 8 : at + 72, :] + r.u1[at + 8 : at + 72, :] + r.u2[at + 8 : at + 72, :]
                    r.psi_o[comp] = total + term[comp][8:72, :]
                    r.psi_o[comp, 0:8, :] = total[0:8, :] + head
                    r.mark_o[comp] = head[:, 0:128]
                else:
                    r.u_o[at : at + 80, :] = term[comp]
                    r.u_o[at + 8 : at + 16, :] = head
            if order < 4:
                r.low_o[...] = r.u_o[...].astype(BF16)

        return body

    def state_body(order):
        def body(r):
            r.wait("zr")
            ham = ham_full(r)
            r.wait("pr")
            state = next_state(r, ham, surface_of(r), order)
            if order == 4:
                r.wait("s0", "s1", "s2")
                r.full[...] = state + r.state[...] + r.s2[...] + r.s1[...] + r.s0[...]
                for x in range(4):
                    for comp in range(2):
                        for q in range(4):
                            at = comp * 8 + q * 2
                            r.sum_o[x, comp, :, q * 512 : (q + 1) * 512] = r.full[at : at + 2, :]
                return
            r.state_o[...] = state
            first_out(r, r.u[8:9, :], r.u[88:89, :])
            r.wait("ham")
            ham_rows(r, state)
            z_out(r)

        return body

    for order in range(1, 5):
        zr = over_z(out["zo"])
        ys = lax.all_gather(out["low_o"], "chan", axis=0)
        part = call(
            surface_body, {**common, "state": inner[-1], "zr": zr, "amp": amp}, {"po": ((8, 32, 512), BF16)},
            surface_scratch, 1_500_000_000
        )["po"]
        pr = lax.all_to_all(part, "chan", 0, 0)
        ins = {**common, "ys": ys, "dipole": dipole, "field": strength, "pot": pot, "pr": pr, "amp": amp, "u": outer[-1]}
        inner_ins = {"info": info, "zr": zr, "pr": pr, "state": inner[-1]}
        if order < 4:
            outs = {"u_o": outer_spec, "low_o": low_spec}
            out = call(outer_body(order), ins, outs, outer_scratch, 4_000_000_000)
            outer.append(out["u_o"])
            inner_ins.update(ham=hams, u=out["u_o"])
            outs = {"zo": z_spec, "state_o": inner_spec}
            out.update(call(state_body(order), inner_ins, outs, {**full_scratch, **z_scratch}, 1_000_000_000))
            inner.append(out["state_o"])
        else:
            for i in range(3):
                ins["u%d" % i] = outer[i]
                inner_ins["s%d" % i] = inner[i]
            total = call(
                state_body(order), inner_ins, {"sum_o": ((4, 2, 2, 2048), F32)}, full_scratch, 1_000_000_000
            )["sum_o"]
            outs = {"psi_o": ((2, 64, 512), F32), "mark_o": ((2, 8, 128), F32)}
            out = call(outer_body(order), ins, outs, outer_scratch, 4_000_000_000)


    def finish(r):
        r.wait("sums")
        r.state_o[...] = r.sums[0]

    state_next = call(
        finish, {"sums": over_x(total), "mark": out["mark_o"]}, {"state_o": ((2, 2, 2048), F32)}, {}, 1_000_000
    )["state_o"]
    return out["psi_o"].transpose(0, 2, 1), state_next


def solution(mesh):
    return jax.shard_map(
        shards,
        mesh=mesh,
        in_specs=(
            P(None, "chan", "sector"),
            P("chan", "sector"),
            P("chan", None, None, None),
            P("chan", None),
            P("chan", None),
            P("chan"),
            P("chan"),
            P("chan", "sector", None),
            P(None, "chan", None),
            P(),
        ),
        out_specs=(P(None, "chan", "sector"), P(None, "chan", None)),
        check_vma=False,
    )
```

time: 1030 us -> 217 us (0.21)
  blocking collectives: 777 us -> 88.8 us
  waiting for transfers between devices: 138 us -> 20 us
  Pallas kernels: 0 us -> 47.4 us
  local copies, waits for them, and re-layouts: 33.2 us -> 4.5 us
  matrix products: 23.3 us -> 0 us
  other arithmetic: 14.4 us -> 0.73 us
  starting transfers between devices: 27.3 us -> 39.6 us
    all_gather x8 -> x0, blocking collectives: 503 us -> none  [the longest x4 451 us: shards(): ham_rows = lax.all_gather(own_rows, 'sector', axis=2, tiled=True)]
    psum x2 -> x0, blocking collectives: 274 us -> none  [from_root(): return lax.psum(kept, axis)]
    unnamed x8 -> x4, waiting for transfers between devices: 138 us -> 0.07 us
    all_to_all x0 -> x6, blocking collectives: none -> 88.8 us  [the longest x3 58 us: over_z(): return lax.all_to_all(piece, 'sector', 0, 0, axis_index_groups=z_groups)]
    pallas_call x0 -> x16, Pallas kernels: none -> 47.4 us  [call(): pl.pallas_call(kernel, out_shape=[jax.ShapeDtypeStruct(shape, kind) for s...]
    all_to_all x0 -> x4, starting transfers between devices: none -> 33.6 us  [the longest x1 14.9 us: over_z(): return lax.all_to_all(piece, 'sector', 0, 0, axis_index_groups=z_groups)]
    dot_general x16 -> x0, matrix products: 23.3 us -> none  [the longest x4 11.1 us: shards(): jnp.einsum('bjci,zbjip->zbcp', dipole, picked, preferred_element_type=jnp...]
    ppermute x8 -> x2, starting transfers between devices: 27 us -> 5.83 us  [the longest x1 3.92 us: shards(): right = lax.ppermute(out['head'], 'sector', down)]
  transfers between devices with their start and end apart: 14 -> 10, of which waited for: 2 -> 4; matrix products, arithmetic and copies ran while one was open for 4% -> 0% of each run, Pallas kernels for 0% -> 12%
where the time goes in v2:
time: 217 us; the launch traced here: 216 us
  blocking collectives  88.8 us (41%)
  Pallas kernels  47.4 us (22%)
  starting transfers between devices  39.6 us (18%)
  waiting for transfers between devices  20 us (9%)
  between operations  14.6 us (7%)
  local copies, waits for them, and re-layouts  4.5 us (2%)
    all_to_all x3, blocking collectives, over_z(): return lax.all_to_all(piece, 'sector', 0, 0, axis_index_groups=z_groups)  58 us
    pallas_call x16, Pallas kernels, call(): pl.pallas_call(kernel, out_shape=[jax.ShapeDtypeStruct(shape, kind) for s...  47.4 us
    all_to_all x3, blocking collectives, shards(): pr = lax.all_to_all(part, 'chan', 0, 0)  30.7 us
    all_to_all x1, starting transfers between devices, over_z(): return lax.all_to_all(piece, 'sector', 0, 0, axis_index_groups=z_groups)  14.9 us
    all_to_all x2, starting transfers between devices, over_x(): return lax.all_to_all(piece, 'sector', 0, 0, axis_index_groups=x_groups)  14.3 us
    all_to_all x1, waiting for transfers between devices, over_z(): return lax.all_to_all(piece, 'sector', 0, 0, axis_index_groups=z_groups)  8.93 us
    all_to_all x1, waiting for transfers between devices, shards(): pr = lax.all_to_all(part, 'chan', 0, 0)  6.85 us
    all_to_all x1, starting transfers between devices, shards(): pr = lax.all_to_all(part, 'chan', 0, 0)  4.53 us
  transfers between devices with their start and end apart: 10, of which 4 were waited for; matrix products, arithmetic and copies ran while one was open for 0% of the time, Pallas kernels for 12%

profile of v2, /device:TPU:6, one launch (start us, length us, event | category | flops | bytes accessed | tf_op | source)
XLA Modules:
  0.0 215.7 jit_solution(3054853978388077296)
XLA Ops:
  7.2 0.8 reshape.10
  7.9 0.7 pad_add_fusion.refs_0_
  8.7 0.9 copy-done
  9.6 0.9 copy-done.1
  10.6 0.8 copy-done.3
  11.4 1.6 shard_map.113
  13.0 9.4 %all-to-all-start = ((bf16[4,2,32,2048]{3,2,1,0:T(8,128)(2,1)}), bf16[4,2,32,2048]{3,2,1,0:T(8,128)(2,1)S(1)}, u32[]{:S(2)}, u32[]{:S(2)}) async-start(bf16[4,2,32,2048]{3,2,1,0:T(8,128)(2,1)} %get-tuple-element.29), calls=%async_computation | async-start | bytes 2097152 | tf_op jit(solution)/shard_map/all_to_all | solution.py:251
  22.4 1.9 collective-permute-start
  24.3 3.9 %collective-permute-start.1 = (f32[24,512]{1,0:T(8,128)S(1)}, f32[24,512]{1,0:T(8,128)S(1)}, u32[]{:S(2)}, u32[]{:S(2)}) collective-permute-start(f32[24,512]{1,0:T(8,128)S(1)} %get-tuple-element.28), channel_id=1, source_target_pairs={{8,0},{16,8},{24,16},{32,24},{40,32},{48,40},{56,48},{64,56},{72,6... | collective-permute-start | bytes 147464 | tf_op jit(solution)/shard_map/ppermute | solution.py:288
  28.2 3.1 %collective-permute-done.refs_3_ = f32[24,512]{1,0:T(8,128)S(1)} collective-permute-done((f32[24,512]{1,0:T(8,128)S(1)}, f32[24,512]{1,0:T(8,128)S(1)}, u32[]{:S(2)}, u32[]{:S(2)}) %collective-permute-start) | collective-permute-done | bytes 49184 | tf_op jit(solution)/shard_map/ppermute | solution.py:287
  31.3 1.1 collective-permute-done.1.refs_4_
  32.4 0.0 all-to-all-done.refs_6_
  32.4 1.0 copy-done.8
  33.4 2.7 %shard_map.114 = (bf16[4,2,32,2048]{3,2,1,0:T(8,128)(2,1)}, f32[160,512]{1,0:T(8,128)S(1)}, f32[80,512]{1,0:T(8,128)S(1)}, f32[16,512]{1,0:T(8,128)S(1)}, bf16[1...) custom-call(s32[128]{0:T(128)S(1)} %pad_add_fusion.refs_0_, f32[2,64,512]{2,1,0:T(8,128)S(1)} %bitcast.12, ...), custom_call_target="tpu_custom_call" | custom-call | flops 1000000000 | bytes 1024 | tf_op jit(solution)/shard_map/pallas_call | solution.py:74
  36.0 0.0 all-gather.9.cloned.1.call-update
  36.1 14.9 %all-to-all-start.1 = ((f32[16,1,1536]{2,1,0:T(1,128)}), f32[16,1,1536]{2,1,0:T(1,128)S(1)}, u32[]{:S(2)}, u32[]{:S(2)}) async-start(f32[16,1,1536]{2,1,0:T(1,128)} %get-tuple-element.34), calls=%async_computation.1 | async-start | bytes 196608 | tf_op jit(solution)/shard_map/all_to_all | solution.py:248
  50.9 0.0 copy-start.6
  50.9 4.2 %shard_map.115 = (bf16[512,2048]{1,0:T(8,128)(2,1)}, bf16[2,8,256,256]{3,2,1,0:T(8,128)(2,1)}) custom-call(bf16[512,2048]{1,0:T(8,128)(2,1)} %refs_0_.1, bf16[2,8,256,256]{3,2,1,0:T(8,128)(2,1)} %refs_1_.3), custom_call_target="tpu_custom_call" | custom-call | flops 1000000 | bytes 1024 | tf_op jit(solution)/shard_map/pallas_call | solution.py:74
  55.1 8.9 %all-to-all-done.1.refs_3_.refs_1_ = f32[16,1,1536]{2,1,0:T(1,128)S(1)} async-done(((f32[16,1,1536]{2,1,0:T(1,128)}), f32[16,1,1536]{2,1,0:T(1,128)S(1)}, u32[]{:S(2)}, u32[]{:S(2)}) %all-to-all-start.1) | async-done | bytes 98336 | tf_op jit(solution)/shard_map/all_to_all | solution.py:248
  64.1 3.4 %shard_map.116 = bf16[8,32,512]{2,1,0:T(8,128)(2,1)} custom-call(s32[128]{0:T(128)S(1)} %pad_add_fusion.refs_0_, s32[1,512]{1,0:T(1,128)S(1)} %bitcast.15, f32[16,512]{1,0:T(8,128)S(1)} %get-tuple-element.33.refs_2_.refs_3_.refs_4_, f32[16,1,1536]{2,1,0:T(1,128)S(1)} %all-to-all-done.1.refs_3_.refs_1_, bf16[512,2048]{1,0:T(8,128)(2,1)} %get-tuple-element.35.refs_4_.refs_7_), custom_call_target="tpu_custom_call" | custom-call | flops 1500000000 | bytes 1024 | tf_op jit(solution)/shard_map/pallas_call | solution.py:74
  67.5 4.5 %all-to-all-start.2 = ((bf16[8,32,512]{2,1,0:T(8,128)(2,1)}), bf16[8,32,512]{2,1,0:T(8,128)(2,1)S(1)}, u32[]{:S(2)}, u32[]{:S(2)}) async-start(bf16[8,32,512]{2,1,0:T(8,128)(2,1)} %shard_map.116), calls=%async_computation.2 | async-start | bytes 524288 | tf_op jit(solution)/shard_map/all_to_all | solution.py:388
  72.0 0.0 all-gather.11.cloned.1.call-start
  72.7 6.8 %all-to-all-done.2.refs_6_.refs_2_ = bf16[8,32,512]{2,1,0:T(8,128)(2,1)S(1)} async-done(((bf16[8,32,512]{2,1,0:T(8,128)(2,1)}), bf16[8,32,512]{2,1,0:T(8,128)(2,1)S(1)}, u32[]{:S(2)}, u32[]{:S(2)}) %all-to-all-start.2) | async-done | bytes 262176 | tf_op jit(solution)/shard_map/all_to_all | solution.py:388
  79.6 5.6 %shard_map.117 = (f32[160,512]{1,0:T(8,128)S(1)}, bf16[160,512]{1,0:T(8,128)(2,1)}) custom-call(s32[128]{0:T(128)S(1)} %pad_add_fusion.refs_0_, s32[1,512]{1,0:T(1,128)S(1)} %bitcast.16, bf16[8,160,512]{2,1,0:T(8,128)(2,1)} %bitcast.24, bf16[2,8,256,256]{3,2,1,0:T(8,128)(2,1)} %get-tuple-element.31.refs_3_, f32[128]{0:T(128)S(1)} %broadcast_in_dim.16.refs_4_, ...), custom_call_target="tpu_custom_call" | custom-call | flops 4000000000 | bytes 1024 | tf_op jit(solution)/shard_map/pallas_call | solution.py:74
  85.1 0.0 all-gather.11.cloned.1.call-update
  85.2 0.0 all-gather.13.cloned.1.call-start
  85.2 1.1 shard_map.118
  86.3 19.4 %all_to_all.50.refs_3_.refs_1_ = f32[16,1,1536]{2,1,0:T(1,128)S(1)} all-to-all(f32[16,1,1536]{2,1,0:T(1,128)S(1)} %get-tuple-element.41), channel_id=1, replica_groups={{0,32,64,96,128,160,192,224,256,288,320,352,384,416,448,480},{8,40,72,1..., dimensions={0} | all-to-all | bytes 196608 | tf_op jit(solution)/shard_map/all_to_all | solution.py:248
  105.7 2.7 %shard_map.119 = bf16[8,32,512]{2,1,0:T(8,128)(2,1)S(1)} custom-call(s32[128]{0:T(128)S(1)} %pad_add_fusion.refs_0_, s32[1,512]{1,0:T(1,128)S(1)} %bitcast.17, f32[16,512]{1,0:T(8,128)S(1)} %get-tuple-element.40.refs_2_.refs_3_.refs_5_, f32[16,1,1536]{2,1,0:T(1,128)S(1)} %all_to_all.50.refs_3_.refs_1_, bf16[512,2048]{1,0:T(8,128)(2,1)} %get-tuple-element.35.refs_4_.refs_7_), custom_call_target="tpu_custom_call" | custom-call | flops 1500000000 | bytes 1024 | tf_op jit(solution)/shard_map/pallas_call | solution.py:74
  108.5 10.4 %all_to_all.51.refs_6_.refs_2_ = bf16[8,32,512]{2,1,0:T(8,128)(2,1)S(1)} all-to-all(bf16[8,32,512]{2,1,0:T(8,128)(2,1)S(1)} %shard_map.119), channel_id=1, replica_groups=mesh['sector'=64,'chan'=8] {'chan'}, dimensions={0} | all-to-all | bytes 524288 | tf_op jit(solution)/shard_map/all_to_all | solution.py:388
  118.9 5.5 %shard_map.120 = (f32[160,512]{1,0:T(8,128)S(1)}, bf16[160,512]{1,0:T(8,128)(2,1)}) custom-call(s32[128]{0:T(128)S(1)} %pad_add_fusion.refs_0_, s32[1,512]{1,0:T(1,128)S(1)} %bitcast.18, bf16[8,160,512]{2,1,0:T(8,128)(2,1)} %bitcast.25, bf16[2,8,256,256]{3,2,1,0:T(8,128)(2,1)} %get-tuple-element.31.refs_3_, f32[128]{0:T(128)S(1)} %broadcast_in_dim.16.refs_4_, ...), custom_call_target="tpu_custom_call" | custom-call | flops 4000000000 | bytes 1024 | tf_op jit(solution)/shard_map/pallas_call | solution.py:74
  124.4 0.0 all-gather.13.cloned.1.call-update
  124.4 0.0 all-gather.15.cloned.1.call-start
  124.5 1.1 shard_map.121
  125.5 19.1 %all_to_all.52.refs_3_.refs_1_ = f32[16,1,1536]{2,1,0:T(1,128)S(1)} all-to-all(f32[16,1,1536]{2,1,0:T(1,128)S(1)} %get-tuple-element.45), channel_id=1, replica_groups={{0,32,64,96,128,160,192,224,256,288,320,352,384,416,448,480},{8,40,72,1..., dimensions={0} | all-to-all | bytes 196608 | tf_op jit(solution)/shard_map/all_to_all | solution.py:248
  144.7 2.7 %shard_map.122 = bf16[8,32,512]{2,1,0:T(8,128)(2,1)S(1)} custom-call(s32[128]{0:T(128)S(1)} %pad_add_fusion.refs_0_, s32[1,512]{1,0:T(1,128)S(1)} %bitcast.19, f32[16,512]{1,0:T(8,128)S(1)} %get-tuple-element.44.refs_2_.refs_3_.refs_6_, f32[16,1,1536]{2,1,0:T(1,128)S(1)} %all_to_all.52.refs_3_.refs_1_, bf16[512,2048]{1,0:T(8,128)(2,1)} %get-tuple-element.35.refs_4_.refs_7_), custom_call_target="tpu_custom_call" | custom-call | flops 1500000000 | bytes 1024 | tf_op jit(solution)/shard_map/pallas_call | solution.py:74
  147.4 10.4 %all_to_all.53.refs_6_.refs_2_ = bf16[8,32,512]{2,1,0:T(8,128)(2,1)S(1)} all-to-all(bf16[8,32,512]{2,1,0:T(8,128)(2,1)S(1)} %shard_map.122), channel_id=1, replica_groups=mesh['sector'=64,'chan'=8] {'chan'}, dimensions={0} | all-to-all | bytes 524288 | tf_op jit(solution)/shard_map/all_to_all | solution.py:388
  157.8 5.5 %shard_map.123 = (f32[160,512]{1,0:T(8,128)S(1)}, bf16[160,512]{1,0:T(8,128)(2,1)}) custom-call(s32[128]{0:T(128)S(1)} %pad_add_fusion.refs_0_, s32[1,512]{1,0:T(1,128)S(1)} %bitcast.20, bf16[8,160,512]{2,1,0:T(8,128)(2,1)} %bitcast.26, bf16[2,8,256,256]{3,2,1,0:T(8,128)(2,1)} %get-tuple-element.31.refs_3_, f32[128]{0:T(128)S(1)} %broadcast_in_dim.16.refs_4_, ...), custom_call_target="tpu_custom_call" | custom-call | flops 4000000000 | bytes 1024 | tf_op jit(solution)/shard_map/pallas_call | solution.py:74
  163.3 0.0 all-gather.15.cloned.1.call-update
  163.3 1.1 shard_map.124
  164.4 19.4 %all_to_all.54.refs_3_.refs_1_ = f32[16,1,1536]{2,1,0:T(1,128)S(1)} all-to-all(f32[16,1,1536]{2,1,0:T(1,128)S(1)} %get-tuple-element.49), channel_id=1, replica_groups={{0,32,64,96,128,160,192,224,256,288,320,352,384,416,448,480},{8,40,72,1..., dimensions={0} | all-to-all | bytes 196608 | tf_op jit(solution)/shard_map/all_to_all | solution.py:248
  183.8 2.7 %shard_map.125 = bf16[8,32,512]{2,1,0:T(8,128)(2,1)S(1)} custom-call(s32[128]{0:T(128)S(1)} %pad_add_fusion.refs_0_, s32[1,512]{1,0:T(1,128)S(1)} %bitcast.21, f32[16,512]{1,0:T(8,128)S(1)} %get-tuple-element.48.refs_2_.refs_3_, f32[16,1,1536]{2,1,0:T(1,128)S(1)} %all_to_all.54.refs_3_.refs_1_, bf16[512,2048]{1,0:T(8,128)(2,1)} %get-tuple-element.35.refs_4_.refs_7_), custom_call_target="tpu_custom_call" | custom-call | flops 1500000000 | bytes 1024 | tf_op jit(solution)/shard_map/pallas_call | solution.py:74
  186.5 9.9 %all_to_all.55.refs_6_.refs_2_ = bf16[8,32,512]{2,1,0:T(8,128)(2,1)S(1)} all-to-all(bf16[8,32,512]{2,1,0:T(8,128)(2,1)S(1)} %shard_map.125), channel_id=1, replica_groups=mesh['sector'=64,'chan'=8] {'chan'}, dimensions={0} | all-to-all | bytes 524288 | tf_op jit(solution)/shard_map/all_to_all | solution.py:388
  196.5 1.3 shard_map.127
  197.8 4.9 %all-to-all-start.9 = ((f32[4,2,2,2048]{3,2,1,0:T(2,128)}), f32[4,2,2,2048]{3,2,1,0:T(2,128)S(1)}, u32[]{:S(2)}, u32[]{:S(2)}) async-start(f32[4,2,2,2048]{3,2,1,0:T(2,128)} %shard_map.127), calls=%async_computation.9 | async-start | bytes 262144 | tf_op jit(solution)/shard_map/all_to_all | solution.py:251
  202.7 5.6 %shard_map.126 = (f32[2,64,512]{2,1,0:T(8,128)}, f32[2,8,128]{2,1,0:T(8,128)S(1)}) custom-call(s32[128]{0:T(128)S(1)} %pad_add_fusion.refs_0_, s32[1,512]{1,0:T(1,128)S(1)} %bitcast.22, bf16[8,160,512]{2,1,0:T(8,128)(2,1)} %bitcast.23, bf16[2,8,256,256]{3,2,1,0:T(8,128)(2,1)} %get-tuple-element.31.refs_3_, f32[128]{0:T(128)S(1)} %broadcast_in_dim.16.refs_4_, ...), custom_call_target="tpu_custom_call" | custom-call | flops 4000000000 | bytes 1024 | tf_op jit(solution)/shard_map/pallas_call | solution.py:74
  208.3 0.0 all-to-all-done.9.refs_0_
  208.3 0.8 shard_map.128
  (20 shorter events, 0.0 us)
Async XLA Ops:
  8.7 1.0 copy-start
  9.6 0.9 copy-start.1
  10.6 0.8 copy-start.3
  11.4 22.0 %copy-start.2 = (f32[2,512,64]{1,2,0:T(8,128)S(1)}, f32[2,512,64]{1,2,0:T(8,128)}, u32[]{:S(2)}) copy-start(f32[2,512,64]{1,2,0:T(8,128)} %param.10) | copy-start | bytes 786436
  11.4 22.0 %copy-start.4 = (bf16[512,64]{0,1:T(8,128)(2,1)S(1)}, bf16[512,64]{0,1:T(8,128)(2,1)}, u32[]{:S(2)}) copy-start(bf16[512,64]{0,1:T(8,128)(2,1)} %param.11) | copy-start | bytes 196612
  11.4 22.0 %copy-start.5 = (f32[2,2,2048]{2,1,0:T(2,128)S(1)}, f32[2,2,2048]{2,1,0:T(2,128)}, u32[]{:S(2)}) copy-start(f32[2,2,2048]{2,1,0:T(2,128)} %refs_5_.1) | copy-start | bytes 98308
  13.0 19.4 %all-to-all-start = ((bf16[4,2,32,2048]{3,2,1,0:T(8,128)(2,1)}), bf16[4,2,32,2048]{3,2,1,0:T(8,128)(2,1)S(1)}, u32[]{:S(2)}, u32[]{:S(2)}) async-start(bf16[4,2,32,2048]{3,2,1,0:T(8,128)(2,1)} %get-tuple-element.29), calls=%async_computation | async-start | bytes 2097152 | tf_op jit(solution)/shard_map/all_to_all | solution.py:251
  22.4 57.2 %all-gather.9.cloned.1.call-start = ((), (), s32[]{:S(2)}) async-start(), calls=%async_computation.10 | async-start | bytes 1474560 | tf_op jit(solution)/shard_map/all_gather | solution.py:383
  22.4 8.9 %collective-permute-start = (f32[24,512]{1,0:T(8,128)S(1)}, f32[24,512]{1,0:T(8,128)S(1)}, u32[]{:S(2)}, u32[]{:S(2)}) collective-permute-start(f32[24,512]{1,0:T(8,128)S(1)} %get-tuple-element.27), channel_id=1, source_target_pairs={{0,8},{8,16},{16,24},{24,32},{32,40},{40,48},{48,56},{56,64},{64,7... | collective-permute-start | bytes 147464 | tf_op jit(solution)/shard_map/ppermute | solution.py:287
  24.3 8.1 %collective-permute-start.1 = (f32[24,512]{1,0:T(8,128)S(1)}, f32[24,512]{1,0:T(8,128)S(1)}, u32[]{:S(2)}, u32[]{:S(2)}) collective-permute-start(f32[24,512]{1,0:T(8,128)S(1)} %get-tuple-element.28), channel_id=1, source_target_pairs={{8,0},{16,8},{24,16},{32,24},{40,32},{48,40},{56,48},{64,56},{72,6... | collective-permute-start | bytes 147464 | tf_op jit(solution)/shard_map/ppermute | solution.py:288
  32.4 1.0 copy-start.8
  36.1 28.0 %all-to-all-start.1 = ((f32[16,1,1536]{2,1,0:T(1,128)}), f32[16,1,1536]{2,1,0:T(1,128)S(1)}, u32[]{:S(2)}, u32[]{:S(2)}) async-start(f32[16,1,1536]{2,1,0:T(1,128)} %get-tuple-element.34), calls=%async_computation.1 | async-start | bytes 196608 | tf_op jit(solution)/shard_map/all_to_all | solution.py:248
  50.9 13.1 %copy-start.6 = (s32[512]{0:T(512)S(1)}, s32[512]{0:T(512)}, u32[]{:S(2)}) copy-start(s32[512]{0:T(512)} %param.15) | copy-start | bytes 6148
  67.5 12.1 %all-to-all-start.2 = ((bf16[8,32,512]{2,1,0:T(8,128)(2,1)}), bf16[8,32,512]{2,1,0:T(8,128)(2,1)S(1)}, u32[]{:S(2)}, u32[]{:S(2)}) async-start(bf16[8,32,512]{2,1,0:T(8,128)(2,1)} %shard_map.116), calls=%async_computation.2 | async-start | bytes 524288 | tf_op jit(solution)/shard_map/all_to_all | solution.py:388
  72.0 46.9 %all-gather.11.cloned.1.call-start = ((), (), s32[]{:S(2)}) async-start(), calls=%async_computation.11 | async-start | bytes 1474560 | tf_op jit(solution)/shard_map/all_gather | solution.py:383
  79.6 5.7 %copy-start.7 = (bf16[4,2,32,2048]{3,2,1,0:T(8,128)(2,1)S(1)}, bf16[4,2,32,2048]{3,2,1,0:T(8,128)(2,1)}, u32[]{:S(2)}) copy-start(bf16[4,2,32,2048]{3,2,1,0:T(8,128)(2,1)} %get-tuple-element.38.refs_4_) | copy-start | bytes 3145732
  85.2 72.6 %all-gather.13.cloned.1.call-start = ((), (), s32[]{:S(2)}) async-start(), calls=%async_computation.12 | async-start | bytes 1474560 | tf_op jit(solution)/shard_map/all_gather | solution.py:383
  124.4 78.3 %all-gather.15.cloned.1.call-start = ((), (), s32[]{:S(2)}) async-start(), calls=%async_computation.13 | async-start | bytes 1474560 | tf_op jit(solution)/shard_map/all_gather | solution.py:383
  197.8 10.5 %all-to-all-start.9 = ((f32[4,2,2,2048]{3,2,1,0:T(2,128)}), f32[4,2,2,2048]{3,2,1,0:T(2,128)S(1)}, u32[]{:S(2)}, u32[]{:S(2)}) async-start(f32[4,2,2,2048]{3,2,1,0:T(2,128)} %shard_map.127), calls=%async_computation.9 | async-start | bytes 262144 | tf_op jit(solution)/shard_map/all_to_all | solution.py:251
Sparse Core Ops, SparseCore 0:
  36.2 35.3 all-gather.8
  85.3 25.4 all-gather.10
  124.5 24.5 all-gather.12
  163.4 24.4 all-gather.14

commit v3 on v2

--- a/solution.py
+++ b/solution.py
@@ -16,15 +16,15 @@
 KINETIC = 1.0 / 48.0
 
 
-KEPT = ("u", "state", "amp", "dipole", "ham", "mark")
-BIG = ("keep_amp", "keep_dipole", "keep_ham", "ys")
+KEPT = ("after", "u", "local", "rows", "more", "state", "ham", "mark")
+BIG = ("amp", "dipole", "keep_ham", "ys", "spread_ham")
 
 
 def call(body, ins, outs, scratch, flops):
     arrays = dict(ins)
     scratch = dict(scratch)
     for name, value in arrays.items():
-        if name not in ("info", "field") + KEPT and not name.startswith("keep_"):
+        if name not in ("info", "field") + KEPT and not name.startswith(("keep_", "spread_")):
             scratch[name + "_v"] = VMEM(value.shape, value.dtype)
     scratch["info_s"] = SMEM((128,), jnp.int32)
     scratch["field_s"] = SMEM((128,), F32)
@@ -38,15 +38,19 @@
         copies = {}
 
         def target(name):
-            if name.startswith("keep_"):
-                return getattr(r, name[5:] + "_o")
+            if name.startswith(("keep_", "spread_")):
+                return getattr(r, name.split("_")[1] + "_o")
             return getattr(r, name + ("_s" if name in ("info", "field") else "_v"))
 
         def start(name):
             source, dest = getattr(r, "hbm_" + name), target(name)
             views = [(source, dest)]
-            if name == "keep_dipole":
+            if name == "dipole":
                 views = [(source.at[b, pl.ds(j, 4)], dest.at[b, pl.ds(j, 4)]) for b in range(2) for j in (0, 4)]
+            elif name == "amp":
+                views = [(source.at[:, pl.ds(q * 512, 512)], dest.at[:, pl.ds(q * 512, 512)]) for q in range(4)]
+            elif name == "spread_ham":
+                views = [(source, dest.at[x]) for x in range(4)]
             elif name in BIG:
                 size = source.shape[0] // 4
                 views = [(source.at[pl.ds(i * size, size)], dest.at[pl.ds(i * size, size)]) for i in range(4)]
@@ -60,14 +64,19 @@
             for name in wanted:
                 if name in copies:
                     for copy in copies.pop(name):
-                        copy.wait()
+                        if copy is not None:
+                            copy.wait()
                     setattr(r, name, target(name))
 
+        def part(name, i):
+            copies[name][i].wait()
+            copies[name][i] = None
+
         r.wait = wait
+        r.part = part
         for name in arrays:
             if name not in KEPT:
                 start(name)
-        wait("info")
         body(r)
         wait(*list(copies))
 
@@ -106,7 +115,8 @@
     quarter = (row >> 1) & 3
     total = jnp.zeros((128, 512), F32)
     for q in range(4):
-        part = dot_t(states, r.amp[:, q * 512 : (q + 1) * 512])
+        r.part("amp", q)
+        part = dot_t(states, r.amp_v[:, q * 512 : (q + 1) * 512])
         total = total + jnp.where(quarter == q, part, 0.0)
     block = (row >> 4) * 2 + (row & 1)
     total = jnp.where(block == r.sym[...], total, 0.0)
@@ -122,7 +132,8 @@
     chosen = jnp.where(block == r.sym[...], jnp.where(((row >> 1) & 1) == 0, first0, first1), 0.0)
     both = jnp.concatenate(split(chosen), axis=0)
     for q in range(4):
-        part = dot(both, r.amp[:, q * 512 : (q + 1) * 512])
+        r.part("amp", q)
+        part = dot(both, r.amp_v[:, q * 512 : (q + 1) * 512])
         r.sum[...] = part[:32] + part[32:]
         for c in range(8):
             for comp in range(2):
@@ -138,6 +149,7 @@
 
 
 def mask_of(r):
+    r.wait("info")
     row = rows_of((16, 512))
     lane = lax.broadcasted_iota(jnp.int32, (16, 512), 1)
     size = jnp.where((row & 1) == 0, r.info[16], r.info[17])
@@ -163,7 +175,7 @@
     return r.zr[0, :, 512:1024], r.zr[0, :, 1024:1536]
 
 
-def ham_rows(r, state):
+def ham_rows(r, state, out):
     both = jnp.concatenate(split(state), axis=0)
     row = rows_of((16, 128))
     total = jnp.zeros((16, 128), F32)
@@ -179,7 +191,7 @@
             at = comp * 8 + block
             rows = [r.sums[at + 2 * q : at + 2 * q + 1, :] for q in range(4)]
             lanes = (comp * 2 + block) * 128
-            r.piece[:, lanes : lanes + 128] = (rows[0] + rows[1]) + (rows[2] + rows[3])
+            out[:, lanes : lanes + 128] = (rows[0] + rows[1]) + (rows[2] + rows[3])
 
 
 def first_out(r, first0, first1):
@@ -194,21 +206,23 @@
 
 
 def dipole_image(r):
+    r.wait("info")
     for b in range(2):
         total = None
         for j in range(8):
+            if j % 4 == 0:
+                r.part("dipole", b * 2 + j // 4)
             n = r.info[b * 8 + j]
             lanes = pl.ds(pl.multiple_of((n & 1) * 256, 256), 256)
-            part = dot_t(r.ys[n >> 1, 0:160, lanes], r.dipole[b, j])
+            part = dot_t(r.ys[n >> 1, 0:160, lanes], r.dipole_v[b, j])
             total = part if total is None else total + part
         r.dip[:, b * 256 : (b + 1) * 256] = total
 
 
-def outer_term(r, order):
+def local_term(r, order):
+    r.wait("info")
     images = []
-    row = rows_of((80, 512))
-    point = r.info[18] * 64 + row - 8
-    radius = (point + 1).astype(F32) * (1.0 / r.points)
+    point = r.info[18] * 64 + rows_of((80, 512)) - 8
     for comp in range(2):
         u = r.u[comp * 80 : (comp + 1) * 80, :]
         r.pad[comp, 0:8, :] = jnp.zeros((8, 512), F32)
@@ -216,12 +230,20 @@
         r.pad[comp, 88:96, :] = jnp.zeros((8, 512), F32)
         stencil = 16.0 * (r.pad[comp, 7:87, :] + r.pad[comp, 9:89, :]) - 30.0 * u
         stencil = stencil - (r.pad[comp, 6:86, :] + r.pad[comp, 10:90, :])
-        image = -KINETIC * stencil + r.pot[...] * u + r.field[0] * radius * r.dip[comp * 80 : (comp + 1) * 80, :]
+        image = -KINETIC * stencil + r.pot[...] * u
         images.append(jnp.where((point >= 0) & (point < r.all_points), image, 0.0))
     return images[1] * (1.0 / order), images[0] * (-1.0 / order)
 
 
+def dipole_term(r, order):
+    r.wait("info")
+    point = r.info[18] * 64 + rows_of((80, 512)) - 8
+    factor = r.field[0] * (1.0 / order) * ((point + 1).astype(F32) * (1.0 / r.all_points))
+    return factor * r.dip[80:160, :], -factor * r.dip[0:80, :]
+
+
 def ghost_term(r, order):
+    r.wait("info")
     row = rows_of((8, 512))
     hub = jnp.where(r.info[18] == 0, 1.0 / order, 0.0).astype(F32)
     images = []
@@ -258,13 +280,12 @@
     z_scratch = {"sums": VMEM((16, 128), F32), "piece": VMEM((1, 1536), F32)}
     surface_scratch = {"sum": VMEM((32, 512), F32), "terms": VMEM((128, 512), F32)}
     full_scratch = {"full": VMEM((16, 512), F32)}
-    outer_scratch = {"dip": VMEM((160, 512), F32), "pad": VMEM((2, 96, 512), F32)}
-
-
-    def prepare(r):
-        r.wait("ham", "psi", "pot")
-        for x in range(4):
-            r.copies[x] = r.ham[...]
+    dipole_scratch = {"dip": VMEM((160, 512), F32)}
+    local_scratch = {"pad": VMEM((2, 96, 512), F32)}
+
+
+    def ends(r):
+        r.wait("psi", "pot")
         for comp in range(2):
             r.head[comp * 8 : (comp + 1) * 8, :] = r.psi[comp, 0:8, :]
             r.tail[comp * 8 : (comp + 1) * 8, :] = r.psi[comp, 56:64, :]
@@ -272,18 +293,9 @@
         r.tail[16:24, :] = r.pot[56:64, :].astype(F32)
 
     own = {"psi": psi.transpose(0, 2, 1), "pot": potential.T}
-    out = call(
-        prepare,
-        {"info": info, "ham": inner_ham, **own},
-        {"copies": ((4,) + inner_ham.shape, BF16), "head": end_spec, "tail": end_spec},
-        {}, 1_000_000,
-    )
-    hams = over_x(out["copies"])
-    out_kept = call(
-        lambda r: None, {"keep_amp": amp, "keep_dipole": dipole},
-        {"amp_o": (amp.shape, BF16), "dipole_o": (dipole.shape, BF16)}, {}, 1_000_000,
-    )
-    amp, dipole = out_kept["amp_o"], out_kept["dipole_o"]
+    spread = call(lambda r: None, {"spread_ham": inner_ham}, {"ham_o": ((4,) + inner_ham.shape, BF16)}, {}, 1_000_000)
+    out = call(ends, own, {"head": end_spec, "tail": end_spec}, {}, 1_000_000)
+    hams = over_x(spread["ham_o"])
     left = lax.ppermute(out["tail"], "sector", up)
     right = lax.ppermute(out["head"], "sector", down)
 
@@ -306,7 +318,7 @@
         first_out(r, r.u_o[8:9, :], r.u_o[88:89, :])
         r.wait("keep_ham")
         r.ham = r.ham_o
-        ham_rows(r, state)
+        ham_rows(r, state, r.piece)
         z_out(r)
 
     out = call(
@@ -324,43 +336,22 @@
     def surface_body(r):
         for c in range(8):
             r.po[c, 16:32, :] = r.state[...].astype(BF16)
-        r.wait("zr", "sym", "amp")
+        r.wait("zr", "sym")
         surface_part(r, *first_received(r))
         for c in range(8):
             r.po[c, 0:16, :] = r.terms[c * 16 : (c + 1) * 16, :].astype(BF16)
 
-    def outer_body(order):
+    def ghost_out(r, order):
+        r.wait("pr", "sym")
+        more = ghost_term(r, order)
+        for comp in range(2):
+            r.more_o[comp] = more[comp]
+
+    def middle_body(order):
         def body(r):
-            r.points = float(all_points)
             r.all_points = all_points
-            r.wait("pr", "sym")
-            more = ghost_term(r, order)
-            r.wait("ys", "field", "pot")
-            dipole_image(r)
-            term = outer_term(r, order)
-            for comp in range(2):
-                at = comp * 80
-                head = term[comp][8:16, :] + more[comp]
-                if order == 4:
-                    r.wait("u0", "u1", "u2")
-                    total = r.u[at + 8 : at + 72, :] + r.u0[at + 8 : at + 72, :] + r.u1[at + 8 : at + 72, :] + r.u2[at + 8 : at + 72, :]
-                    r.psi_o[comp] = total + term[comp][8:72, :]
-                    r.psi_o[comp, 0:8, :] = total[0:8, :] + head
-                    r.mark_o[comp] = head[:, 0:128]
-                else:
-                    r.u_o[at : at + 80, :] = term[comp]
-                    r.u_o[at + 8 : at + 16, :] = head
-            if order < 4:
-                r.low_o[...] = r.u_o[...].astype(BF16)
-
-        return body
-
-    def state_body(order):
-        def body(r):
-            r.wait("zr")
-            ham = ham_full(r)
-            r.wait("pr")
-            state = next_state(r, ham, surface_of(r), order)
+            r.wait("zr", "pr")
+            state = next_state(r, ham_full(r), surface_of(r), order)
             if order == 4:
                 r.wait("s0", "s1", "s2")
                 r.full[...] = state + r.state[...] + r.s2[...] + r.s1[...] + r.s0[...]
@@ -369,42 +360,90 @@
                         for q in range(4):
                             at = comp * 8 + q * 2
                             r.sum_o[x, comp, :, q * 512 : (q + 1) * 512] = r.full[at : at + 2, :]
+                ghost_out(r, order)
                 return
             r.state_o[...] = state
-            first_out(r, r.u[8:9, :], r.u[88:89, :])
-            r.wait("ham")
-            ham_rows(r, state)
-            z_out(r)
+            ham_rows(r, state, r.rows_o)
+            ghost_out(r, order)
+
+        return body
+
+    def local_body(order):
+        def body(r):
+            r.all_points = all_points
+            r.wait("pot")
+            term = local_term(r, order)
+            for comp in range(2):
+                r.local_o[comp * 80 : (comp + 1) * 80, :] = term[comp]
+            if order == 4:
+                r.wait("u0", "u1", "u2")
+                r.local_o[...] = r.local_o[...] + r.u0[...] + r.u1[...] + r.u2[...] + r.u[...]
+
+        return body
+
+    def dipole_body(order):
+        def body(r):
+            r.all_points = all_points
+            r.wait("ys", "field")
+            dipole_image(r)
+            term = dipole_term(r, order)
+            for comp in range(2):
+                at = slice(comp * 80 + 8, comp * 80 + 16)
+                r.dip[at, :] = term[comp][8:16, :] + r.more[comp]
+            for comp in range(2):
+                at = comp * 80
+                if order == 4:
+                    r.psi_o[comp, 0:8, :] = r.local[at + 8 : at + 16, :] + r.dip[at + 8 : at + 16, :]
+                    r.psi_o[comp, 8:64, :] = r.local[at + 16 : at + 72, :] + term[comp][16:72, :]
+                    r.mark_o[comp] = term[comp][0:8, 0:128]
+                else:
+                    total = r.local[at : at + 80, :] + term[comp]
+                    r.u_o[at : at + 80, :] = total
+                    r.u_o[at + 8 : at + 16, :] = r.local[at + 8 : at + 16, :] + r.dip[at + 8 : at + 16, :]
+                    r.low_o[at : at + 80, :] = r.u_o[at : at + 80, :].astype(BF16)
+            if order < 4:
+                first_out(r, r.u_o[8:9, :], r.u_o[88:89, :])
+                r.piece[:, 0:512] = r.rows[...]
+                z_out(r)
 
         return body
 
     for order in range(1, 5):
         zr = over_z(out["zo"])
         ys = lax.all_gather(out["low_o"], "chan", axis=0)
+        local_ins = {"info": info, "pot": pot, "u": outer[-1]}
+        if order == 4:
+            local_ins.update(u0=outer[0], u1=outer[1], u2=outer[2])
+        local = call(local_body(order), local_ins, {"local_o": outer_spec}, local_scratch, 1_000_000_000)["local_o"]
         part = call(
-            surface_body, {**common, "state": inner[-1], "zr": zr, "amp": amp}, {"po": ((8, 32, 512), BF16)},
+            surface_body, {"sym": common["sym"], "after": local, "state": inner[-1], "zr": zr, "amp": amp}, {"po": ((8, 32, 512), BF16)},
             surface_scratch, 1_500_000_000
         )["po"]
         pr = lax.all_to_all(part, "chan", 0, 0)
-        ins = {**common, "ys": ys, "dipole": dipole, "field": strength, "pot": pot, "pr": pr, "amp": amp, "u": outer[-1]}
         inner_ins = {"info": info, "zr": zr, "pr": pr, "state": inner[-1]}
+        ghost_ins = {**common, "pr": pr, "amp": amp}
+        if order == 4:
+            for i in range(3):
+                inner_ins["s%d" % i] = inner[i]
+        ins = {"info": info, "ys": ys, "dipole": dipole, "field": strength, "local": local}
+        more_spec = ((2, 8, 512), F32)
         if order < 4:
-            outs = {"u_o": outer_spec, "low_o": low_spec}
-            out = call(outer_body(order), ins, outs, outer_scratch, 4_000_000_000)
+            outs = {"state_o": inner_spec, "rows_o": ((1, 512), F32), "more_o": more_spec}
+            part = call(
+                middle_body(order), {**inner_ins, **ghost_ins, "ham": hams}, outs, {**full_scratch, **z_scratch}, 2_000_000_000
+            )
+            inner.append(part["state_o"])
+            ins.update(more=part["more_o"], rows=part["rows_o"])
+            outs = {"zo": z_spec, "u_o": outer_spec, "low_o": low_spec}
+            out = call(dipole_body(order), ins, outs, {**dipole_scratch, **z_scratch}, 4_000_000_000)
             outer.append(out["u_o"])
-            inner_ins.update(ham=hams, u=out["u_o"])
-            outs = {"zo": z_spec, "state_o": inner_spec}
-            out.update(call(state_body(order), inner_ins, outs, {**full_scratch, **z_scratch}, 1_000_000_000))
-            inner.append(out["state_o"])
         else:
-            for i in range(3):
-                ins["u%d" % i] = outer[i]
-                inner_ins["s%d" % i] = inner[i]
-            total = call(
-                state_body(order), inner_ins, {"sum_o": ((4, 2, 2, 2048), F32)}, full_scratch, 1_000_000_000
-            )["sum_o"]
+            outs = {"sum_o": ((4, 2, 2, 2048), F32), "more_o": more_spec}
+            part = call(middle_body(4), {**inner_ins, **ghost_ins}, outs, full_scratch, 2_000_000_000)
+            total = part["sum_o"]
+            ins["more"] = part["more_o"]
             outs = {"psi_o": ((2, 64, 512), F32), "mark_o": ((2, 8, 128), F32)}
-            out = call(outer_body(order), ins, outs, outer_scratch, 4_000_000_000)
+            out = call(dipole_body(4), ins, outs, dipole_scratch, 4_000_000_000)
 
 
     def finish(r):

time: 217 us -> 209 us (0.963)
  blocking collectives: 88.8 us -> 31.7 us
  waiting for transfers between devices: 20 us -> 61.4 us
  starting transfers between devices: 39.6 us -> 53.7 us
  Pallas kernels: 47.4 us -> 43.6 us
    all_to_all x3 -> x0, blocking collectives: 58 us -> none  [over_z(): return lax.all_to_all(piece, 'sector', 0, 0, axis_index_groups=z_groups)]
    all_to_all x1 -> x4, waiting for transfers between devices: 8.93 us -> 50.4 us  [over_z(): return lax.all_to_all(piece, 'sector', 0, 0, axis_index_groups=z_groups)]
    all_to_all x1 -> x4, starting transfers between devices: 14.9 us -> 28.2 us  [over_z(): return lax.all_to_all(piece, 'sector', 0, 0, axis_index_groups=z_groups)]
    pallas_call x16 -> x20, Pallas kernels: 47.4 us -> 43.6 us  [call(): pl.pallas_call(kernel, out_shape=[jax.ShapeDtypeStruct(shape, kind) for s...]
  transfers between devices with their start and end apart: 10 -> 13, of which waited for: 4 -> 7; matrix products, arithmetic and copies ran while one was open for 0% -> 0% of each run, Pallas kernels for 12% -> 13%
where the time goes in v3:
time: 209 us; the launch traced here: 208 us
  waiting for transfers between devices  61.4 us (29%)
  starting transfers between devices  53.7 us (26%)
  Pallas kernels  43.6 us (21%)
  blocking collectives  31.7 us (15%)
  between operations  14.7 us (7%)
  local copies, waits for them, and re-layouts  2.39 us (1%)
    all_to_all x4, waiting for transfers between devices, over_z(): return lax.all_to_all(piece, 'sector', 0, 0, axis_index_groups=z_groups)  50.4 us
    pallas_call x20, Pallas kernels, call(): pl.pallas_call(kernel, out_shape=[jax.ShapeDtypeStruct(shape, kind) for s...  43.6 us
    all_to_all x3, blocking collectives, shards(): pr = lax.all_to_all(part, 'chan', 0, 0)  31.7 us
    all_to_all x4, starting transfers between devices, over_z(): return lax.all_to_all(piece, 'sector', 0, 0, axis_index_groups=z_groups)  28.2 us
    all_to_all x2, starting transfers between devices, over_x(): return lax.all_to_all(piece, 'sector', 0, 0, axis_index_groups=x_groups)  15 us
    all_to_all x1, waiting for transfers between devices, shards(): pr = lax.all_to_all(part, 'chan', 0, 0)  6.85 us
    all_to_all x1, starting transfers between devices, shards(): pr = lax.all_to_all(part, 'chan', 0, 0)  4.51 us
  transfers between devices with their start and end apart: 13, of which 7 were waited for; matrix products, arithmetic and copies ran while one was open for 0% of the time, Pallas kernels for 13%

profile of v3, /device:TPU:6, one launch (start us, length us, event | category | flops | bytes accessed | tf_op | source)
XLA Modules:
  0.0 207.5 jit_solution(275999885915354130)
XLA Ops:
  7.2 0.9 copy-done
  8.1 1.1 shard_map.114
  9.3 10.2 %all-to-all-start = ((bf16[4,2,32,2048]{3,2,1,0:T(8,128)(2,1)}), bf16[4,2,32,2048]{3,2,1,0:T(8,128)(2,1)}, u32[]{:S(2)}, u32[]{:S(2)}) async-start(bf16[4,2,32,2048]{3,2,1,0:T(8,128)(2,1)} %shard_map.114), calls=%async_computation | async-start | bytes 2097152 | tf_op jit(solution)/shard_map/all_to_all | solution.py:273
  19.5 0.1 shard_map.113
  19.6 1.9 collective-permute-start
  21.6 3.9 %collective-permute-start.1 = (f32[24,512]{1,0:T(8,128)S(1)}, f32[24,512]{1,0:T(8,128)S(1)}, u32[]{:S(2)}, u32[]{:S(2)}) collective-permute-start(f32[24,512]{1,0:T(8,128)S(1)} %get-tuple-element.33), channel_id=1, source_target_pairs={{8,0},{16,8},{24,16},{32,24},{40,32},{48,40},{56,48},{64,56},{72,6... | collective-permute-start | bytes 147464 | tf_op jit(solution)/shard_map/ppermute | solution.py:300
  25.5 0.1 reshape.10
  25.6 0.1 pad_add_fusion.refs_0_
  25.7 2.6 %collective-permute-done.refs_3_ = f32[24,512]{1,0:T(8,128)S(1)} collective-permute-done((f32[24,512]{1,0:T(8,128)S(1)}, f32[24,512]{1,0:T(8,128)S(1)}, u32[]{:S(2)}, u32[]{:S(2)}) %collective-permute-start) | collective-permute-done | bytes 49184 | tf_op jit(solution)/shard_map/ppermute | solution.py:299
  28.2 1.4 collective-permute-done.1.refs_4_
  29.7 2.6 %shard_map.115 = (bf16[4,2,32,2048]{3,2,1,0:T(8,128)(2,1)}, f32[160,512]{1,0:T(8,128)S(1)}, f32[80,512]{1,0:T(8,128)S(1)}, f32[16,512]{1,0:T(8,128)S(1)}, bf16[1...) custom-call(s32[128]{0:T(128)S(1)} %pad_add_fusion.refs_0_, f32[2,64,512]{2,1,0:T(8,128)S(1)} %bitcast.12, ...), custom_call_target="tpu_custom_call" | custom-call | flops 1000000000 | bytes 1024 | tf_op jit(solution)/shard_map/pallas_call | solution.py:83
  32.3 14.5 %all-to-all-start.1 = ((f32[16,1,1536]{2,1,0:T(1,128)}), f32[16,1,1536]{2,1,0:T(1,128)S(1)}, u32[]{:S(2)}, u32[]{:S(2)}) async-start(f32[16,1,1536]{2,1,0:T(1,128)} %get-tuple-element.37), calls=%async_computation.1 | async-start | bytes 196608 | tf_op jit(solution)/shard_map/all_to_all | solution.py:270
  46.9 0.9 shard_map.116.refs_1_.refs_4_
  47.8 12.2 %all-to-all-done.1.refs_3_.refs_1_ = f32[16,1,1536]{2,1,0:T(1,128)S(1)} async-done(((f32[16,1,1536]{2,1,0:T(1,128)}), f32[16,1,1536]{2,1,0:T(1,128)S(1)}, u32[]{:S(2)}, u32[]{:S(2)}) %all-to-all-start.1) | async-done | bytes 98336 | tf_op jit(solution)/shard_map/all_to_all | solution.py:270
  60.0 3.0 %shard_map.117 = bf16[8,32,512]{2,1,0:T(8,128)(2,1)} custom-call(s32[1,512]{1,0:T(1,128)S(1)} %bitcast.16, f32[160,512]{1,0:T(8,128)S(1)} %shard_map.116.refs_1_.refs_4_, f32[16,512]{1,0:T(8,128)S(1)} %get-tuple-element.38.refs_2_.refs_3_.refs_4_, f32[16,1,1536]{2,1,0:T(1,128)S(1)} %all-to-all-done.1.refs_3_.refs_1_, bf16[512,2048]{1,0:T(8,128)(2,1)} %refs_8_.1), custom_call_target="tpu_custom_call" | custom-call | flops 1500000000 | bytes 1024 | tf_op jit(solution)/shard_map/pallas_call | solution.py:83
  63.0 4.5 %all-to-all-start.2 = ((bf16[8,32,512]{2,1,0:T(8,128)(2,1)}), bf16[8,32,512]{2,1,0:T(8,128)(2,1)S(1)}, u32[]{:S(2)}, u32[]{:S(2)}) async-start(bf16[8,32,512]{2,1,0:T(8,128)(2,1)} %shard_map.117), calls=%async_computation.2 | async-start | bytes 524288 | tf_op jit(solution)/shard_map/all_to_all | solution.py:422
  67.5 0.0 all-gather.11.cloned.1.call-start
  68.2 6.8 %all-to-all-done.2.refs_2_ = bf16[8,32,512]{2,1,0:T(8,128)(2,1)S(1)} async-done(((bf16[8,32,512]{2,1,0:T(8,128)(2,1)}), bf16[8,32,512]{2,1,0:T(8,128)(2,1)S(1)}, u32[]{:S(2)}, u32[]{:S(2)}) %all-to-all-start.2) | async-done | bytes 262176 | tf_op jit(solution)/shard_map/all_to_all | solution.py:422
  75.0 2.5 %shard_map.118 = (f32[16,512]{1,0:T(8,128)S(1)}, f32[1,512]{1,0:T(1,128)S(1)}, f32[2,8,512]{2,1,0:T(8,128)S(1)}) custom-call(s32[128]{0:T(128)S(1)} %pad_add_fusion.refs_0_, f32[16,1,1536]{2,1,0:T(1,128)S(1)} %all-to-all-done.1.refs_3_.refs_1_, bf16[8,32,512]{2,1,0:T(8,128)(2,1)S(1)} %all-to-all-done.2.refs_2_, ...), custom_call_target="tpu_custom_call" | custom-call | flops 2000000000 | bytes 1024 | tf_op jit(solution)/shard_map/pallas_call | solution.py:83
  77.6 0.0 all-gather.9.cloned.1.call-done
  77.6 3.7 %shard_map.119 = (f32[16,1,1536]{2,1,0:T(1,128)}, f32[160,512]{1,0:T(8,128)S(1)}, bf16[160,512]{1,0:T(8,128)(2,1)}) custom-call(s32[128]{0:T(128)S(1)} %pad_add_fusion.refs_0_, bf16[8,160,512]{2,1,0:T(8,128)(2,1)} %bitcast.24, bf16[2,8,256,256]{3,2,1,0:T(8,128)(2,1)} %refs_2_.7, f32[128]{0:T(128)S(1)} %broadcast_in_dim.16.refs_3_, ...), custom_call_target="tpu_custom_call" | custom-call | flops 4000000000 | bytes 1024 | tf_op jit(solution)/shard_map/pallas_call | solution.py:83
  81.4 4.3 %all-to-all-start.3 = ((f32[16,1,1536]{2,1,0:T(1,128)}), f32[16,1,1536]{2,1,0:T(1,128)S(1)}, u32[]{:S(2)}, u32[]{:S(2)}) async-start(f32[16,1,1536]{2,1,0:T(1,128)} %get-tuple-element.44), calls=%async_computation.3 | async-start | bytes 196608 | tf_op jit(solution)/shard_map/all_to_all | solution.py:270
  85.7 0.0 all-gather.13.cloned.1.call-start
  85.7 0.9 shard_map.120.refs_1_.refs_4_
  86.7 13.0 %all-to-all-done.3.refs_3_.refs_1_ = f32[16,1,1536]{2,1,0:T(1,128)S(1)} async-done(((f32[16,1,1536]{2,1,0:T(1,128)}), f32[16,1,1536]{2,1,0:T(1,128)S(1)}, u32[]{:S(2)}, u32[]{:S(2)}) %all-to-all-start.3) | async-done | bytes 98336 | tf_op jit(solution)/shard_map/all_to_all | solution.py:270
  99.6 2.2 %shard_map.121 = bf16[8,32,512]{2,1,0:T(8,128)(2,1)S(1)} custom-call(s32[1,512]{1,0:T(1,128)S(1)} %bitcast.18, f32[160,512]{1,0:T(8,128)S(1)} %shard_map.120.refs_1_.refs_4_, f32[16,512]{1,0:T(8,128)S(1)} %get-tuple-element.45.refs_2_.refs_3_.refs_5_, f32[16,1,1536]{2,1,0:T(1,128)S(1)} %all-to-all-done.3.refs_3_.refs_1_, bf16[512,2048]{1,0:T(8,128)(2,1)} %refs_8_.1), custom_call_target="tpu_custom_call" | custom-call | flops 1500000000 | bytes 1024 | tf_op jit(solution)/shard_map/pallas_call | solution.py:83
  101.9 10.2 %all_to_all.50.refs_2_ = bf16[8,32,512]{2,1,0:T(8,128)(2,1)S(1)} all-to-all(bf16[8,32,512]{2,1,0:T(8,128)(2,1)S(1)} %shard_map.121), channel_id=1, replica_groups=mesh['sector'=64,'chan'=8] {'chan'}, dimensions={0} | all-to-all | bytes 524288 | tf_op jit(solution)/shard_map/all_to_all | solution.py:422
  112.0 2.5 %shard_map.122 = (f32[16,512]{1,0:T(8,128)S(1)}, f32[1,512]{1,0:T(1,128)S(1)}, f32[2,8,512]{2,1,0:T(8,128)S(1)}) custom-call(s32[128]{0:T(128)S(1)} %pad_add_fusion.refs_0_, f32[16,1,1536]{2,1,0:T(1,128)S(1)} %all-to-all-done.3.refs_3_.refs_1_, bf16[8,32,512]{2,1,0:T(8,128)(2,1)S(1)} %all_to_all.50.refs_2_, ...), custom_call_target="tpu_custom_call" | custom-call | flops 2000000000 | bytes 1024 | tf_op jit(solution)/shard_map/pallas_call | solution.py:83
  114.6 3.7 %shard_map.123 = (f32[16,1,1536]{2,1,0:T(1,128)}, f32[160,512]{1,0:T(8,128)S(1)}, bf16[160,512]{1,0:T(8,128)(2,1)}) custom-call(s32[128]{0:T(128)S(1)} %pad_add_fusion.refs_0_, bf16[8,160,512]{2,1,0:T(8,128)(2,1)} %bitcast.26, bf16[2,8,256,256]{3,2,1,0:T(8,128)(2,1)} %refs_2_.7, f32[128]{0:T(128)S(1)} %broadcast_in_dim.16.refs_3_, ...), custom_call_target="tpu_custom_call" | custom-call | flops 4000000000 | bytes 1024 | tf_op jit(solution)/shard_map/pallas_call | solution.py:83
  118.4 4.8 %all-to-all-start.5 = ((f32[16,1,1536]{2,1,0:T(1,128)}), f32[16,1,1536]{2,1,0:T(1,128)S(1)}, u32[]{:S(2)}, u32[]{:S(2)}) async-start(f32[16,1,1536]{2,1,0:T(1,128)} %get-tuple-element.50), calls=%async_computation.5 | async-start | bytes 196608 | tf_op jit(solution)/shard_map/all_to_all | solution.py:270
  123.1 0.0 all-gather.15.cloned.1.call-start
  123.2 0.9 shard_map.124.refs_1_.refs_4_
  124.1 12.9 %all-to-all-done.5.refs_3_.refs_1_ = f32[16,1,1536]{2,1,0:T(1,128)S(1)} async-done(((f32[16,1,1536]{2,1,0:T(1,128)}), f32[16,1,1536]{2,1,0:T(1,128)S(1)}, u32[]{:S(2)}, u32[]{:S(2)}) %all-to-all-start.5) | async-done | bytes 98336 | tf_op jit(solution)/shard_map/all_to_all | solution.py:270
  137.0 2.2 %shard_map.125 = bf16[8,32,512]{2,1,0:T(8,128)(2,1)S(1)} custom-call(s32[1,512]{1,0:T(1,128)S(1)} %bitcast.20, f32[160,512]{1,0:T(8,128)S(1)} %shard_map.124.refs_1_.refs_4_, f32[16,512]{1,0:T(8,128)S(1)} %get-tuple-element.51.refs_2_.refs_3_.refs_6_, f32[16,1,1536]{2,1,0:T(1,128)S(1)} %all-to-all-done.5.refs_3_.refs_1_, bf16[512,2048]{1,0:T(8,128)(2,1)} %refs_8_.1), custom_call_target="tpu_custom_call" | custom-call | flops 1500000000 | bytes 1024 | tf_op jit(solution)/shard_map/pallas_call | solution.py:83
  139.2 10.7 %all_to_all.51.refs_2_ = bf16[8,32,512]{2,1,0:T(8,128)(2,1)S(1)} all-to-all(bf16[8,32,512]{2,1,0:T(8,128)(2,1)S(1)} %shard_map.125), channel_id=1, replica_groups=mesh['sector'=64,'chan'=8] {'chan'}, dimensions={0} | all-to-all | bytes 524288 | tf_op jit(solution)/shard_map/all_to_all | solution.py:422
  149.9 2.5 %shard_map.126 = (f32[16,512]{1,0:T(8,128)S(1)}, f32[1,512]{1,0:T(1,128)S(1)}, f32[2,8,512]{2,1,0:T(8,128)S(1)}) custom-call(s32[128]{0:T(128)S(1)} %pad_add_fusion.refs_0_, f32[16,1,1536]{2,1,0:T(1,128)S(1)} %all-to-all-done.5.refs_3_.refs_1_, bf16[8,32,512]{2,1,0:T(8,128)(2,1)S(1)} %all_to_all.51.refs_2_, ...), custom_call_target="tpu_custom_call" | custom-call | flops 2000000000 | bytes 1024 | tf_op jit(solution)/shard_map/pallas_call | solution.py:83
  152.4 0.0 all-gather.13.cloned.1.call-done
  152.4 3.7 %shard_map.127 = (f32[16,1,1536]{2,1,0:T(1,128)}, f32[160,512]{1,0:T(8,128)S(1)}, bf16[160,512]{1,0:T(8,128)(2,1)}) custom-call(s32[128]{0:T(128)S(1)} %pad_add_fusion.refs_0_, bf16[8,160,512]{2,1,0:T(8,128)(2,1)} %bitcast.25, bf16[2,8,256,256]{3,2,1,0:T(8,128)(2,1)} %refs_2_.7, f32[128]{0:T(128)S(1)} %broadcast_in_dim.16.refs_3_, ...), custom_call_target="tpu_custom_call" | custom-call | flops 4000000000 | bytes 1024 | tf_op jit(solution)/shard_map/pallas_call | solution.py:83
  156.2 4.7 %all-to-all-start.7 = ((f32[16,1,1536]{2,1,0:T(1,128)}), f32[16,1,1536]{2,1,0:T(1,128)S(1)}, u32[]{:S(2)}, u32[]{:S(2)}) async-start(f32[16,1,1536]{2,1,0:T(1,128)} %get-tuple-element.56), calls=%async_computation.7 | async-start | bytes 196608 | tf_op jit(solution)/shard_map/all_to_all | solution.py:270
  160.9 1.1 shard_map.128.refs_1_.refs_4_
  162.0 12.4 %all-to-all-done.7.refs_3_.refs_1_ = f32[16,1,1536]{2,1,0:T(1,128)S(1)} async-done(((f32[16,1,1536]{2,1,0:T(1,128)}), f32[16,1,1536]{2,1,0:T(1,128)S(1)}, u32[]{:S(2)}, u32[]{:S(2)}) %all-to-all-start.7) | async-done | bytes 98336 | tf_op jit(solution)/shard_map/all_to_all | solution.py:270
  174.4 2.2 %shard_map.129 = bf16[8,32,512]{2,1,0:T(8,128)(2,1)S(1)} custom-call(s32[1,512]{1,0:T(1,128)S(1)} %bitcast.22, f32[160,512]{1,0:T(8,128)S(1)} %shard_map.128.refs_1_.refs_4_, f32[16,512]{1,0:T(8,128)S(1)} %get-tuple-element.57.refs_2_.refs_3_, f32[16,1,1536]{2,1,0:T(1,128)S(1)} %all-to-all-done.7.refs_3_.refs_1_, bf16[512,2048]{1,0:T(8,128)(2,1)} %refs_8_.1), custom_call_target="tpu_custom_call" | custom-call | flops 1500000000 | bytes 1024 | tf_op jit(solution)/shard_map/pallas_call | solution.py:83
  176.5 10.8 %all_to_all.52.refs_2_ = bf16[8,32,512]{2,1,0:T(8,128)(2,1)S(1)} all-to-all(bf16[8,32,512]{2,1,0:T(8,128)(2,1)S(1)} %shard_map.129), channel_id=1, replica_groups=mesh['sector'=64,'chan'=8] {'chan'}, dimensions={0} | all-to-all | bytes 524288 | tf_op jit(solution)/shard_map/all_to_all | solution.py:422
  187.3 3.0 %shard_map.130 = (f32[4,2,2,2048]{3,2,1,0:T(2,128)}, f32[2,8,512]{2,1,0:T(8,128)S(1)}) custom-call(s32[128]{0:T(128)S(1)} %pad_add_fusion.refs_0_, f32[16,1,1536]{2,1,0:T(1,128)S(1)} %all-to-all-done.7.refs_3_.refs_1_, bf16[8,32,512]{2,1,0:T(8,128)(2,1)S(1)} %all_to_all.52.refs_2_, f32[16,512]{1,0:T(8,128)S(1)} %get-tuple-element.57.refs_2_.refs_3_, ...), custom_call_target="tpu_custom_call" | custom-call | flops 2000000000 | bytes 1024 | tf_op jit(solution)/shard_map/pallas_call | solution.py:83
  190.3 4.8 %all-to-all-start.9 = ((f32[4,2,2,2048]{3,2,1,0:T(2,128)}), f32[4,2,2,2048]{3,2,1,0:T(2,128)S(1)}, u32[]{:S(2)}, u32[]{:S(2)}) async-start(f32[4,2,2,2048]{3,2,1,0:T(2,128)} %get-tuple-element.60), calls=%async_computation.9 | async-start | bytes 262144 | tf_op jit(solution)/shard_map/all_to_all | solution.py:273
  195.1 1.3 copy-done.3
  196.4 3.7 %shard_map.131 = (f32[2,64,512]{2,1,0:T(8,128)}, f32[2,8,128]{2,1,0:T(8,128)S(1)}) custom-call(s32[128]{0:T(128)S(1)} %pad_add_fusion.refs_0_, bf16[8,160,512]{2,1,0:T(8,128)(2,1)S(1)} %bitcast.15, bf16[2,8,256,256]{3,2,1,0:T(8,128)(2,1)} %refs_2_.7, f32[128]{0:T(128)S(1)} %broadcast_in_dim.16.refs_3_, f32[160,512]{1,0:T(8,128)S(1)} %shard_map.128.refs_1_.refs_4_, ...), custom_call_target="tpu_custom_call" | custom-call | flops 4000000000 | bytes 1024 | tf_op jit(solution)/shard_map/pallas_call | solution.py:83
  200.2 0.8 shard_map.132
  (27 shorter events, 0.1 us)
Async XLA Ops:
  7.2 1.0 copy-start
  9.2 10.3 %copy-start.1 = (f32[2,512,64]{1,2,0:T(8,128)S(1)}, f32[2,512,64]{1,2,0:T(8,128)}, u32[]{:S(2)}) copy-start(f32[2,512,64]{1,2,0:T(8,128)} %param.10) | copy-start | bytes 786436
  9.2 10.3 %copy-start.2 = (bf16[512,64]{0,1:T(8,128)(2,1)S(1)}, bf16[512,64]{0,1:T(8,128)(2,1)}, u32[]{:S(2)}) copy-start(bf16[512,64]{0,1:T(8,128)(2,1)} %param.11) | copy-start | bytes 196612
  9.2 16.3 %copy-start.8 = (s32[2,8]{1,0:T(2,128)S(1)}, s32[2,8]{1,0:T(2,128)}, u32[]{:S(2)}) copy-start(s32[2,8]{1,0:T(2,128)} %param.13) | copy-start | bytes 196
  9.2 16.3 %copy-start.7 = (s32[2]{0:T(128)S(1)}, s32[2]{0:T(128)}, u32[]{:S(2)}) copy-start(s32[2]{0:T(128)} %param.16) | copy-start | bytes 28
  9.3 20.4 %copy-start.4 = (f32[2,2,2048]{2,1,0:T(2,128)S(1)}, f32[2,2,2048]{2,1,0:T(2,128)}, u32[]{:S(2)}) copy-start(f32[2,2,2048]{2,1,0:T(2,128)} %refs_5_.4) | copy-start | bytes 98308
  9.3 20.4 %all-to-all-start = ((bf16[4,2,32,2048]{3,2,1,0:T(8,128)(2,1)}), bf16[4,2,32,2048]{3,2,1,0:T(8,128)(2,1)}, u32[]{:S(2)}, u32[]{:S(2)}) async-start(bf16[4,2,32,2048]{3,2,1,0:T(8,128)(2,1)} %shard_map.114), calls=%async_computation | async-start | bytes 2097152 | tf_op jit(solution)/shard_map/all_to_all | solution.py:273
  19.5 58.1 %all-gather.9.cloned.1.call-start = ((), (), s32[]{:S(2)}) async-start(), calls=%async_computation.10 | async-start | bytes 1474560 | tf_op jit(solution)/shard_map/all_gather | solution.py:413
  19.6 8.6 %collective-permute-start = (f32[24,512]{1,0:T(8,128)S(1)}, f32[24,512]{1,0:T(8,128)S(1)}, u32[]{:S(2)}, u32[]{:S(2)}) collective-permute-start(f32[24,512]{1,0:T(8,128)S(1)} %get-tuple-element.32), channel_id=1, source_target_pairs={{0,8},{8,16},{16,24},{24,32},{32,40},{40,48},{48,56},{56,64},{64,7... | collective-permute-start | bytes 147464 | tf_op jit(solution)/shard_map/ppermute | solution.py:299
  21.6 8.1 %collective-permute-start.1 = (f32[24,512]{1,0:T(8,128)S(1)}, f32[24,512]{1,0:T(8,128)S(1)}, u32[]{:S(2)}, u32[]{:S(2)}) collective-permute-start(f32[24,512]{1,0:T(8,128)S(1)} %get-tuple-element.33), channel_id=1, source_target_pairs={{8,0},{16,8},{24,16},{32,24},{40,32},{48,40},{56,48},{64,56},{72,6... | collective-permute-start | bytes 147464 | tf_op jit(solution)/shard_map/ppermute | solution.py:300
  32.3 27.6 %all-to-all-start.1 = ((f32[16,1,1536]{2,1,0:T(1,128)}), f32[16,1,1536]{2,1,0:T(1,128)S(1)}, u32[]{:S(2)}, u32[]{:S(2)}) async-start(f32[16,1,1536]{2,1,0:T(1,128)} %get-tuple-element.37), calls=%async_computation.1 | async-start | bytes 196608 | tf_op jit(solution)/shard_map/all_to_all | solution.py:270
  46.9 13.1 %copy-start.5 = (s32[512]{0:T(512)S(1)}, s32[512]{0:T(512)}, u32[]{:S(2)}) copy-start(s32[512]{0:T(512)} %param.15) | copy-start | bytes 6148
  60.0 15.0 %copy-start.6 = (bf16[4,2,32,2048]{3,2,1,0:T(8,128)(2,1)S(1)}, bf16[4,2,32,2048]{3,2,1,0:T(8,128)(2,1)}, u32[]{:S(2)}) copy-start(bf16[4,2,32,2048]{3,2,1,0:T(8,128)(2,1)} %get-tuple-element.39.refs_6_) | copy-start | bytes 3145732
  63.0 12.1 %all-to-all-start.2 = ((bf16[8,32,512]{2,1,0:T(8,128)(2,1)}), bf16[8,32,512]{2,1,0:T(8,128)(2,1)S(1)}, u32[]{:S(2)}, u32[]{:S(2)}) async-start(bf16[8,32,512]{2,1,0:T(8,128)(2,1)} %shard_map.117), calls=%async_computation.2 | async-start | bytes 524288 | tf_op jit(solution)/shard_map/all_to_all | solution.py:422
  67.5 47.1 %all-gather.11.cloned.1.call-start = ((), (), s32[]{:S(2)}) async-start(), calls=%async_computation.11 | async-start | bytes 1474560 | tf_op jit(solution)/shard_map/all_gather | solution.py:413
  81.4 18.3 %all-to-all-start.3 = ((f32[16,1,1536]{2,1,0:T(1,128)}), f32[16,1,1536]{2,1,0:T(1,128)S(1)}, u32[]{:S(2)}, u32[]{:S(2)}) async-start(f32[16,1,1536]{2,1,0:T(1,128)} %get-tuple-element.44), calls=%async_computation.3 | async-start | bytes 196608 | tf_op jit(solution)/shard_map/all_to_all | solution.py:270
  85.7 66.7 %all-gather.13.cloned.1.call-start = ((), (), s32[]{:S(2)}) async-start(), calls=%async_computation.12 | async-start | bytes 1474560 | tf_op jit(solution)/shard_map/all_gather | solution.py:413
  118.4 18.6 %all-to-all-start.5 = ((f32[16,1,1536]{2,1,0:T(1,128)}), f32[16,1,1536]{2,1,0:T(1,128)S(1)}, u32[]{:S(2)}, u32[]{:S(2)}) async-start(f32[16,1,1536]{2,1,0:T(1,128)} %get-tuple-element.50), calls=%async_computation.5 | async-start | bytes 196608 | tf_op jit(solution)/shard_map/all_to_all | solution.py:270
  123.1 72.0 %all-gather.15.cloned.1.call-start = ((), (), s32[]{:S(2)}) async-start(), calls=%async_computation.13 | async-start | bytes 1474560 | tf_op jit(solution)/shard_map/all_gather | solution.py:413
  156.2 18.1 %all-to-all-start.7 = ((f32[16,1,1536]{2,1,0:T(1,128)}), f32[16,1,1536]{2,1,0:T(1,128)S(1)}, u32[]{:S(2)}, u32[]{:S(2)}) async-start(f32[16,1,1536]{2,1,0:T(1,128)} %get-tuple-element.56), calls=%async_computation.7 | async-start | bytes 196608 | tf_op jit(solution)/shard_map/all_to_all | solution.py:270
  190.3 9.8 %all-to-all-start.9 = ((f32[4,2,2,2048]{3,2,1,0:T(2,128)}), f32[4,2,2,2048]{3,2,1,0:T(2,128)S(1)}, u32[]{:S(2)}, u32[]{:S(2)}) async-start(f32[4,2,2,2048]{3,2,1,0:T(2,128)} %get-tuple-element.60), calls=%async_computation.9 | async-start | bytes 262144 | tf_op jit(solution)/shard_map/all_to_all | solution.py:273
  195.1 1.3 copy-start.3
Sparse Core Ops, SparseCore 0:
  32.5 34.9 all-gather.8
  81.5 23.4 all-gather.10
  118.5 24.1 all-gather.12
  156.3 23.9 all-gather.14

commit v4 on v3

--- a/solution.py
+++ b/solution.py
@@ -245,10 +245,9 @@
 def ghost_term(r, order):
     r.wait("info")
     row = rows_of((8, 512))
-    hub = jnp.where(r.info[18] == 0, 1.0 / order, 0.0).astype(F32)
     images = []
     for ghost in ghost_of(r):
-        ghost = ghost * hub
+        ghost = jnp.where(r.info[18] == 0, ghost * (1.0 / order), 0.0)
         images.append(jnp.where(row == 0, (-15.0 * KINETIC) * ghost, jnp.where(row == 1, KINETIC * ghost, 0.0)))
     return images[1], -images[0]
 

time: 209 us -> 209 us (level)
  no operation moved by 1% of the time
where the time goes in v4:
time: 209 us; the launch traced here: 208 us
  waiting for transfers between devices  61.4 us (29%)
  starting transfers between devices  53.7 us (26%)
  Pallas kernels  43.6 us (21%)
  blocking collectives  31.7 us (15%)
  between operations  14.7 us (7%)
  local copies, waits for them, and re-layouts  2.39 us (1%)
    all_to_all x4, waiting for transfers between devices, over_z(): return lax.all_to_all(piece, 'sector', 0, 0, axis_index_groups=z_groups)  50.4 us
    pallas_call x20, Pallas kernels, call(): pl.pallas_call(kernel, out_shape=[jax.ShapeDtypeStruct(shape, kind) for s...  43.6 us
    all_to_all x3, blocking collectives, shards(): pr = lax.all_to_all(part, 'chan', 0, 0)  31.7 us
    all_to_all x4, starting transfers between devices, over_z(): return lax.all_to_all(piece, 'sector', 0, 0, axis_index_groups=z_groups)  28.2 us
    all_to_all x2, starting transfers between devices, over_x(): return lax.all_to_all(piece, 'sector', 0, 0, axis_index_groups=x_groups)  14.9 us
    all_to_all x1, waiting for transfers between devices, shards(): pr = lax.all_to_all(part, 'chan', 0, 0)  6.85 us
    all_to_all x1, starting transfers between devices, shards(): pr = lax.all_to_all(part, 'chan', 0, 0)  4.51 us
  transfers between devices with their start and end apart: 13, of which 7 were waited for; matrix products, arithmetic and copies ran while one was open for 0% of the time, Pallas kernels for 13%

profile of v4, /device:TPU:6, one launch (start us, length us, event | category | flops | bytes accessed | tf_op | source)
XLA Modules:
  0.0 207.5 jit_solution(20141713029896819)
XLA Ops:
  7.2 0.9 copy-done
  8.1 1.1 shard_map.114
  9.3 10.2 %all-to-all-start = ((bf16[4,2,32,2048]{3,2,1,0:T(8,128)(2,1)}), bf16[4,2,32,2048]{3,2,1,0:T(8,128)(2,1)}, u32[]{:S(2)}, u32[]{:S(2)}) async-start(bf16[4,2,32,2048]{3,2,1,0:T(8,128)(2,1)} %shard_map.114), calls=%async_computation | async-start | bytes 2097152 | tf_op jit(solution)/shard_map/all_to_all | solution.py:272
  19.5 0.1 shard_map.113
  19.6 1.9 collective-permute-start
  21.6 3.9 %collective-permute-start.1 = (f32[24,512]{1,0:T(8,128)S(1)}, f32[24,512]{1,0:T(8,128)S(1)}, u32[]{:S(2)}, u32[]{:S(2)}) collective-permute-start(f32[24,512]{1,0:T(8,128)S(1)} %get-tuple-element.33), channel_id=1, source_target_pairs={{8,0},{16,8},{24,16},{32,24},{40,32},{48,40},{56,48},{64,56},{72,6... | collective-permute-start | bytes 147464 | tf_op jit(solution)/shard_map/ppermute | solution.py:299
  25.5 0.1 reshape.10
  25.6 0.1 pad_add_fusion.refs_0_
  25.7 2.6 %collective-permute-done.refs_3_ = f32[24,512]{1,0:T(8,128)S(1)} collective-permute-done((f32[24,512]{1,0:T(8,128)S(1)}, f32[24,512]{1,0:T(8,128)S(1)}, u32[]{:S(2)}, u32[]{:S(2)}) %collective-permute-start) | collective-permute-done | bytes 49184 | tf_op jit(solution)/shard_map/ppermute | solution.py:298
  28.2 1.4 collective-permute-done.1.refs_4_
  29.7 2.6 %shard_map.115 = (bf16[4,2,32,2048]{3,2,1,0:T(8,128)(2,1)}, f32[160,512]{1,0:T(8,128)S(1)}, f32[80,512]{1,0:T(8,128)S(1)}, f32[16,512]{1,0:T(8,128)S(1)}, bf16[1...) custom-call(s32[128]{0:T(128)S(1)} %pad_add_fusion.refs_0_, f32[2,64,512]{2,1,0:T(8,128)S(1)} %bitcast.12, ...), custom_call_target="tpu_custom_call" | custom-call | flops 1000000000 | bytes 1024 | tf_op jit(solution)/shard_map/pallas_call | solution.py:83
  32.3 14.5 %all-to-all-start.1 = ((f32[16,1,1536]{2,1,0:T(1,128)}), f32[16,1,1536]{2,1,0:T(1,128)S(1)}, u32[]{:S(2)}, u32[]{:S(2)}) async-start(f32[16,1,1536]{2,1,0:T(1,128)} %get-tuple-element.37), calls=%async_computation.1 | async-start | bytes 196608 | tf_op jit(solution)/shard_map/all_to_all | solution.py:269
  46.9 0.9 shard_map.116.refs_1_.refs_4_
  47.8 12.2 %all-to-all-done.1.refs_3_.refs_1_ = f32[16,1,1536]{2,1,0:T(1,128)S(1)} async-done(((f32[16,1,1536]{2,1,0:T(1,128)}), f32[16,1,1536]{2,1,0:T(1,128)S(1)}, u32[]{:S(2)}, u32[]{:S(2)}) %all-to-all-start.1) | async-done | bytes 98336 | tf_op jit(solution)/shard_map/all_to_all | solution.py:269
  60.0 3.0 %shard_map.117 = bf16[8,32,512]{2,1,0:T(8,128)(2,1)} custom-call(s32[1,512]{1,0:T(1,128)S(1)} %bitcast.16, f32[160,512]{1,0:T(8,128)S(1)} %shard_map.116.refs_1_.refs_4_, f32[16,512]{1,0:T(8,128)S(1)} %get-tuple-element.38.refs_2_.refs_3_.refs_4_, f32[16,1,1536]{2,1,0:T(1,128)S(1)} %all-to-all-done.1.refs_3_.refs_1_, bf16[512,2048]{1,0:T(8,128)(2,1)} %refs_8_.1), custom_call_target="tpu_custom_call" | custom-call | flops 1500000000 | bytes 1024 | tf_op jit(solution)/shard_map/pallas_call | solution.py:83
  63.0 4.5 %all-to-all-start.2 = ((bf16[8,32,512]{2,1,0:T(8,128)(2,1)}), bf16[8,32,512]{2,1,0:T(8,128)(2,1)S(1)}, u32[]{:S(2)}, u32[]{:S(2)}) async-start(bf16[8,32,512]{2,1,0:T(8,128)(2,1)} %shard_map.117), calls=%async_computation.2 | async-start | bytes 524288 | tf_op jit(solution)/shard_map/all_to_all | solution.py:421
  67.5 0.0 all-gather.11.cloned.1.call-start
  68.2 6.8 %all-to-all-done.2.refs_2_ = bf16[8,32,512]{2,1,0:T(8,128)(2,1)S(1)} async-done(((bf16[8,32,512]{2,1,0:T(8,128)(2,1)}), bf16[8,32,512]{2,1,0:T(8,128)(2,1)S(1)}, u32[]{:S(2)}, u32[]{:S(2)}) %all-to-all-start.2) | async-done | bytes 262176 | tf_op jit(solution)/shard_map/all_to_all | solution.py:421
  75.0 2.5 %shard_map.118 = (f32[16,512]{1,0:T(8,128)S(1)}, f32[1,512]{1,0:T(1,128)S(1)}, f32[2,8,512]{2,1,0:T(8,128)S(1)}) custom-call(s32[128]{0:T(128)S(1)} %pad_add_fusion.refs_0_, f32[16,1,1536]{2,1,0:T(1,128)S(1)} %all-to-all-done.1.refs_3_.refs_1_, bf16[8,32,512]{2,1,0:T(8,128)(2,1)S(1)} %all-to-all-done.2.refs_2_, ...), custom_call_target="tpu_custom_call" | custom-call | flops 2000000000 | bytes 1024 | tf_op jit(solution)/shard_map/pallas_call | solution.py:83
  77.6 0.0 all-gather.9.cloned.1.call-done
  77.6 3.7 %shard_map.119 = (f32[16,1,1536]{2,1,0:T(1,128)}, f32[160,512]{1,0:T(8,128)S(1)}, bf16[160,512]{1,0:T(8,128)(2,1)}) custom-call(s32[128]{0:T(128)S(1)} %pad_add_fusion.refs_0_, bf16[8,160,512]{2,1,0:T(8,128)(2,1)} %bitcast.24, bf16[2,8,256,256]{3,2,1,0:T(8,128)(2,1)} %refs_2_.7, f32[128]{0:T(128)S(1)} %broadcast_in_dim.16.refs_3_, ...), custom_call_target="tpu_custom_call" | custom-call | flops 4000000000 | bytes 1024 | tf_op jit(solution)/shard_map/pallas_call | solution.py:83
  81.4 4.3 %all-to-all-start.3 = ((f32[16,1,1536]{2,1,0:T(1,128)}), f32[16,1,1536]{2,1,0:T(1,128)S(1)}, u32[]{:S(2)}, u32[]{:S(2)}) async-start(f32[16,1,1536]{2,1,0:T(1,128)} %get-tuple-element.44), calls=%async_computation.3 | async-start | bytes 196608 | tf_op jit(solution)/shard_map/all_to_all | solution.py:269
  85.7 0.0 all-gather.13.cloned.1.call-start
  85.7 0.9 shard_map.120.refs_1_.refs_4_
  86.7 13.0 %all-to-all-done.3.refs_3_.refs_1_ = f32[16,1,1536]{2,1,0:T(1,128)S(1)} async-done(((f32[16,1,1536]{2,1,0:T(1,128)}), f32[16,1,1536]{2,1,0:T(1,128)S(1)}, u32[]{:S(2)}, u32[]{:S(2)}) %all-to-all-start.3) | async-done | bytes 98336 | tf_op jit(solution)/shard_map/all_to_all | solution.py:269
  99.6 2.2 %shard_map.121 = bf16[8,32,512]{2,1,0:T(8,128)(2,1)S(1)} custom-call(s32[1,512]{1,0:T(1,128)S(1)} %bitcast.18, f32[160,512]{1,0:T(8,128)S(1)} %shard_map.120.refs_1_.refs_4_, f32[16,512]{1,0:T(8,128)S(1)} %get-tuple-element.45.refs_2_.refs_3_.refs_5_, f32[16,1,1536]{2,1,0:T(1,128)S(1)} %all-to-all-done.3.refs_3_.refs_1_, bf16[512,2048]{1,0:T(8,128)(2,1)} %refs_8_.1), custom_call_target="tpu_custom_call" | custom-call | flops 1500000000 | bytes 1024 | tf_op jit(solution)/shard_map/pallas_call | solution.py:83
  101.9 10.2 %all_to_all.50.refs_2_ = bf16[8,32,512]{2,1,0:T(8,128)(2,1)S(1)} all-to-all(bf16[8,32,512]{2,1,0:T(8,128)(2,1)S(1)} %shard_map.121), channel_id=1, replica_groups=mesh['sector'=64,'chan'=8] {'chan'}, dimensions={0} | all-to-all | bytes 524288 | tf_op jit(solution)/shard_map/all_to_all | solution.py:421
  112.0 2.5 %shard_map.122 = (f32[16,512]{1,0:T(8,128)S(1)}, f32[1,512]{1,0:T(1,128)S(1)}, f32[2,8,512]{2,1,0:T(8,128)S(1)}) custom-call(s32[128]{0:T(128)S(1)} %pad_add_fusion.refs_0_, f32[16,1,1536]{2,1,0:T(1,128)S(1)} %all-to-all-done.3.refs_3_.refs_1_, bf16[8,32,512]{2,1,0:T(8,128)(2,1)S(1)} %all_to_all.50.refs_2_, ...), custom_call_target="tpu_custom_call" | custom-call | flops 2000000000 | bytes 1024 | tf_op jit(solution)/shard_map/pallas_call | solution.py:83
  114.6 0.0 all-gather.11.cloned.1.call-done
  114.6 3.7 %shard_map.123 = (f32[16,1,1536]{2,1,0:T(1,128)}, f32[160,512]{1,0:T(8,128)S(1)}, bf16[160,512]{1,0:T(8,128)(2,1)}) custom-call(s32[128]{0:T(128)S(1)} %pad_add_fusion.refs_0_, bf16[8,160,512]{2,1,0:T(8,128)(2,1)} %bitcast.26, bf16[2,8,256,256]{3,2,1,0:T(8,128)(2,1)} %refs_2_.7, f32[128]{0:T(128)S(1)} %broadcast_in_dim.16.refs_3_, ...), custom_call_target="tpu_custom_call" | custom-call | flops 4000000000 | bytes 1024 | tf_op jit(solution)/shard_map/pallas_call | solution.py:83
  118.4 4.7 %all-to-all-start.5 = ((f32[16,1,1536]{2,1,0:T(1,128)}), f32[16,1,1536]{2,1,0:T(1,128)S(1)}, u32[]{:S(2)}, u32[]{:S(2)}) async-start(f32[16,1,1536]{2,1,0:T(1,128)} %get-tuple-element.50), calls=%async_computation.5 | async-start | bytes 196608 | tf_op jit(solution)/shard_map/all_to_all | solution.py:269
  123.1 0.0 all-gather.15.cloned.1.call-start
  123.2 0.9 shard_map.124.refs_1_.refs_4_
  124.1 12.9 %all-to-all-done.5.refs_3_.refs_1_ = f32[16,1,1536]{2,1,0:T(1,128)S(1)} async-done(((f32[16,1,1536]{2,1,0:T(1,128)}), f32[16,1,1536]{2,1,0:T(1,128)S(1)}, u32[]{:S(2)}, u32[]{:S(2)}) %all-to-all-start.5) | async-done | bytes 98336 | tf_op jit(solution)/shard_map/all_to_all | solution.py:269
  137.0 2.2 %shard_map.125 = bf16[8,32,512]{2,1,0:T(8,128)(2,1)S(1)} custom-call(s32[1,512]{1,0:T(1,128)S(1)} %bitcast.20, f32[160,512]{1,0:T(8,128)S(1)} %shard_map.124.refs_1_.refs_4_, f32[16,512]{1,0:T(8,128)S(1)} %get-tuple-element.51.refs_2_.refs_3_.refs_6_, f32[16,1,1536]{2,1,0:T(1,128)S(1)} %all-to-all-done.5.refs_3_.refs_1_, bf16[512,2048]{1,0:T(8,128)(2,1)} %refs_8_.1), custom_call_target="tpu_custom_call" | custom-call | flops 1500000000 | bytes 1024 | tf_op jit(solution)/shard_map/pallas_call | solution.py:83
  139.2 10.7 %all_to_all.51.refs_2_ = bf16[8,32,512]{2,1,0:T(8,128)(2,1)S(1)} all-to-all(bf16[8,32,512]{2,1,0:T(8,128)(2,1)S(1)} %shard_map.125), channel_id=1, replica_groups=mesh['sector'=64,'chan'=8] {'chan'}, dimensions={0} | all-to-all | bytes 524288 | tf_op jit(solution)/shard_map/all_to_all | solution.py:421
  149.9 2.5 %shard_map.126 = (f32[16,512]{1,0:T(8,128)S(1)}, f32[1,512]{1,0:T(1,128)S(1)}, f32[2,8,512]{2,1,0:T(8,128)S(1)}) custom-call(s32[128]{0:T(128)S(1)} %pad_add_fusion.refs_0_, f32[16,1,1536]{2,1,0:T(1,128)S(1)} %all-to-all-done.5.refs_3_.refs_1_, bf16[8,32,512]{2,1,0:T(8,128)(2,1)S(1)} %all_to_all.51.refs_2_, ...), custom_call_target="tpu_custom_call" | custom-call | flops 2000000000 | bytes 1024 | tf_op jit(solution)/shard_map/pallas_call | solution.py:83
  152.4 3.7 %shard_map.127 = (f32[16,1,1536]{2,1,0:T(1,128)}, f32[160,512]{1,0:T(8,128)S(1)}, bf16[160,512]{1,0:T(8,128)(2,1)}) custom-call(s32[128]{0:T(128)S(1)} %pad_add_fusion.refs_0_, bf16[8,160,512]{2,1,0:T(8,128)(2,1)} %bitcast.25, bf16[2,8,256,256]{3,2,1,0:T(8,128)(2,1)} %refs_2_.7, f32[128]{0:T(128)S(1)} %broadcast_in_dim.16.refs_3_, ...), custom_call_target="tpu_custom_call" | custom-call | flops 4000000000 | bytes 1024 | tf_op jit(solution)/shard_map/pallas_call | solution.py:83
  156.2 4.7 %all-to-all-start.7 = ((f32[16,1,1536]{2,1,0:T(1,128)}), f32[16,1,1536]{2,1,0:T(1,128)S(1)}, u32[]{:S(2)}, u32[]{:S(2)}) async-start(f32[16,1,1536]{2,1,0:T(1,128)} %get-tuple-element.56), calls=%async_computation.7 | async-start | bytes 196608 | tf_op jit(solution)/shard_map/all_to_all | solution.py:269
  160.9 1.1 shard_map.128.refs_1_.refs_4_
  162.0 12.4 %all-to-all-done.7.refs_3_.refs_1_ = f32[16,1,1536]{2,1,0:T(1,128)S(1)} async-done(((f32[16,1,1536]{2,1,0:T(1,128)}), f32[16,1,1536]{2,1,0:T(1,128)S(1)}, u32[]{:S(2)}, u32[]{:S(2)}) %all-to-all-start.7) | async-done | bytes 98336 | tf_op jit(solution)/shard_map/all_to_all | solution.py:269
  174.4 2.2 %shard_map.129 = bf16[8,32,512]{2,1,0:T(8,128)(2,1)S(1)} custom-call(s32[1,512]{1,0:T(1,128)S(1)} %bitcast.22, f32[160,512]{1,0:T(8,128)S(1)} %shard_map.128.refs_1_.refs_4_, f32[16,512]{1,0:T(8,128)S(1)} %get-tuple-element.57.refs_2_.refs_3_, f32[16,1,1536]{2,1,0:T(1,128)S(1)} %all-to-all-done.7.refs_3_.refs_1_, bf16[512,2048]{1,0:T(8,128)(2,1)} %refs_8_.1), custom_call_target="tpu_custom_call" | custom-call | flops 1500000000 | bytes 1024 | tf_op jit(solution)/shard_map/pallas_call | solution.py:83
  176.6 10.8 %all_to_all.52.refs_2_ = bf16[8,32,512]{2,1,0:T(8,128)(2,1)S(1)} all-to-all(bf16[8,32,512]{2,1,0:T(8,128)(2,1)S(1)} %shard_map.129), channel_id=1, replica_groups=mesh['sector'=64,'chan'=8] {'chan'}, dimensions={0} | all-to-all | bytes 524288 | tf_op jit(solution)/shard_map/all_to_all | solution.py:421
  187.4 3.0 %shard_map.130 = (f32[4,2,2,2048]{3,2,1,0:T(2,128)}, f32[2,8,512]{2,1,0:T(8,128)S(1)}) custom-call(s32[128]{0:T(128)S(1)} %pad_add_fusion.refs_0_, f32[16,1,1536]{2,1,0:T(1,128)S(1)} %all-to-all-done.7.refs_3_.refs_1_, bf16[8,32,512]{2,1,0:T(8,128)(2,1)S(1)} %all_to_all.52.refs_2_, f32[16,512]{1,0:T(8,128)S(1)} %get-tuple-element.57.refs_2_.refs_3_, ...), custom_call_target="tpu_custom_call" | custom-call | flops 2000000000 | bytes 1024 | tf_op jit(solution)/shard_map/pallas_call | solution.py:83
  190.4 4.7 %all-to-all-start.9 = ((f32[4,2,2,2048]{3,2,1,0:T(2,128)}), f32[4,2,2,2048]{3,2,1,0:T(2,128)S(1)}, u32[]{:S(2)}, u32[]{:S(2)}) async-start(f32[4,2,2,2048]{3,2,1,0:T(2,128)} %get-tuple-element.60), calls=%async_computation.9 | async-start | bytes 262144 | tf_op jit(solution)/shard_map/all_to_all | solution.py:272
  195.1 1.3 copy-done.3
  196.4 3.7 %shard_map.131 = (f32[2,64,512]{2,1,0:T(8,128)}, f32[2,8,128]{2,1,0:T(8,128)S(1)}) custom-call(s32[128]{0:T(128)S(1)} %pad_add_fusion.refs_0_, bf16[8,160,512]{2,1,0:T(8,128)(2,1)S(1)} %bitcast.15, bf16[2,8,256,256]{3,2,1,0:T(8,128)(2,1)} %refs_2_.7, f32[128]{0:T(128)S(1)} %broadcast_in_dim.16.refs_3_, f32[160,512]{1,0:T(8,128)S(1)} %shard_map.128.refs_1_.refs_4_, ...), custom_call_target="tpu_custom_call" | custom-call | flops 4000000000 | bytes 1024 | tf_op jit(solution)/shard_map/pallas_call | solution.py:83
  200.2 0.8 shard_map.132
  (27 shorter events, 0.1 us)
Async XLA Ops:
  7.2 1.0 copy-start
  9.2 10.3 %copy-start.1 = (f32[2,512,64]{1,2,0:T(8,128)S(1)}, f32[2,512,64]{1,2,0:T(8,128)}, u32[]{:S(2)}) copy-start(f32[2,512,64]{1,2,0:T(8,128)} %param.10) | copy-start | bytes 786436
  9.2 10.3 %copy-start.2 = (bf16[512,64]{0,1:T(8,128)(2,1)S(1)}, bf16[512,64]{0,1:T(8,128)(2,1)}, u32[]{:S(2)}) copy-start(bf16[512,64]{0,1:T(8,128)(2,1)} %param.11) | copy-start | bytes 196612
  9.2 16.3 %copy-start.8 = (s32[2,8]{1,0:T(2,128)S(1)}, s32[2,8]{1,0:T(2,128)}, u32[]{:S(2)}) copy-start(s32[2,8]{1,0:T(2,128)} %param.13) | copy-start | bytes 196
  9.2 16.3 %copy-start.7 = (s32[2]{0:T(128)S(1)}, s32[2]{0:T(128)}, u32[]{:S(2)}) copy-start(s32[2]{0:T(128)} %param.16) | copy-start | bytes 28
  9.3 20.4 %copy-start.4 = (f32[2,2,2048]{2,1,0:T(2,128)S(1)}, f32[2,2,2048]{2,1,0:T(2,128)}, u32[]{:S(2)}) copy-start(f32[2,2,2048]{2,1,0:T(2,128)} %refs_5_.4) | copy-start | bytes 98308
  9.3 20.4 %all-to-all-start = ((bf16[4,2,32,2048]{3,2,1,0:T(8,128)(2,1)}), bf16[4,2,32,2048]{3,2,1,0:T(8,128)(2,1)}, u32[]{:S(2)}, u32[]{:S(2)}) async-start(bf16[4,2,32,2048]{3,2,1,0:T(8,128)(2,1)} %shard_map.114), calls=%async_computation | async-start | bytes 2097152 | tf_op jit(solution)/shard_map/all_to_all | solution.py:272
  19.5 58.1 %all-gather.9.cloned.1.call-start = ((), (), s32[]{:S(2)}) async-start(), calls=%async_computation.10 | async-start | bytes 1474560 | tf_op jit(solution)/shard_map/all_gather | solution.py:412
  19.6 8.6 %collective-permute-start = (f32[24,512]{1,0:T(8,128)S(1)}, f32[24,512]{1,0:T(8,128)S(1)}, u32[]{:S(2)}, u32[]{:S(2)}) collective-permute-start(f32[24,512]{1,0:T(8,128)S(1)} %get-tuple-element.32), channel_id=1, source_target_pairs={{0,8},{8,16},{16,24},{24,32},{32,40},{40,48},{48,56},{56,64},{64,7... | collective-permute-start | bytes 147464 | tf_op jit(solution)/shard_map/ppermute | solution.py:298
  21.6 8.1 %collective-permute-start.1 = (f32[24,512]{1,0:T(8,128)S(1)}, f32[24,512]{1,0:T(8,128)S(1)}, u32[]{:S(2)}, u32[]{:S(2)}) collective-permute-start(f32[24,512]{1,0:T(8,128)S(1)} %get-tuple-element.33), channel_id=1, source_target_pairs={{8,0},{16,8},{24,16},{32,24},{40,32},{48,40},{56,48},{64,56},{72,6... | collective-permute-start | bytes 147464 | tf_op jit(solution)/shard_map/ppermute | solution.py:299
  32.3 27.6 %all-to-all-start.1 = ((f32[16,1,1536]{2,1,0:T(1,128)}), f32[16,1,1536]{2,1,0:T(1,128)S(1)}, u32[]{:S(2)}, u32[]{:S(2)}) async-start(f32[16,1,1536]{2,1,0:T(1,128)} %get-tuple-element.37), calls=%async_computation.1 | async-start | bytes 196608 | tf_op jit(solution)/shard_map/all_to_all | solution.py:269
  46.9 13.1 %copy-start.5 = (s32[512]{0:T(512)S(1)}, s32[512]{0:T(512)}, u32[]{:S(2)}) copy-start(s32[512]{0:T(512)} %param.15) | copy-start | bytes 6148
  60.0 15.0 %copy-start.6 = (bf16[4,2,32,2048]{3,2,1,0:T(8,128)(2,1)S(1)}, bf16[4,2,32,2048]{3,2,1,0:T(8,128)(2,1)}, u32[]{:S(2)}) copy-start(bf16[4,2,32,2048]{3,2,1,0:T(8,128)(2,1)} %get-tuple-element.39.refs_6_) | copy-start | bytes 3145732
  63.0 12.1 %all-to-all-start.2 = ((bf16[8,32,512]{2,1,0:T(8,128)(2,1)}), bf16[8,32,512]{2,1,0:T(8,128)(2,1)S(1)}, u32[]{:S(2)}, u32[]{:S(2)}) async-start(bf16[8,32,512]{2,1,0:T(8,128)(2,1)} %shard_map.117), calls=%async_computation.2 | async-start | bytes 524288 | tf_op jit(solution)/shard_map/all_to_all | solution.py:421
  67.5 47.1 %all-gather.11.cloned.1.call-start = ((), (), s32[]{:S(2)}) async-start(), calls=%async_computation.11 | async-start | bytes 1474560 | tf_op jit(solution)/shard_map/all_gather | solution.py:412
  81.4 18.3 %all-to-all-start.3 = ((f32[16,1,1536]{2,1,0:T(1,128)}), f32[16,1,1536]{2,1,0:T(1,128)S(1)}, u32[]{:S(2)}, u32[]{:S(2)}) async-start(f32[16,1,1536]{2,1,0:T(1,128)} %get-tuple-element.44), calls=%async_computation.3 | async-start | bytes 196608 | tf_op jit(solution)/shard_map/all_to_all | solution.py:269
  85.7 66.7 %all-gather.13.cloned.1.call-start = ((), (), s32[]{:S(2)}) async-start(), calls=%async_computation.12 | async-start | bytes 1474560 | tf_op jit(solution)/shard_map/all_gather | solution.py:412
  118.4 18.6 %all-to-all-start.5 = ((f32[16,1,1536]{2,1,0:T(1,128)}), f32[16,1,1536]{2,1,0:T(1,128)S(1)}, u32[]{:S(2)}, u32[]{:S(2)}) async-start(f32[16,1,1536]{2,1,0:T(1,128)} %get-tuple-element.50), calls=%async_computation.5 | async-start | bytes 196608 | tf_op jit(solution)/shard_map/all_to_all | solution.py:269
  123.1 72.0 %all-gather.15.cloned.1.call-start = ((), (), s32[]{:S(2)}) async-start(), calls=%async_computation.13 | async-start | bytes 1474560 | tf_op jit(solution)/shard_map/all_gather | solution.py:412
  156.2 18.1 %all-to-all-start.7 = ((f32[16,1,1536]{2,1,0:T(1,128)}), f32[16,1,1536]{2,1,0:T(1,128)S(1)}, u32[]{:S(2)}, u32[]{:S(2)}) async-start(f32[16,1,1536]{2,1,0:T(1,128)} %get-tuple-element.56), calls=%async_computation.7 | async-start | bytes 196608 | tf_op jit(solution)/shard_map/all_to_all | solution.py:269
  190.4 9.8 %all-to-all-start.9 = ((f32[4,2,2,2048]{3,2,1,0:T(2,128)}), f32[4,2,2,2048]{3,2,1,0:T(2,128)S(1)}, u32[]{:S(2)}, u32[]{:S(2)}) async-start(f32[4,2,2,2048]{3,2,1,0:T(2,128)} %get-tuple-element.60), calls=%async_computation.9 | async-start | bytes 262144 | tf_op jit(solution)/shard_map/all_to_all | solution.py:272
  195.1 1.3 copy-start.3
Sparse Core Ops, SparseCore 0:
  32.5 34.9 all-gather.8
  81.5 23.4 all-gather.10
  118.5 24.1 all-gather.12
  156.3 23.9 all-gather.14

commit v5 on v4

--- a/solution.py
+++ b/solution.py
@@ -359,7 +359,6 @@
                         for q in range(4):
                             at = comp * 8 + q * 2
                             r.sum_o[x, comp, :, q * 512 : (q + 1) * 512] = r.full[at : at + 2, :]
-                ghost_out(r, order)
                 return
             r.state_o[...] = state
             ham_rows(r, state, r.rows_o)
@@ -383,12 +382,14 @@
     def dipole_body(order):
         def body(r):
             r.all_points = all_points
+            if order == 4:
+                ghost_out(r, order)
             r.wait("ys", "field")
             dipole_image(r)
             term = dipole_term(r, order)
             for comp in range(2):
                 at = slice(comp * 80 + 8, comp * 80 + 16)
-                r.dip[at, :] = term[comp][8:16, :] + r.more[comp]
+                r.dip[at, :] = term[comp][8:16, :] + (r.more_o if order == 4 else r.more)[comp]
             for comp in range(2):
                 at = comp * 80
                 if order == 4:
@@ -437,11 +438,9 @@
             out = call(dipole_body(order), ins, outs, {**dipole_scratch, **z_scratch}, 4_000_000_000)
             outer.append(out["u_o"])
         else:
-            outs = {"sum_o": ((4, 2, 2, 2048), F32), "more_o": more_spec}
-            part = call(middle_body(4), {**inner_ins, **ghost_ins}, outs, full_scratch, 2_000_000_000)
-            total = part["sum_o"]
-            ins["more"] = part["more_o"]
-            outs = {"psi_o": ((2, 64, 512), F32), "mark_o": ((2, 8, 128), F32)}
+            total = call(middle_body(4), inner_ins, {"sum_o": ((4, 2, 2, 2048), F32)}, full_scratch, 1_000_000_000)["sum_o"]
+            ins.update(ghost_ins)
+            outs = {"psi_o": ((2, 64, 512), F32), "mark_o": ((2, 8, 128), F32), "more_o": more_spec}
             out = call(dipole_body(4), ins, outs, dipole_scratch, 4_000_000_000)
 
 

time: 209 us -> 209 us (level)
  transfers between devices with their start and end apart: 13 -> 13, of which waited for: 7 -> 7; matrix products, arithmetic and copies ran while one was open for 0% -> 0% of each run, Pallas kernels for 13% -> 14%
where the time goes in v5:
time: 209 us; the launch traced here: 208 us
  waiting for transfers between devices  61.3 us (29%)
  starting transfers between devices  54 us (26%)
  Pallas kernels  43.9 us (21%)
  blocking collectives  31.5 us (15%)
  between operations  14.7 us (7%)
  local copies, waits for them, and re-layouts  2.39 us (1%)
    all_to_all x4, waiting for transfers between devices, over_z(): return lax.all_to_all(piece, 'sector', 0, 0, axis_index_groups=z_groups)  50.4 us
    pallas_call x20, Pallas kernels, call(): pl.pallas_call(kernel, out_shape=[jax.ShapeDtypeStruct(shape, kind) for s...  43.9 us
    all_to_all x3, blocking collectives, shards(): pr = lax.all_to_all(part, 'chan', 0, 0)  31.5 us
    all_to_all x4, starting transfers between devices, over_z(): return lax.all_to_all(piece, 'sector', 0, 0, axis_index_groups=z_groups)  28.2 us
    all_to_all x2, starting transfers between devices, over_x(): return lax.all_to_all(piece, 'sector', 0, 0, axis_index_groups=x_groups)  15.3 us
    all_to_all x1, waiting for transfers between devices, shards(): pr = lax.all_to_all(part, 'chan', 0, 0)  6.85 us
    all_to_all x1, starting transfers between devices, shards(): pr = lax.all_to_all(part, 'chan', 0, 0)  4.51 us
  transfers between devices with their start and end apart: 13, of which 7 were waited for; matrix products, arithmetic and copies ran while one was open for 0% of the time, Pallas kernels for 14%

profile of v5, /device:TPU:6, one launch (start us, length us, event | category | flops | bytes accessed | tf_op | source)
XLA Modules:
  0.0 208.0 jit_solution(3742933088513929458)
XLA Ops:
  7.2 0.9 copy-done
  8.1 1.1 shard_map.114
  9.3 10.2 %all-to-all-start = ((bf16[4,2,32,2048]{3,2,1,0:T(8,128)(2,1)}), bf16[4,2,32,2048]{3,2,1,0:T(8,128)(2,1)}, u32[]{:S(2)}, u32[]{:S(2)}) async-start(bf16[4,2,32,2048]{3,2,1,0:T(8,128)(2,1)} %shard_map.114), calls=%async_computation | async-start | bytes 2097152 | tf_op jit(solution)/shard_map/all_to_all | solution.py:272
  19.5 0.1 shard_map.113
  19.6 1.9 collective-permute-start
  21.6 3.9 %collective-permute-start.1 = (f32[24,512]{1,0:T(8,128)S(1)}, f32[24,512]{1,0:T(8,128)S(1)}, u32[]{:S(2)}, u32[]{:S(2)}) collective-permute-start(f32[24,512]{1,0:T(8,128)S(1)} %get-tuple-element.31), channel_id=1, source_target_pairs={{8,0},{16,8},{24,16},{32,24},{40,32},{48,40},{56,48},{64,56},{72,6... | collective-permute-start | bytes 147464 | tf_op jit(solution)/shard_map/ppermute | solution.py:299
  25.5 0.1 reshape.10
  25.6 0.1 pad_add_fusion.refs_0_
  25.7 2.6 %collective-permute-done.refs_3_ = f32[24,512]{1,0:T(8,128)S(1)} collective-permute-done((f32[24,512]{1,0:T(8,128)S(1)}, f32[24,512]{1,0:T(8,128)S(1)}, u32[]{:S(2)}, u32[]{:S(2)}) %collective-permute-start) | collective-permute-done | bytes 49184 | tf_op jit(solution)/shard_map/ppermute | solution.py:298
  28.2 1.4 collective-permute-done.1.refs_4_
  29.7 2.6 %shard_map.115 = (bf16[4,2,32,2048]{3,2,1,0:T(8,128)(2,1)}, f32[160,512]{1,0:T(8,128)S(1)}, f32[80,512]{1,0:T(8,128)S(1)}, f32[16,512]{1,0:T(8,128)S(1)}, bf16[1...) custom-call(s32[128]{0:T(128)S(1)} %pad_add_fusion.refs_0_, f32[2,64,512]{2,1,0:T(8,128)S(1)} %bitcast.12, ...), custom_call_target="tpu_custom_call" | custom-call | flops 1000000000 | bytes 1024 | tf_op jit(solution)/shard_map/pallas_call | solution.py:83
  32.3 14.5 %all-to-all-start.1 = ((f32[16,1,1536]{2,1,0:T(1,128)}), f32[16,1,1536]{2,1,0:T(1,128)S(1)}, u32[]{:S(2)}, u32[]{:S(2)}) async-start(f32[16,1,1536]{2,1,0:T(1,128)} %get-tuple-element.35), calls=%async_computation.1 | async-start | bytes 196608 | tf_op jit(solution)/shard_map/all_to_all | solution.py:269
  46.9 0.9 shard_map.116.refs_1_.refs_4_
  47.8 12.1 %all-to-all-done.1.refs_3_.refs_1_ = f32[16,1,1536]{2,1,0:T(1,128)S(1)} async-done(((f32[16,1,1536]{2,1,0:T(1,128)}), f32[16,1,1536]{2,1,0:T(1,128)S(1)}, u32[]{:S(2)}, u32[]{:S(2)}) %all-to-all-start.1) | async-done | bytes 98336 | tf_op jit(solution)/shard_map/all_to_all | solution.py:269
  59.9 3.0 %shard_map.117 = bf16[8,32,512]{2,1,0:T(8,128)(2,1)} custom-call(s32[1,512]{1,0:T(1,128)S(1)} %bitcast.16, f32[160,512]{1,0:T(8,128)S(1)} %shard_map.116.refs_1_.refs_4_, f32[16,512]{1,0:T(8,128)S(1)} %get-tuple-element.36.refs_2_.refs_3_.refs_4_, f32[16,1,1536]{2,1,0:T(1,128)S(1)} %all-to-all-done.1.refs_3_.refs_1_, bf16[512,2048]{1,0:T(8,128)(2,1)} %refs_7_.1), custom_call_target="tpu_custom_call" | custom-call | flops 1500000000 | bytes 1024 | tf_op jit(solution)/shard_map/pallas_call | solution.py:83
  62.9 4.5 %all-to-all-start.2 = ((bf16[8,32,512]{2,1,0:T(8,128)(2,1)}), bf16[8,32,512]{2,1,0:T(8,128)(2,1)S(1)}, u32[]{:S(2)}, u32[]{:S(2)}) async-start(bf16[8,32,512]{2,1,0:T(8,128)(2,1)} %shard_map.117), calls=%async_computation.2 | async-start | bytes 524288 | tf_op jit(solution)/shard_map/all_to_all | solution.py:422
  67.4 0.0 all-gather.11.cloned.1.call-start
  68.1 6.8 %all-to-all-done.2.refs_2_ = bf16[8,32,512]{2,1,0:T(8,128)(2,1)S(1)} async-done(((bf16[8,32,512]{2,1,0:T(8,128)(2,1)}), bf16[8,32,512]{2,1,0:T(8,128)(2,1)S(1)}, u32[]{:S(2)}, u32[]{:S(2)}) %all-to-all-start.2) | async-done | bytes 262176 | tf_op jit(solution)/shard_map/all_to_all | solution.py:422
  75.0 2.5 %shard_map.118 = (f32[16,512]{1,0:T(8,128)S(1)}, f32[1,512]{1,0:T(1,128)S(1)}, f32[2,8,512]{2,1,0:T(8,128)S(1)}) custom-call(s32[128]{0:T(128)S(1)} %pad_add_fusion.refs_0_, f32[16,1,1536]{2,1,0:T(1,128)S(1)} %all-to-all-done.1.refs_3_.refs_1_, bf16[8,32,512]{2,1,0:T(8,128)(2,1)S(1)} %all-to-all-done.2.refs_2_, ...), custom_call_target="tpu_custom_call" | custom-call | flops 2000000000 | bytes 1024 | tf_op jit(solution)/shard_map/pallas_call | solution.py:83
  77.5 0.0 all-gather.9.cloned.1.call-done
  77.6 3.7 %shard_map.119 = (f32[16,1,1536]{2,1,0:T(1,128)}, f32[160,512]{1,0:T(8,128)S(1)}, bf16[160,512]{1,0:T(8,128)(2,1)}) custom-call(s32[128]{0:T(128)S(1)} %pad_add_fusion.refs_0_, bf16[8,160,512]{2,1,0:T(8,128)(2,1)} %bitcast.24, bf16[2,8,256,256]{3,2,1,0:T(8,128)(2,1)} %refs_2_.7, f32[128]{0:T(128)S(1)} %broadcast_in_dim.16.refs_3_, ...), custom_call_target="tpu_custom_call" | custom-call | flops 4000000000 | bytes 1024 | tf_op jit(solution)/shard_map/pallas_call | solution.py:83
  81.3 4.3 %all-to-all-start.3 = ((f32[16,1,1536]{2,1,0:T(1,128)}), f32[16,1,1536]{2,1,0:T(1,128)S(1)}, u32[]{:S(2)}, u32[]{:S(2)}) async-start(f32[16,1,1536]{2,1,0:T(1,128)} %get-tuple-element.42), calls=%async_computation.3 | async-start | bytes 196608 | tf_op jit(solution)/shard_map/all_to_all | solution.py:269
  85.7 0.0 all-gather.13.cloned.1.call-start
  85.7 0.9 shard_map.120.refs_1_.refs_4_
  86.7 13.0 %all-to-all-done.3.refs_3_.refs_1_ = f32[16,1,1536]{2,1,0:T(1,128)S(1)} async-done(((f32[16,1,1536]{2,1,0:T(1,128)}), f32[16,1,1536]{2,1,0:T(1,128)S(1)}, u32[]{:S(2)}, u32[]{:S(2)}) %all-to-all-start.3) | async-done | bytes 98336 | tf_op jit(solution)/shard_map/all_to_all | solution.py:269
  99.6 2.2 %shard_map.121 = bf16[8,32,512]{2,1,0:T(8,128)(2,1)S(1)} custom-call(s32[1,512]{1,0:T(1,128)S(1)} %bitcast.18, f32[160,512]{1,0:T(8,128)S(1)} %shard_map.120.refs_1_.refs_4_, f32[16,512]{1,0:T(8,128)S(1)} %get-tuple-element.43.refs_2_.refs_3_.refs_5_, f32[16,1,1536]{2,1,0:T(1,128)S(1)} %all-to-all-done.3.refs_3_.refs_1_, bf16[512,2048]{1,0:T(8,128)(2,1)} %refs_7_.1), custom_call_target="tpu_custom_call" | custom-call | flops 1500000000 | bytes 1024 | tf_op jit(solution)/shard_map/pallas_call | solution.py:83
  101.8 10.2 %all_to_all.50.refs_2_ = bf16[8,32,512]{2,1,0:T(8,128)(2,1)S(1)} all-to-all(bf16[8,32,512]{2,1,0:T(8,128)(2,1)S(1)} %shard_map.121), channel_id=1, replica_groups=mesh['sector'=64,'chan'=8] {'chan'}, dimensions={0} | all-to-all | bytes 524288 | tf_op jit(solution)/shard_map/all_to_all | solution.py:422
  112.0 2.5 %shard_map.122 = (f32[16,512]{1,0:T(8,128)S(1)}, f32[1,512]{1,0:T(1,128)S(1)}, f32[2,8,512]{2,1,0:T(8,128)S(1)}) custom-call(s32[128]{0:T(128)S(1)} %pad_add_fusion.refs_0_, f32[16,1,1536]{2,1,0:T(1,128)S(1)} %all-to-all-done.3.refs_3_.refs_1_, bf16[8,32,512]{2,1,0:T(8,128)(2,1)S(1)} %all_to_all.50.refs_2_, ...), custom_call_target="tpu_custom_call" | custom-call | flops 2000000000 | bytes 1024 | tf_op jit(solution)/shard_map/pallas_call | solution.py:83
  114.6 3.7 %shard_map.123 = (f32[16,1,1536]{2,1,0:T(1,128)}, f32[160,512]{1,0:T(8,128)S(1)}, bf16[160,512]{1,0:T(8,128)(2,1)}) custom-call(s32[128]{0:T(128)S(1)} %pad_add_fusion.refs_0_, bf16[8,160,512]{2,1,0:T(8,128)(2,1)} %bitcast.26, bf16[2,8,256,256]{3,2,1,0:T(8,128)(2,1)} %refs_2_.7, f32[128]{0:T(128)S(1)} %broadcast_in_dim.16.refs_3_, ...), custom_call_target="tpu_custom_call" | custom-call | flops 4000000000 | bytes 1024 | tf_op jit(solution)/shard_map/pallas_call | solution.py:83
  118.4 4.7 %all-to-all-start.5 = ((f32[16,1,1536]{2,1,0:T(1,128)}), f32[16,1,1536]{2,1,0:T(1,128)S(1)}, u32[]{:S(2)}, u32[]{:S(2)}) async-start(f32[16,1,1536]{2,1,0:T(1,128)} %get-tuple-element.48), calls=%async_computation.5 | async-start | bytes 196608 | tf_op jit(solution)/shard_map/all_to_all | solution.py:269
  123.1 0.0 all-gather.15.cloned.1.call-start
  123.1 0.9 shard_map.124.refs_1_.refs_4_
  124.1 12.9 %all-to-all-done.5.refs_3_.refs_1_ = f32[16,1,1536]{2,1,0:T(1,128)S(1)} async-done(((f32[16,1,1536]{2,1,0:T(1,128)}), f32[16,1,1536]{2,1,0:T(1,128)S(1)}, u32[]{:S(2)}, u32[]{:S(2)}) %all-to-all-start.5) | async-done | bytes 98336 | tf_op jit(solution)/shard_map/all_to_all | solution.py:269
  136.9 2.2 %shard_map.125 = bf16[8,32,512]{2,1,0:T(8,128)(2,1)S(1)} custom-call(s32[1,512]{1,0:T(1,128)S(1)} %bitcast.20, f32[160,512]{1,0:T(8,128)S(1)} %shard_map.124.refs_1_.refs_4_, f32[16,512]{1,0:T(8,128)S(1)} %get-tuple-element.49.refs_2_.refs_3_.refs_6_, f32[16,1,1536]{2,1,0:T(1,128)S(1)} %all-to-all-done.5.refs_3_.refs_1_, bf16[512,2048]{1,0:T(8,128)(2,1)} %refs_7_.1), custom_call_target="tpu_custom_call" | custom-call | flops 1500000000 | bytes 1024 | tf_op jit(solution)/shard_map/pallas_call | solution.py:83
  139.1 10.7 %all_to_all.51.refs_2_ = bf16[8,32,512]{2,1,0:T(8,128)(2,1)S(1)} all-to-all(bf16[8,32,512]{2,1,0:T(8,128)(2,1)S(1)} %shard_map.125), channel_id=1, replica_groups=mesh['sector'=64,'chan'=8] {'chan'}, dimensions={0} | all-to-all | bytes 524288 | tf_op jit(solution)/shard_map/all_to_all | solution.py:422
  149.8 2.5 %shard_map.126 = (f32[16,512]{1,0:T(8,128)S(1)}, f32[1,512]{1,0:T(1,128)S(1)}, f32[2,8,512]{2,1,0:T(8,128)S(1)}) custom-call(s32[128]{0:T(128)S(1)} %pad_add_fusion.refs_0_, f32[16,1,1536]{2,1,0:T(1,128)S(1)} %all-to-all-done.5.refs_3_.refs_1_, bf16[8,32,512]{2,1,0:T(8,128)(2,1)S(1)} %all_to_all.51.refs_2_, ...), custom_call_target="tpu_custom_call" | custom-call | flops 2000000000 | bytes 1024 | tf_op jit(solution)/shard_map/pallas_call | solution.py:83
  152.3 0.0 all-gather.13.cloned.1.call-done
  152.4 3.7 %shard_map.127 = (f32[16,1,1536]{2,1,0:T(1,128)}, f32[160,512]{1,0:T(8,128)S(1)}, bf16[160,512]{1,0:T(8,128)(2,1)}) custom-call(s32[128]{0:T(128)S(1)} %pad_add_fusion.refs_0_, bf16[8,160,512]{2,1,0:T(8,128)(2,1)} %bitcast.25, bf16[2,8,256,256]{3,2,1,0:T(8,128)(2,1)} %refs_2_.7, f32[128]{0:T(128)S(1)} %broadcast_in_dim.16.refs_3_, ...), custom_call_target="tpu_custom_call" | custom-call | flops 4000000000 | bytes 1024 | tf_op jit(solution)/shard_map/pallas_call | solution.py:83
  156.2 4.7 %all-to-all-start.7 = ((f32[16,1,1536]{2,1,0:T(1,128)}), f32[16,1,1536]{2,1,0:T(1,128)S(1)}, u32[]{:S(2)}, u32[]{:S(2)}) async-start(f32[16,1,1536]{2,1,0:T(1,128)} %get-tuple-element.55), calls=%async_computation.7 | async-start | bytes 196608 | tf_op jit(solution)/shard_map/all_to_all | solution.py:269
  160.8 1.1 shard_map.128.refs_1_.refs_4_
  161.9 12.4 %all-to-all-done.7.refs_3_.refs_1_ = f32[16,1,1536]{2,1,0:T(1,128)S(1)} async-done(((f32[16,1,1536]{2,1,0:T(1,128)}), f32[16,1,1536]{2,1,0:T(1,128)S(1)}, u32[]{:S(2)}, u32[]{:S(2)}) %all-to-all-start.7) | async-done | bytes 98336 | tf_op jit(solution)/shard_map/all_to_all | solution.py:269
  174.3 2.2 %shard_map.129 = bf16[8,32,512]{2,1,0:T(8,128)(2,1)S(1)} custom-call(s32[1,512]{1,0:T(1,128)S(1)} %bitcast.22, f32[160,512]{1,0:T(8,128)S(1)} %shard_map.128.refs_1_.refs_4_, f32[16,512]{1,0:T(8,128)S(1)} %get-tuple-element.54.refs_2_.refs_3_, f32[16,1,1536]{2,1,0:T(1,128)S(1)} %all-to-all-done.7.refs_3_.refs_1_, bf16[512,2048]{1,0:T(8,128)(2,1)} %refs_7_.1), custom_call_target="tpu_custom_call" | custom-call | flops 1500000000 | bytes 1024 | tf_op jit(solution)/shard_map/pallas_call | solution.py:83
  176.5 10.6 %all_to_all.52.refs_6_.refs_2_ = bf16[8,32,512]{2,1,0:T(8,128)(2,1)S(1)} all-to-all(bf16[8,32,512]{2,1,0:T(8,128)(2,1)S(1)} %shard_map.129), channel_id=1, replica_groups=mesh['sector'=64,'chan'=8] {'chan'}, dimensions={0} | all-to-all | bytes 524288 | tf_op jit(solution)/shard_map/all_to_all | solution.py:422
  187.1 1.3 shard_map.131
  188.4 5.1 %all-to-all-start.9 = ((f32[4,2,2,2048]{3,2,1,0:T(2,128)}), f32[4,2,2,2048]{3,2,1,0:T(2,128)S(1)}, u32[]{:S(2)}, u32[]{:S(2)}) async-start(f32[4,2,2,2048]{3,2,1,0:T(2,128)} %shard_map.131), calls=%async_computation.9 | async-start | bytes 262144 | tf_op jit(solution)/shard_map/all_to_all | solution.py:272
  193.5 1.3 copy-done.3
  194.8 5.8 %shard_map.130 = (f32[2,64,512]{2,1,0:T(8,128)}, f32[2,8,128]{2,1,0:T(8,128)S(1)}, f32[2,8,512]{2,1,0:T(8,128)}) custom-call(s32[128]{0:T(128)S(1)} %pad_add_fusion.refs_0_, bf16[8,160,512]{2,1,0:T(8,128)(2,1)S(1)} %bitcast.15, bf16[2,8,256,256]{3,2,1,0:T(8,128)(2,1)} %refs_2_.7, f32[128]{0:T(128)S(1)} %broadcast_in_dim.16.refs_3_, ...), custom_call_target="tpu_custom_call" | custom-call | flops 4000000000 | bytes 1024 | tf_op jit(solution)/shard_map/pallas_call | solution.py:83
  200.6 0.8 shard_map.132
  (27 shorter events, 0.1 us)
Async XLA Ops:
  7.2 1.0 copy-start
  9.2 10.3 %copy-start.1 = (f32[2,512,64]{1,2,0:T(8,128)S(1)}, f32[2,512,64]{1,2,0:T(8,128)}, u32[]{:S(2)}) copy-start(f32[2,512,64]{1,2,0:T(8,128)} %param.10) | copy-start | bytes 786436
  9.2 10.3 %copy-start.2 = (bf16[512,64]{0,1:T(8,128)(2,1)S(1)}, bf16[512,64]{0,1:T(8,128)(2,1)}, u32[]{:S(2)}) copy-start(bf16[512,64]{0,1:T(8,128)(2,1)} %param.11) | copy-start | bytes 196612
  9.2 16.3 %copy-start.8 = (s32[2,8]{1,0:T(2,128)S(1)}, s32[2,8]{1,0:T(2,128)}, u32[]{:S(2)}) copy-start(s32[2,8]{1,0:T(2,128)} %param.13) | copy-start | bytes 196
  9.3 16.3 %copy-start.7 = (s32[2]{0:T(128)S(1)}, s32[2]{0:T(128)}, u32[]{:S(2)}) copy-start(s32[2]{0:T(128)} %param.16) | copy-start | bytes 28
  9.3 20.4 %copy-start.4 = (f32[2,2,2048]{2,1,0:T(2,128)S(1)}, f32[2,2,2048]{2,1,0:T(2,128)}, u32[]{:S(2)}) copy-start(f32[2,2,2048]{2,1,0:T(2,128)} %refs_5_.4) | copy-start | bytes 98308
  9.3 20.4 %all-to-all-start = ((bf16[4,2,32,2048]{3,2,1,0:T(8,128)(2,1)}), bf16[4,2,32,2048]{3,2,1,0:T(8,128)(2,1)}, u32[]{:S(2)}, u32[]{:S(2)}) async-start(bf16[4,2,32,2048]{3,2,1,0:T(8,128)(2,1)} %shard_map.114), calls=%async_computation | async-start | bytes 2097152 | tf_op jit(solution)/shard_map/all_to_all | solution.py:272
  19.5 58.1 %all-gather.9.cloned.1.call-start = ((), (), s32[]{:S(2)}) async-start(), calls=%async_computation.10 | async-start | bytes 1474560 | tf_op jit(solution)/shard_map/all_gather | solution.py:413
  19.6 8.6 %collective-permute-start = (f32[24,512]{1,0:T(8,128)S(1)}, f32[24,512]{1,0:T(8,128)S(1)}, u32[]{:S(2)}, u32[]{:S(2)}) collective-permute-start(f32[24,512]{1,0:T(8,128)S(1)} %get-tuple-element.30), channel_id=1, source_target_pairs={{0,8},{8,16},{16,24},{24,32},{32,40},{40,48},{48,56},{56,64},{64,7... | collective-permute-start | bytes 147464 | tf_op jit(solution)/shard_map/ppermute | solution.py:298
  21.6 8.1 %collective-permute-start.1 = (f32[24,512]{1,0:T(8,128)S(1)}, f32[24,512]{1,0:T(8,128)S(1)}, u32[]{:S(2)}, u32[]{:S(2)}) collective-permute-start(f32[24,512]{1,0:T(8,128)S(1)} %get-tuple-element.31), channel_id=1, source_target_pairs={{8,0},{16,8},{24,16},{32,24},{40,32},{48,40},{56,48},{64,56},{72,6... | collective-permute-start | bytes 147464 | tf_op jit(solution)/shard_map/ppermute | solution.py:299
  32.3 27.6 %all-to-all-start.1 = ((f32[16,1,1536]{2,1,0:T(1,128)}), f32[16,1,1536]{2,1,0:T(1,128)S(1)}, u32[]{:S(2)}, u32[]{:S(2)}) async-start(f32[16,1,1536]{2,1,0:T(1,128)} %get-tuple-element.35), calls=%async_computation.1 | async-start | bytes 196608 | tf_op jit(solution)/shard_map/all_to_all | solution.py:269
  46.9 13.1 %copy-start.5 = (s32[512]{0:T(512)S(1)}, s32[512]{0:T(512)}, u32[]{:S(2)}) copy-start(s32[512]{0:T(512)} %param.15) | copy-start | bytes 6148
  59.9 15.0 %copy-start.6 = (bf16[4,2,32,2048]{3,2,1,0:T(8,128)(2,1)S(1)}, bf16[4,2,32,2048]{3,2,1,0:T(8,128)(2,1)}, u32[]{:S(2)}) copy-start(bf16[4,2,32,2048]{3,2,1,0:T(8,128)(2,1)} %get-tuple-element.37.refs_6_) | copy-start | bytes 3145732
  62.9 12.1 %all-to-all-start.2 = ((bf16[8,32,512]{2,1,0:T(8,128)(2,1)}), bf16[8,32,512]{2,1,0:T(8,128)(2,1)S(1)}, u32[]{:S(2)}, u32[]{:S(2)}) async-start(bf16[8,32,512]{2,1,0:T(8,128)(2,1)} %shard_map.117), calls=%async_computation.2 | async-start | bytes 524288 | tf_op jit(solution)/shard_map/all_to_all | solution.py:422
  67.4 47.1 %all-gather.11.cloned.1.call-start = ((), (), s32[]{:S(2)}) async-start(), calls=%async_computation.11 | async-start | bytes 1474560 | tf_op jit(solution)/shard_map/all_gather | solution.py:413
  81.3 18.3 %all-to-all-start.3 = ((f32[16,1,1536]{2,1,0:T(1,128)}), f32[16,1,1536]{2,1,0:T(1,128)S(1)}, u32[]{:S(2)}, u32[]{:S(2)}) async-start(f32[16,1,1536]{2,1,0:T(1,128)} %get-tuple-element.42), calls=%async_computation.3 | async-start | bytes 196608 | tf_op jit(solution)/shard_map/all_to_all | solution.py:269
  85.7 66.7 %all-gather.13.cloned.1.call-start = ((), (), s32[]{:S(2)}) async-start(), calls=%async_computation.12 | async-start | bytes 1474560 | tf_op jit(solution)/shard_map/all_gather | solution.py:413
  118.4 18.6 %all-to-all-start.5 = ((f32[16,1,1536]{2,1,0:T(1,128)}), f32[16,1,1536]{2,1,0:T(1,128)S(1)}, u32[]{:S(2)}, u32[]{:S(2)}) async-start(f32[16,1,1536]{2,1,0:T(1,128)} %get-tuple-element.48), calls=%async_computation.5 | async-start | bytes 196608 | tf_op jit(solution)/shard_map/all_to_all | solution.py:269
  123.1 70.4 %all-gather.15.cloned.1.call-start = ((), (), s32[]{:S(2)}) async-start(), calls=%async_computation.13 | async-start | bytes 1474560 | tf_op jit(solution)/shard_map/all_gather | solution.py:413
  156.2 18.1 %all-to-all-start.7 = ((f32[16,1,1536]{2,1,0:T(1,128)}), f32[16,1,1536]{2,1,0:T(1,128)S(1)}, u32[]{:S(2)}, u32[]{:S(2)}) async-start(f32[16,1,1536]{2,1,0:T(1,128)} %get-tuple-element.55), calls=%async_computation.7 | async-start | bytes 196608 | tf_op jit(solution)/shard_map/all_to_all | solution.py:269
  188.4 12.2 %all-to-all-start.9 = ((f32[4,2,2,2048]{3,2,1,0:T(2,128)}), f32[4,2,2,2048]{3,2,1,0:T(2,128)S(1)}, u32[]{:S(2)}, u32[]{:S(2)}) async-start(f32[4,2,2,2048]{3,2,1,0:T(2,128)} %shard_map.131), calls=%async_computation.9 | async-start | bytes 262144 | tf_op jit(solution)/shard_map/all_to_all | solution.py:272
  193.5 1.3 copy-start.3
Sparse Core Ops, SparseCore 0:
  32.5 35.0 all-gather.8
  81.5 23.4 all-gather.10
  118.5 24.1 all-gather.12
  156.3 24.1 all-gather.14
